TPU v7x, 128 devices: a whole 4x4x4 slice. The times are simulated.
128 devices in a mesh: ctx: 32 (over z, y, x_hi), wa: 4 (over x_lo, core).
Axes of the slice: x: 4 (x_hi: 2, x_lo: 2; x = x_hi * 2 + x_lo), y: 4, z: 4, core: 2. Of those that a mesh axis runs over, the one named last changes fastest.
Arguments:
- tokens: bfloat16 [4096, 1024], P('ctx'), may hold values from -6 to 6
- norm1_gain: float32 [1024], replicated, may hold values from 0.5 to 1.5
- w_query: bfloat16 [1024, 1024], P(None, 'wa'), may hold values from -0.5 to 0.5
- key_weight: bfloat16 [1024, 512], P(None, 'wa'), may hold values from -0.5 to 0.5
- value_weight: bfloat16 [1024, 512], P(None, 'wa'), may hold values from -0.1875 to 0.1875
- w_out: bfloat16 [1024, 1024], P('wa'), may hold values from -6 to 6
- norm2_gain: float32 [1024], replicated, may hold values from 0.5 to 1.5
- w_router: bfloat16 [1024, 32], replicated, may hold values from -0.09375 to 0.09375
- w_gate: bfloat16 [32, 1024, 512], P('ctx', None, 'wa'), may hold values from -0.1875 to 0.1875
- w_up: bfloat16 [32, 1024, 512], P('ctx', None, 'wa'), may hold values from -0.1875 to 0.1875
- w_down: bfloat16 [32, 512, 1024], P('ctx', 'wa'), may hold values from -1 to 1
- routes: int32 [4096, 8], P('ctx'), may hold values from 0 to 31, all different within a row; in each aligned block of 128 rows (0 to 127, 128 to 255, ...) at most 64 rows name the same one
- cotangent: bfloat16 [4096, 1024], P('ctx'), may hold values from -6 to 6
Outputs:
- output: bfloat16 [4096, 1024], P('ctx')
- grad_tokens: bfloat16 [4096, 1024], P('ctx')
- grad_norm1_gain: float32 [1024], replicated
- grad_w_query: float32 [1024, 1024], P(None, 'wa')
- grad_w_key: float32 [1024, 512], P(None, 'wa')
- grad_w_value: float32 [1024, 512], P(None, 'wa')
- grad_w_out: float32 [1024, 1024], P('wa')
- grad_norm2_gain: float32 [1024], replicated
- grad_w_router: float32 [1024, 32], replicated
- grad_w_gate: float32 [32, 1024, 512], P('ctx', None, 'wa')
- grad_w_up: float32 [32, 1024, 512], P('ctx', None, 'wa')
- grad_w_down: float32 [32, 512, 1024], P('ctx', 'wa')
Inputs may be any that keep to these rules, and one draw needn't show every extreme that they name: `routes`: each row names 8 different experts; in each aligned block of 128 rows no expert is named by more than 64 rows.
All inputs are finite; a program needn't handle non-finite values.
Results may differ from a plain program's by a relative error of at most 0.04.
Values may be sent and summed in bfloat16 or wider, within the bound.
No kernel may reach another device: no remote copies, remote signals or barrier semaphores. Data moves between devices by JAX's collectives and lax.ppermute only.
A program may use at most 128 MiB of HBM per device.

v0:
```python
import math

import jax
import jax.numpy as jnp
from jax import lax
from jax.sharding import PartitionSpec as P

HEAD_DIM = 64


epsilon = 1e-06


def local_positions(first_row, row_count, device_rows, group_count):
    numbers = first_row + jnp.arange(row_count, dtype=jnp.int32)
    owner_index = numbers // device_rows
    within = numbers % device_rows
    halfway = device_rows // 2
    return jnp.where(
        within < halfway,
        owner_index * halfway + within,
        (2 * group_count - 1 - owner_index) * halfway + within - halfway,
    )


def rotary_turn(vectors, token_positions, direction):
    halfway = vectors.shape[-1] // 2
    inverse = jnp.power(10000.0, -2.0 * jnp.arange(halfway, dtype=jnp.float32) / vectors.shape[-1])
    angles = token_positions.astype(jnp.float32)[:, None] * inverse[None, :]
    cosine = jnp.cos(angles)[:, None, :]
    sine_part = direction * jnp.sin(angles)[:, None, :]
    leading = vectors[..., :halfway]
    trailing = vectors[..., halfway:]
    return jnp.concatenate(
        [leading * cosine - trailing * sine_part, trailing * cosine + leading * sine_part], -1
    )


def local(
    tokens,
    norm1_gain,
    w_query,
    key_weight,
    value_weight,
    w_out,
    norm2_gain,
    w_router,
    w_gate,
    w_up,
    w_down,
    routes,
    cotangent,
):
    group_count = lax.axis_size("ctx")
    device_rows = tokens.shape[0]
    model_width = tokens.shape[1]
    query_heads = w_query.shape[1] // HEAD_DIM
    key_heads = key_weight.shape[1] // HEAD_DIM
    group_size = query_heads // key_heads
    key_width = key_heads * HEAD_DIM
    local_experts = w_gate.shape[0]
    expert_count = w_router.shape[1]
    route_count = routes.shape[1]
    capacity = device_rows // 2
    all_rows = device_rows * group_count
    key_block = math.gcd(all_rows, 1024)
    block_count = all_rows // key_block
    token_positions = local_positions(
        lax.axis_index("ctx") * device_rows, device_rows, device_rows, group_count
    )
    widened = tokens.astype(jnp.float32)
    root_first = lax.rsqrt(jnp.mean(widened * widened, -1, keepdims=True) + epsilon)
    unit_first = widened * root_first
    first_normalized = (unit_first * norm1_gain).astype(jnp.bfloat16)
    query_pre = jnp.dot(first_normalized, w_query, preferred_element_type=jnp.float32).reshape(
        device_rows, query_heads, HEAD_DIM
    )
    key_pre = jnp.dot(first_normalized, key_weight, preferred_element_type=jnp.float32).reshape(
        device_rows, key_heads, HEAD_DIM
    )
    value_pre = jnp.dot(first_normalized, value_weight, preferred_element_type=jnp.float32)
    query_rows = (
        rotary_turn(query_pre, token_positions, 1.0)
        .astype(jnp.bfloat16)
        .reshape(device_rows, key_heads, group_size, HEAD_DIM)
    )
    keys_here = (
        rotary_turn(key_pre, token_positions, 1.0)
        .astype(jnp.bfloat16)
        .reshape(device_rows, key_width)
    )
    keys_values = jnp.concatenate([keys_here, value_pre.astype(jnp.bfloat16)], 1)
    gathered = lax.all_gather(keys_values, "ctx", axis=0, tiled=True)

    def key_slice(number):
        piece = lax.dynamic_slice_in_dim(gathered, number * key_block, key_block, 0)
        key_part = piece[:, :key_width].reshape(key_block, key_heads, HEAD_DIM)
        value_part = piece[:, key_width:].reshape(key_block, key_heads, HEAD_DIM)
        allowed = (
            local_positions(number * key_block, key_block, device_rows, group_count)[None, :]
            <= token_positions[:, None]
        )
        scores = (
            jnp.einsum("rjgd,sjd->jgrs", query_rows, key_part, preferred_element_type=jnp.float32)
            / HEAD_DIM
        )
        return (key_part, value_part, allowed, scores)

    def attend(carry, number):
        running_max, running_sum, running_acc = carry
        key_part, value_part, allowed, scores = key_slice(number)
        new_max = jnp.maximum(running_max, jnp.max(jnp.where(allowed, scores, -1e30), -1))
        weights = jnp.where(allowed, jnp.exp(scores - new_max[..., None]), 0.0)
        factor = jnp.exp(running_max - new_max)
        new_sum = running_sum * factor + jnp.sum(weights, -1)
        new_acc = running_acc * factor[..., None] + jnp.einsum(
            "jgrs,sjd->jgrd",
            weights.astype(jnp.bfloat16),
            value_part,
            preferred_element_type=jnp.float32,
        )
        return ((new_max, new_sum, new_acc), None)

    start_max = jnp.full((key_heads, group_size, device_rows), -1e30, jnp.float32)
    start_sum = jnp.zeros((key_heads, group_size, device_rows), jnp.float32)
    start_acc = jnp.zeros((key_heads, group_size, device_rows, HEAD_DIM), jnp.float32)
    (final_max, final_sum, final_acc), unused = lax.scan(
        attend, (start_max, start_sum, start_acc), jnp.arange(block_count)
    )
    context_full = final_acc / final_sum[..., None]
    log_mass = final_max + jnp.log(final_sum)
    context = (
        jnp.transpose(context_full, (2, 0, 1, 3))
        .reshape(device_rows, query_heads * HEAD_DIM)
        .astype(jnp.bfloat16)
    )
    mixed = lax.psum(
        jnp.dot(context, w_out, preferred_element_type=jnp.float32).astype(jnp.bfloat16), "wa"
    ).astype(jnp.float32)
    middle = widened + mixed
    root_second = lax.rsqrt(jnp.mean(middle * middle, -1, keepdims=True) + epsilon)
    unit_second = middle * root_second
    normed_second = (unit_second * norm2_gain).astype(jnp.bfloat16)
    logits = jnp.dot(normed_second, w_router, preferred_element_type=jnp.float32)
    picks_int = (
        routes[:, :, None] == jnp.arange(expert_count, dtype=jnp.int32)[None, None, :]
    ).astype(jnp.int32)
    picks = picks_int.astype(jnp.float32)
    chosen = jnp.sum(picks * logits[:, None, :], -1)
    gates = jax.nn.softmax(chosen, -1)
    running_count = jnp.cumsum(jnp.sum(picks_int, 1), 0)
    slot_of = jnp.sum(picks_int * running_count[:, None, :], -1) - 1
    target = (routes * capacity + slot_of).reshape(-1)
    pair_rows = (
        jnp.full((expert_count * capacity,), device_rows * route_count, jnp.int32)
        .at[target]
        .set(jnp.arange(device_rows * route_count, dtype=jnp.int32))
    )
    source_rows = pair_rows // route_count

    def dispatch(buffer):
        moved = lax.all_to_all(
            buffer.reshape(group_count, local_experts * capacity, model_width),
            "ctx",
            split_axis=0,
            concat_axis=0,
            tiled=True,
        )
        return moved.reshape(group_count, local_experts, capacity, model_width)

    def collect(outgoing):
        moved = lax.all_to_all(
            outgoing.reshape(group_count, local_experts * capacity, model_width),
            "ctx",
            split_axis=0,
            concat_axis=0,
            tiled=True,
        )
        flat = moved.reshape(expert_count * capacity, model_width)
        return flat[target].reshape(device_rows, route_count, model_width)

    padded_second = jnp.concatenate([normed_second, jnp.zeros((1, model_width), jnp.bfloat16)], 0)
    arrived = dispatch(padded_second[source_rows])
    gate_pre = jnp.einsum("scrd,cdf->scrf", arrived, w_gate, preferred_element_type=jnp.float32)
    up_pre = jnp.einsum("scrd,cdf->scrf", arrived, w_up, preferred_element_type=jnp.float32)
    sigma = jax.nn.sigmoid(gate_pre)
    active = (gate_pre * sigma * up_pre).astype(jnp.bfloat16)
    expert_part = jnp.einsum(
        "scrf,cfd->scrd", active, w_down, preferred_element_type=jnp.float32
    ).astype(jnp.bfloat16)
    pieces = collect(expert_part).astype(jnp.float32)
    cot_wide = cotangent.astype(jnp.float32)
    moe_part = jnp.einsum("tk,tkd->td", gates, pieces)
    d_gates_part = jnp.einsum("tkd,td->tk", pieces, cot_wide)
    moe_sum, d_gates = (
        lax.psum(moe_part.astype(jnp.bfloat16), "wa").astype(jnp.float32),
        lax.psum(d_gates_part.astype(jnp.bfloat16), "wa").astype(jnp.float32),
    )
    output = (middle + moe_sum).astype(jnp.bfloat16)
    d_part = (gates[:, :, None] * cot_wide[:, None, :]).astype(jnp.bfloat16)
    padded_grad = jnp.concatenate(
        [
            d_part.reshape(device_rows * route_count, model_width),
            jnp.zeros((1, model_width), jnp.bfloat16),
        ],
        0,
    )
    d_arrived = dispatch(padded_grad[pair_rows])
    d_active = jnp.einsum("scrd,cfd->scrf", d_arrived, w_down, preferred_element_type=jnp.float32)
    d_gate_pre = (d_active * up_pre * sigma * (1.0 + gate_pre * (1.0 - sigma))).astype(jnp.bfloat16)
    d_up_pre = (d_active * gate_pre * sigma).astype(jnp.bfloat16)
    grad_w_down = jnp.einsum(
        "scrf,scrd->cfd", active, d_arrived, preferred_element_type=jnp.float32
    )
    grad_w_gate = jnp.einsum(
        "scrd,scrf->cdf", arrived, d_gate_pre, preferred_element_type=jnp.float32
    )
    grad_w_up = jnp.einsum("scrd,scrf->cdf", arrived, d_up_pre, preferred_element_type=jnp.float32)
    d_inputs = (
        jnp.einsum("scrf,cdf->scrd", d_gate_pre, w_gate, preferred_element_type=jnp.float32)
        + jnp.einsum("scrf,cdf->scrd", d_up_pre, w_up, preferred_element_type=jnp.float32)
    ).astype(jnp.bfloat16)
    d_pieces = collect(d_inputs)
    d_second_part = jnp.sum(d_pieces.astype(jnp.float32), 1)
    d_chosen = gates * (d_gates - jnp.sum(gates * d_gates, -1, keepdims=True))
    d_logits = jnp.sum(picks * d_chosen[:, :, None], 1).astype(jnp.bfloat16)
    grad_router = jnp.einsum(
        "td,te->de", normed_second, d_logits, preferred_element_type=jnp.float32
    )
    d_second = lax.psum(d_second_part.astype(jnp.bfloat16), "wa").astype(jnp.float32) + jnp.einsum(
        "te,de->td", d_logits, w_router, preferred_element_type=jnp.float32
    )
    scaled_second = d_second * norm2_gain
    grad_gain_second = jnp.sum(d_second * unit_second, 0)
    d_middle = cot_wide + root_second * (
        scaled_second - unit_second * jnp.mean(scaled_second * unit_second, -1, keepdims=True)
    )
    d_mixed = d_middle.astype(jnp.bfloat16)
    grad_out = jnp.einsum("tf,td->fd", context, d_mixed, preferred_element_type=jnp.float32)
    d_context = (
        jnp.einsum("td,fd->tf", d_mixed, w_out, preferred_element_type=jnp.float32)
        .astype(jnp.bfloat16)
        .reshape(device_rows, key_heads, group_size, HEAD_DIM)
    )
    row_delta = jnp.einsum("rjgd,jgrd->jgr", d_context.astype(jnp.float32), context_full)

    def reverse(carry, number):
        key_part, value_part, allowed, scores = key_slice(number)
        probs = jnp.where(allowed, jnp.exp(scores - log_mass[..., None]), 0.0)
        d_probs = jnp.einsum(
            "rjgd,sjd->jgrs", d_context, value_part, preferred_element_type=jnp.float32
        )
        d_scores = (probs * (d_probs - row_delta[..., None])).astype(jnp.bfloat16)
        carry = carry + jnp.einsum(
            "jgrs,sjd->rjgd", d_scores, key_part, preferred_element_type=jnp.float32
        )
        key_grad = (
            jnp.einsum("jgrs,rjgd->sjd", d_scores, query_rows, preferred_element_type=jnp.float32)
            / HEAD_DIM
        )
        value_grad = jnp.einsum(
            "jgrs,rjgd->sjd",
            probs.astype(jnp.bfloat16),
            d_context,
            preferred_element_type=jnp.float32,
        )
        return (
            carry,
            jnp.concatenate(
                [key_grad.reshape(key_block, key_width), value_grad.reshape(key_block, key_width)],
                1,
            ),
        )

    d_query_sum, d_blocks = lax.scan(
        reverse,
        jnp.zeros((device_rows, key_heads, group_size, HEAD_DIM), jnp.float32),
        jnp.arange(block_count),
    )
    own_grads = lax.psum_scatter(
        d_blocks.reshape(all_rows, 2 * key_width).astype(jnp.bfloat16),
        "ctx",
        scatter_dimension=0,
        tiled=True,
    ).astype(jnp.float32)
    d_query = (
        rotary_turn(
            (d_query_sum / HEAD_DIM).reshape(device_rows, query_heads, HEAD_DIM),
            token_positions,
            -1.0,
        )
        .astype(jnp.bfloat16)
        .reshape(device_rows, query_heads * HEAD_DIM)
    )
    d_key = (
        rotary_turn(
            own_grads[:, :key_width].reshape(device_rows, key_heads, HEAD_DIM),
            token_positions,
            -1.0,
        )
        .astype(jnp.bfloat16)
        .reshape(device_rows, key_width)
    )
    d_value = own_grads[:, key_width:].astype(jnp.bfloat16)
    grad_query = jnp.einsum(
        "td,tf->df", first_normalized, d_query, preferred_element_type=jnp.float32
    )
    grad_key = jnp.einsum("td,tf->df", first_normalized, d_key, preferred_element_type=jnp.float32)
    grad_value = jnp.einsum(
        "td,tf->df", first_normalized, d_value, preferred_element_type=jnp.float32
    )
    d_first_part = (
        jnp.einsum("tf,df->td", d_query, w_query, preferred_element_type=jnp.float32)
        + jnp.einsum("tf,df->td", d_key, key_weight, preferred_element_type=jnp.float32)
        + jnp.einsum("tf,df->td", d_value, value_weight, preferred_element_type=jnp.float32)
    )
    d_first = lax.psum(d_first_part.astype(jnp.bfloat16), "wa").astype(jnp.float32)
    scaled_first = d_first * norm1_gain
    grad_gain_first = jnp.sum(d_first * unit_first, 0)
    grad_tokens = (
        d_middle
        + root_first
        * (scaled_first - unit_first * jnp.mean(scaled_first * unit_first, -1, keepdims=True))
    ).astype(jnp.bfloat16)
    summed = (
        lax.psum(grad_query.astype(jnp.bfloat16), "ctx").astype(jnp.float32),
        lax.psum(grad_key.astype(jnp.bfloat16), "ctx").astype(jnp.float32),
        lax.psum(grad_value.astype(jnp.bfloat16), "ctx").astype(jnp.float32),
        lax.psum(grad_out.astype(jnp.bfloat16), "ctx").astype(jnp.float32),
        lax.psum(grad_gain_first.astype(jnp.bfloat16), "ctx").astype(jnp.float32),
        lax.psum(grad_gain_second.astype(jnp.bfloat16), "ctx").astype(jnp.float32),
        lax.psum(grad_router.astype(jnp.bfloat16), "ctx").astype(jnp.float32),
    )
    return (
        output,
        grad_tokens,
        summed[4],
        summed[0],
        summed[1],
        summed[2],
        summed[3],
        summed[5],
        summed[6],
        grad_w_gate,
        grad_w_up,
        grad_w_down,
    )


def solution(mesh):
    in_specs = (
        P("ctx", None),
        P(),
        P(None, "wa"),
        P(None, "wa"),
        P(None, "wa"),
        P("wa", None),
        P(),
        P(),
        P("ctx", None, "wa"),
        P("ctx", None, "wa"),
        P("ctx", "wa", None),
        P("ctx", None),
        P("ctx", None),
    )
    out_specs = (
        P("ctx", None),
        P("ctx", None),
        P(),
        P(None, "wa"),
        P(None, "wa"),
        P(None, "wa"),
        P("wa", None),
        P(),
        P(),
        P("ctx", None, "wa"),
        P("ctx", None, "wa"),
        P("ctx", "wa", None),
    )
    return jax.shard_map(local, mesh=mesh, in_specs=in_specs, out_specs=out_specs, check_vma=False)
```

profile of v0, /device:TPU:0, one launch (start us, length us, event | category | flops | bytes accessed | tf_op | source)
XLA Modules:
  0.0 1117.5 jit_solution(16598540947415450437)
XLA Ops:
  7.3 1.2 fusion.52
  8.5 1.4 convolution_convert_fusion.8
  9.9 1.4 fusion.97
  14.5 74.1 %all-gather.2.cloned.1.call-done = bf16[4096,256]{0,1:T(8,128)(2,1)} async-done(((bf16[128,256]{0,1:T(8,128)(2,1)}), bf16[4096,256]{0,1:T(8,128)(2,1)}) %all-gather.2.cloned.1.call-update) | async-done | bytes 2097168 | tf_op jit(solution)/shard_map/all_gather | solution.py:93
  88.6 16.5 %while.32 = (s32[]{:T(128)}, f32[2,2,128]{2,1,0:T(2,128)S(1)}, f32[2,2,128]{2,1,0:T(2,128)S(1)}, f32[2,2,128,64]{2,3,1,0:T(8,128)S(1)}, s32[4]{0:T(128)S(1)}, /*...) while((s32[]{:T(128)}, f32[2,2,128]{2,1,0:T(2,128)S(1)}, ...), condition=%wide.region_4.5_spmd.clone, body=%wide.region_1.4_spmd.clone.sunk | while | flops 140249088 | bytes 8758503 | solution.py:127
  90.1 1.1 fusion.172
  94.2 1.1 fusion.172
  98.4 1.1 fusion.172
  102.5 1.1 fusion.172
  107.3 4.3 scatter_custom_fusion
  112.3 28.6 %all-reduce.10.cloned.1.call-done = bf16[128,1024]{1,0:T(8,128)(2,1)} async-done(((bf16[128,1024]{1,0:T(8,128)(2,1)}), bf16[128,1024]{1,0:T(8,128)(2,1)}) %all-reduce.10.cloned.1.call-update) | async-done | bytes 262160 | tf_op jit(solution)/shard_map/psum | solution.py:137
  140.8 1.1 multiply_reduce_fusion.2
  142.0 1.1 multiply_convert_fusion.3
  143.1 9.6 gather_fusion
  152.7 63.1 %all_to_all.20 = bf16[32,64,1024]{2,1,0:T(8,128)(2,1)S(1)} all-to-all(bf16[32,64,1024]{2,1,0:T(8,128)(2,1)} %bitcast.277), channel_id=1, replica_groups=mesh['ctx'=32,'wa'=4] {'ctx'}, dimensions={0} | all-to-all | bytes 8388608 | tf_op jit(solution)/shard_map/all_to_all | solution.py:162
  215.8 1.3 convolution_bitcast_fusion.4
  217.8 2.3 multiply_convert_fusion.2
  220.0 3.2 convolution_convert_fusion
  223.3 5.2 all-to-all-start.1
  230.0 50.8 %all-to-all-done.1 = bf16[32,64,1024]{2,1,0:T(8,128)(2,1)} async-done(((bf16[32,64,1024]{2,1,0:T(8,128)(2,1)}), bf16[32,64,1024]{2,1,0:T(8,128)(2,1)}, u32[]{:S(2)}, u32[]{:S(2)}) %all-to-all-start.1) | async-done | bytes 4194336 | tf_op jit(solution)/shard_map/all_to_all | solution.py:172
  280.8 8.1 gather_fusion.1
  288.9 3.0 fusion.36
  292.0 1.5 copy.88
  293.5 5.8 psum.87
  299.2 1.2 fusion.82
  302.1 9.7 gather_fusion.2
  311.7 63.2 %all_to_all.21 = bf16[32,64,1024]{2,1,0:T(8,128)(2,1)S(1)} all-to-all(bf16[32,64,1024]{2,1,0:T(8,128)(2,1)} %bitcast.278), channel_id=1, replica_groups=mesh['ctx'=32,'wa'=4] {'ctx'}, dimensions={0} | all-to-all | bytes 8388608 | tf_op jit(solution)/shard_map/all_to_all | solution.py:162
  375.0 1.5 multiply_convert_fusion
  377.0 1.2 fusion.56
  378.3 3.2 add_convert_fusion
  381.5 5.0 all-to-all-start.3
  387.2 51.8 %all-to-all-done.3 = bf16[32,64,1024]{2,1,0:T(8,128)(2,1)} async-done(((bf16[32,64,1024]{2,1,0:T(8,128)(2,1)}), bf16[32,64,1024]{2,1,0:T(8,128)(2,1)}, u32[]{:S(2)}, u32[]{:S(2)}) %all-to-all-start.3) | async-done | bytes 4194336 | tf_op jit(solution)/shard_map/all_to_all | solution.py:172
  438.9 7.7 gather_fusion.3
  446.7 2.1 bitcast_reduce_fusion
  449.3 36.5 %all-reduce.12.cloned.1.call-done = bf16[128,1024]{1,0:T(8,128)(2,1)} async-done(((bf16[128,1024]{1,0:T(8,128)(2,1)}), bf16[128,1024]{1,0:T(8,128)(2,1)}) %all-reduce.12.cloned.1.call-update) | async-done | bytes 262160 | tf_op jit(solution)/shard_map/psum | solution.py:230
  485.7 1.9 multiply_reduce_fusion
  487.7 1.3 multiply_add_fusion
  489.5 29.3 %while.33 = (s32[]{:T(128)}, f32[128,2,2,64]{0,3,2,1:T(8,128)}, bf16[4,1024,256]{2,1,0:T(8,128)(2,1)}, s32[4]{0:T(128)S(1)}, bf16[4096,256]{0,1:T(8,128)(2,1)}, ...) while((s32[]{:T(128)}, f32[128,2,2,64]{0,3,2,1:T(8,128)}, ...), condition=%wide.region_22.23_spmd.clone, body=%wide.region_21.22_spmd.clone.sunk | while | flops 340753920 | bytes 15742201 | solution.py:275
  491.0 1.1 fusion.187
  497.7 1.1 fusion.187
  500.3 1.9 fusion.190
  505.2 1.1 fusion.187
  507.9 1.9 fusion.190
  512.8 1.1 fusion.187
  515.4 1.9 fusion.190
  518.9 1.0 copy.85
  523.7 1.1 convolution_convert_fusion.1
  525.1 183.7 %reduce-scatter.2.cloned.1.call-done = bf16[128,256]{1,0:T(8,128)(2,1)} async-done(((bf16[4096,256]{1,0:T(8,128)(2,1)}), bf16[128,256]{1,0:T(8,128)(2,1)}) %reduce-scatter.2.cloned.1.call-update) | async-done | bytes 65552 | tf_op jit(solution)/shard_map/reduce_scatter | solution.py:280
  710.0 1.7 fusion.40
  711.8 1.2 convolution_convert_fusion.2
  713.0 1.0 convolution_convert_fusion.4
  714.1 1.0 convolution_convert_fusion.3
  715.1 3.9 convolution_bitcast_fusion.7
  719.1 2.1 convolution_bitcast_fusion.5
  721.2 2.1 convolution_bitcast_fusion.6
  723.2 21.3 %all-reduce.16.cloned.1.call-done = (bf16[128,1024]{1,0:T(8,128)(2,1)}, bf16[128,1024]{1,0:T(8,128)(2,1)}) async-done(((bf16[128,1024]{1,0:T(8,128)(2,1)}, bf16[128,1024]{1,0:T(8,128)(2,1)}), (bf16[128,1024]{1,0:T(8,128)(2,1)}, bf16[128,1024]{1,0:T(8,128)(2,1)})) %all-reduce.16.cloned.1.call-update) | async-done | bytes 524304 | tf_op jit(solution)/shard_map/psum | solution.py:196
  744.6 1.2 fusion.51
  745.8 96.7 %all-reduce.2 = (bf16[1024]{0:T(1024)(128)(2,1)S(1)}, bf16[1024]{0:T(1024)(128)(2,1)S(1)}) all-reduce(bf16[1024]{0:T(1024)(128)(2,1)S(1)} %get-tuple-element.332, bf16[1024]{0:T(1024)(128)(2,1)S(1)} %copy-done.64), channel_id=1, replica_groups=mesh['ctx'=32,'wa'=4] {'ctx'}, use_global_device_ids=true, to_apply=%region_27.28 | all-reduce | flops 2048 | bytes 8192 | tf_op jit(solution)/shard_map/psum | solution.py:330
  843.7 2.1 fusion.48
  845.8 257.4 %all-reduce.14.cloned.1.call-done = (bf16[1024,256]{1,0:T(8,128)(2,1)}, bf16[1024,128]{1,0:T(8,128)(2,1)}, bf16[1024,128]{1,0:T(8,128)(2,1)}, bf16[256,1024]{1,0:T(8,128)(2,1)}, bf16[1024,32]{0,1:T(8,128)(2,1)}) async-done(((bf16[1024,256]{1,0:T(8,128)(2,1)}, bf16[1024,128]{1,0:T(8,128)(2,1)}, bf16[1024,128]{1,0:T(8,128)(2,1)}, bf16[256,1024]{1,0:T(8,128)(2,1)}, bf16[1024,32]{0,1:T(8,128)(2,1)}), ...) | async-done | bytes 1638416 | tf_op jit(solution)/shard_map/psum | solution.py:326
  1103.2 1.6 convert_element_type.245
  1104.8 2.1 convert_element_type.235
  1106.9 1.8 convert_element_type.237
  1109.5 1.1 convert_element_type.241
  (304 shorter events, 45.2 us)
Async XLA Ops:
  7.2 98.5 %copy-start = (bf16[256,1024]{1,0:T(8,128)(2,1)S(1)}, bf16[256,1024]{1,0:T(8,128)(2,1)}, u32[]{:S(2)}) copy-start(bf16[256,1024]{1,0:T(8,128)(2,1)} %param.22) | copy-start | bytes 1572868
  7.2 6.9 copy-start.1
  7.2 6.9 copy-start.38
  7.2 6.6 copy-start.46
  7.2 6.9 copy-start.13
  7.2 81.4 %all-gather.2.cloned.1.call-start = ((), (), s32[]{:S(2)}) async-start(), calls=%async_computation.5 | async-start | bytes 2162688 | tf_op jit(solution)/shard_map/all_gather | solution.py:93
  8.5 80.1 %copy-start.60 = (f32[128]{0:T(128)}, f32[128]{0:T(128)S(1)}, u32[]{:S(2)}) copy-start(f32[128]{0:T(128)S(1)} %add_rsqrt_fusion.1) | copy-start | bytes 1540
  12.7 128.1 %all-reduce.10.cloned.1.call-start = ((), (), s32[]{:S(2)}) async-start(), calls=%async_computation.6 | async-start | bytes 524288 | tf_op jit(solution)/shard_map/psum | solution.py:137
  88.6 53.3 %copy-start.54 = (f32[1024]{0:T(1024)S(1)}, f32[1024]{0:T(1024)}, u32[]{:S(2)}) copy-start(f32[1024]{0:T(1024)} %param.23) | copy-start | bytes 12292
  105.1 36.8 %copy-start.25 = (f32[2,2,128,64]{2,3,1,0:T(8,128)}, f32[2,2,128,64]{2,3,1,0:T(8,128)S(1)}, u32[]{:S(2)}) copy-start(f32[2,2,128,64]{2,3,1,0:T(8,128)S(1)} %get-tuple-element.249) | copy-start | bytes 393220
  105.1 47.6 %copy-start.43 = (f32[2,2,128]{2,1,0:T(2,128)}, f32[2,2,128]{2,1,0:T(2,128)S(1)}, u32[]{:S(2)}) copy-start(f32[2,2,128]{2,1,0:T(2,128)S(1)} %get-tuple-element.250) | copy-start | bytes 6148
  142.0 10.7 copy-start.66
  143.0 86.1 %copy-start.9 = (bf16[128,1024]{1,0:T(8,128)(2,1)}, bf16[128,1024]{1,0:T(8,128)(2,1)S(1)}, u32[]{:S(2)}) copy-start(bf16[128,1024]{1,0:T(8,128)(2,1)S(1)} %multiply_convert_fusion.3) | copy-start | bytes 786436
  152.7 63.1 %copy-start.18 = (bf16[1,1024,128]{2,1,0:T(8,128)(2,1)S(1)}, bf16[1,1024,128]{2,1,0:T(8,128)(2,1)}, u32[]{:S(2)}) copy-start(bf16[1,1024,128]{2,1,0:T(8,128)(2,1)} %param.25) | copy-start | bytes 786436
  217.8 2.3 copy-start.16
  217.8 2.3 copy-start.27
  220.0 3.2 copy-start.11
  223.3 5.2 copy-start.15
  223.3 5.3 copy-start.63
  223.3 5.9 copy-start.32
  223.3 6.1 copy-start.47
  223.3 57.5 %all-to-all-start.1 = ((bf16[32,64,1024]{2,1,0:T(8,128)(2,1)}), bf16[32,64,1024]{2,1,0:T(8,128)(2,1)}, u32[]{:S(2)}, u32[]{:S(2)}) async-start(bf16[32,64,1024]{2,1,0:T(8,128)(2,1)} %convolution_convert_fusion), calls=%async_computation.1 | async-start | bytes 8388608 | tf_op jit(solution)/shard_map/all_to_all | solution.py:172
  229.4 51.4 %copy-start.53 = (f32[128,8]{0,1:T(8,128)}, f32[128,8]{0,1:T(8,128)S(1)}, u32[]{:S(2)}) copy-start(f32[128,8]{0,1:T(8,128)S(1)} %fusion.70) | copy-start | bytes 12292
  229.4 51.4 %copy-start.65 = (f32[128]{0:T(128)}, f32[128]{0:T(128)S(1)}, u32[]{:S(2)}) copy-start(f32[128]{0:T(128)S(1)} %reduce_max.21) | copy-start | bytes 1540
  288.9 3.1 copy-start.5
  311.7 63.2 %copy-start.17 = (f32[32,1,64,128]{3,2,0,1:T(8,128)S(1)}, f32[32,1,64,128]{3,2,0,1:T(8,128)}, u32[]{:S(2)}) copy-start(f32[32,1,64,128]{3,2,0,1:T(8,128)} %copy-done.16) | copy-start | bytes 3145732
  311.7 63.2 %copy-start.28 = (bf16[1,128,1024]{2,1,0:T(8,128)(2,1)S(1)}, bf16[1,128,1024]{2,1,0:T(8,128)(2,1)}, u32[]{:S(2)}) copy-start(bf16[1,128,1024]{2,1,0:T(8,128)(2,1)} %param.27) | copy-start | bytes 786436
  311.7 63.2 %copy-start.70 = (f32[32,1,64,128]{3,2,0,1:T(8,128)S(1)}, f32[32,1,64,128]{3,2,0,1:T(8,128)}, u32[]{:S(2)}) copy-start(f32[32,1,64,128]{3,2,0,1:T(8,128)} %get-tuple-element.407) | copy-start | bytes 3145732
  381.5 5.1 copy-start.37
  381.5 5.1 copy-start.44
  381.5 57.5 %copy-start.56 = (s32[1024]{0:T(1024)S(1)}, s32[1024]{0:T(1024)}, u32[]{:S(2)}) copy-start(s32[1024]{0:T(1024)} %broadcast_clamp_fusion) | copy-start | bytes 12292
  381.5 57.4 %all-to-all-start.3 = ((bf16[32,64,1024]{2,1,0:T(8,128)(2,1)}), bf16[32,64,1024]{2,1,0:T(8,128)(2,1)}, u32[]{:S(2)}, u32[]{:S(2)}) async-start(bf16[32,64,1024]{2,1,0:T(8,128)(2,1)} %add_convert_fusion), calls=%async_computation.3 | async-start | bytes 8388608 | tf_op jit(solution)/shard_map/all_to_all | solution.py:172
  386.5 99.3 %all-reduce.12.cloned.1.call-start = ((), (), s32[]{:S(2)}) async-start(), calls=%async_computation.7 | async-start | bytes 524288 | tf_op jit(solution)/shard_map/psum | solution.py:230
  446.6 2.5 copy-start.52
  446.6 2.5 copy-start.59
  446.7 2.5 copy-start.69
  446.7 2.5 copy-start.48
  446.7 39.1 %copy-start.7 = (bf16[128,1024]{1,0:T(8,128)(2,1)S(1)}, bf16[128,1024]{1,0:T(8,128)(2,1)}, u32[]{:S(2)}) copy-start(bf16[128,1024]{1,0:T(8,128)(2,1)} %all-reduce.10.cloned.1.call-done) | copy-start | bytes 786436
  446.7 39.1 %copy-start.33 = (bf16[1024,32]{0,1:T(8,128)(2,1)S(1)}, bf16[1024,32]{0,1:T(8,128)(2,1)}, u32[]{:S(2)}) copy-start(bf16[1024,32]{0,1:T(8,128)(2,1)} %param.24) | copy-start | bytes 196612
  446.7 39.0 %copy-start.55 = (f32[1024]{0:T(1024)S(1)}, f32[1024]{0:T(1024)}, u32[]{:S(2)}) copy-start(f32[1024]{0:T(1024)} %param.23) | copy-start | bytes 12292
  446.7 39.0 %copy-start.67 = (f32[128]{0:T(128)S(1)}, f32[128]{0:T(128)}, u32[]{:S(2)}) copy-start(f32[128]{0:T(128)} %copy-done.66) | copy-start | bytes 1540
  448.9 260.0 %reduce-scatter.2.cloned.1.call-start = ((), (), s32[]{:S(2)}) async-start(), calls=%async_computation.8 | async-start | bytes 2162688 | tf_op jit(solution)/shard_map/reduce_scatter | solution.py:280
  449.2 38.5 %copy-start.49 = (bf16[128,32]{0,1:T(8,128)(2,1)}, bf16[128,32]{0,1:T(8,128)(2,1)S(1)}, u32[]{:S(2)}) copy-start(bf16[128,32]{0,1:T(8,128)(2,1)S(1)} %fusion.71) | copy-start | bytes 24580
  449.2 40.2 %copy-start.26 = (f32[2,2,128,64]{2,3,1,0:T(8,128)S(1)}, f32[2,2,128,64]{2,3,1,0:T(8,128)}, u32[]{:S(2)}) copy-start(f32[2,2,128,64]{2,3,1,0:T(8,128)} %copy-done.25) | copy-start | bytes 393220
  449.2 40.2 %copy-start.45 = (f32[2,2,128]{2,1,0:T(2,128)S(1)}, f32[2,2,128]{2,1,0:T(2,128)}, u32[]{:S(2)}) copy-start(f32[2,2,128]{2,1,0:T(2,128)} %copy-done.43) | copy-start | bytes 6148
  449.3 40.3 %copy-start.68 = (f32[2,2,128]{2,1,0:T(2,128)S(1)}, f32[2,2,128]{2,1,0:T(2,128)}, u32[]{:S(2)}) copy-start(f32[2,2,128]{2,1,0:T(2,128)} %log_add_fusion) | copy-start | bytes 6148
  518.9 225.7 %all-reduce.16.cloned.1.call-start = ((), (), s32[]{:S(2)}) async-start(), calls=%async_computation.10 | async-start | bytes 1048576 | tf_op jit(solution)/shard_map/psum | solution.py:196
  520.4 3.2 copy-start.41
  521.1 3.7 copy-start.14
  521.2 188.6 %copy-start.42 = (f32[128,32]{0,1:T(8,128)S(1)}, f32[128,32]{0,1:T(8,128)}, u32[]{:S(2)}) copy-start(f32[128,32]{0,1:T(8,128)} %get-tuple-element.403) | copy-start | bytes 49156
  521.2 188.6 %copy-start.34 = (bf16[1024,128]{1,0:T(8,128)(2,1)S(1)}, bf16[1024,128]{1,0:T(8,128)(2,1)}, u32[]{:S(2)}) copy-start(bf16[1024,128]{1,0:T(8,128)(2,1)} %param.20) | copy-start | bytes 786436
  523.7 186.3 %copy-start.35 = (bf16[1024,128]{1,0:T(8,128)(2,1)S(1)}, bf16[1024,128]{1,0:T(8,128)(2,1)}, u32[]{:S(2)}) copy-start(bf16[1024,128]{1,0:T(8,128)(2,1)} %param.21) | copy-start | bytes 786436
  524.8 187.0 %copy-start.39 = (f32[1024]{0:T(1024)S(1)}, f32[1024]{0:T(1024)}, u32[]{:S(2)}) copy-start(f32[1024]{0:T(1024)} %param.18) | copy-start | bytes 12292
  524.8 187.0 %copy-start.61 = (f32[128]{0:T(128)S(1)}, f32[128]{0:T(128)}, u32[]{:S(2)}) copy-start(f32[128]{0:T(128)} %copy-done.60) | copy-start | bytes 1540
  709.8 4.3 copy-start.40
  711.7 3.4 copy-start.12
  711.8 391.5 %all-reduce.14.cloned.1.call-start = ((), (), s32[]{:S(2)}) async-start(), calls=%async_computation.9 | async-start | bytes 3276800 | tf_op jit(solution)/shard_map/psum | solution.py:326
  715.1 3.9 copy-start.4
  715.1 3.9 copy-start.23
  719.1 2.1 copy-start.21
  721.2 24.7 %copy-start.64 = (bf16[1024]{0:T(1024)(128)(2,1)S(1)}, bf16[1024]{0:T(1024)(128)(2,1)}, u32[]{:S(2)}) copy-start(bf16[1024]{0:T(1024)(128)(2,1)} %get-tuple-element.330) | copy-start | bytes 6148
  721.2 122.6 %copy-start.8 = (bf16[128,1024]{1,0:T(8,128)(2,1)S(1)}, bf16[128,1024]{1,0:T(8,128)(2,1)}, u32[]{:S(2)}) copy-start(bf16[128,1024]{1,0:T(8,128)(2,1)} %all-reduce.10.cloned.1.call-done) | copy-start | bytes 786436
  1103.2 5.4 copy-start.31
  1103.2 6.3 copy-start.24
  (15 other events, 20.2 us)
Sparse Core Ops, SparseCore 0:
  12.8 75.7 all-gather.1
  106.8 33.9 all-reduce.9
  449.0 36.7 all-reduce.11
  519.0 189.8 reduce-scatter.1
  712.0 32.5 all-reduce.15
  748.1 355.0 all-reduce.13
where the time goes:
time: 1120 us
  waiting for transfers between devices  704 us (63%)
  blocking collectives  229 us (20%)
  local copies, waits for them, and re-layouts  65.1 us (6%)
  matrix products  57 us (5%)
  other arithmetic  30.8 us (3%)
  between operations  15.1 us (1%)
    psum x1, waiting for transfers between devices, local(): lax.psum(grad_query.astype(jnp.bfloat16), 'ctx').astype(jnp.float32)  257 us
    reduce_scatter x1, waiting for transfers between devices, local(): lax.psum_scatter(d_blocks.reshape(all_rows, 2 * key_width).astype(jnp.bfl...  184 us
    all_to_all x2, blocking collectives, dispatch(): lax.all_to_all(buffer.reshape(group_count, local_experts * capacity, mode...  126 us
    all_to_all x2, waiting for transfers between devices, collect(): lax.all_to_all(outgoing.reshape(group_count, local_experts * capacity, mo...  103 us
    psum x1, blocking collectives, local(): lax.psum(grad_gain_first.astype(jnp.bfloat16), 'ctx').astype(jnp.float32)  96.7 us
    all_gather x1, waiting for transfers between devices, local(): gathered = lax.all_gather(keys_values, 'ctx', axis=0, tiled=True)  74.1 us
    psum x1, waiting for transfers between devices, local(): lax.psum(d_second_part.astype(jnp.bfloat16), 'wa').astype(jnp.float32)  36.5 us
    psum x1, waiting for transfers between devices, local(): lax.psum(jnp.dot(context, w_out, preferred_element_type=jnp.float32).asty...  28.6 us
  transfers between devices with their start and end apart: 8, of which 8 were waited for; matrix products, arithmetic and copies ran while one was open for 3% of the time, Pallas kernels for 0%

commit v1 on v0

v1 whole, which is shorter than its diff:
```python
import jax
import jax.numpy as jnp
from jax import lax
from jax.experimental import pallas as pl
from jax.experimental.pallas import tpu as pltpu
from jax.sharding import PartitionSpec as P

HEAD_DIM = 64
CHUNK = 8

epsilon = 1e-06
f32 = jnp.float32
bf16 = jnp.bfloat16
CORE_SWAP = [(0, 1), (1, 0), (2, 3), (3, 2)]
CHIP_SWAP = [(0, 2), (2, 0), (1, 3), (3, 1)]
PARTNER = [(i, i ^ 2) for i in range(32)]
VMEM = pl.BlockSpec(memory_space=pltpu.VMEM)
SMEM = pl.BlockSpec(memory_space=pltpu.SMEM)


def dot(a, b):
    return jnp.dot(a, b, preferred_element_type=f32)


def dot_nt(a, b):
    return lax.dot_general(a, b, (((1,), (1,)), ((), ())), preferred_element_type=f32)


def dot_tn(a, b):
    return lax.dot_general(a, b, (((0,), (0,)), ((), ())), preferred_element_type=f32)


def exchange(value, axes):
    return lax.all_to_all(value, axes, split_axis=0, concat_axis=0, tiled=True)


def shape(dims, dtype=bf16):
    return jax.ShapeDtypeStruct(dims, dtype)


def on_device(kernel, name, in_specs, outs, scratch=(), megabytes=16, flops=0):
    return pl.pallas_call(
        kernel,
        out_shape=outs,
        in_specs=in_specs,
        out_specs=tuple(VMEM for _ in outs),
        scratch_shapes=list(scratch),
        cost_estimate=pl.CostEstimate(flops=flops, bytes_accessed=8_000_000, transcendentals=0) if flops else None,
        compiler_params=pltpu.CompilerParams(vmem_limit_bytes=megabytes * 1024 * 1024),
        name=name,
    )


def local_positions(first_row, row_count, device_rows, group_count):
    numbers = first_row + jnp.arange(row_count, dtype=jnp.int32)
    owner_index = numbers // device_rows
    within = numbers % device_rows
    halfway = device_rows // 2
    return jnp.where(
        within < halfway,
        owner_index * halfway + within,
        (2 * group_count - 1 - owner_index) * halfway + within - halfway,
    )


def angles_of(block):
    positions = local_positions(block * 128, 128, 128, 32)
    inverse = jnp.power(10000.0, -2.0 * jnp.arange(32, dtype=f32) / HEAD_DIM)
    return positions.astype(f32)[:, None] * inverse[None, :]


def lanes_of(dims):
    return lax.broadcasted_iota(jnp.int32, dims, len(dims) - 1)


def swap_halves(x):
    return pltpu.roll(x, 64, 1)


def turn_lanes(x, cosine, sine):
    lead = (lanes_of(x.shape) & 63) < 32
    return x * cosine + jnp.where(lead, pltpu.roll(x, 96, 1), pltpu.roll(x, 32, 1)) * sine


def turn_rows(x, cosine, sine):
    lead, trail = x[0:32], x[32:64]
    return jnp.concatenate([lead * cosine - trail * sine, trail * cosine + lead * sine], 0)


def prelude_kernel(
    at_ref, tokens_ref, gain_ref, wq_ref, wk_ref, wv_ref, cos_ref, sin_ref, cos_t_ref, sin_t_ref,
    kv_ref, normed_ref, q_ref, q_give_ref,
):
    side = at_ref[2]
    x = tokens_ref[...].astype(f32)
    root = lax.rsqrt(jnp.mean(x * x, -1, keepdims=True) + epsilon)
    normed = (x * root * gain_ref[...]).astype(bf16)
    normed_ref[...] = normed
    k = dot(normed, wk_ref[...])
    v = dot(normed, wv_ref[...])
    low = lanes_of(k.shape) < 64
    heads = (
        jnp.where(low, k, swap_halves(v)),
        jnp.where(low, swap_halves(k), v),
    )
    heads = [turn_lanes(y, cos_ref[...], sin_ref[...]).astype(bf16) for y in heads]
    for d in range(32):
        kv_ref[d] = heads[(d >> 1) & 1]
    qt = dot(normed, wq_ref[...]).T
    turned = [
        turn_rows(qt[64 * h : 64 * h + 64], cos_t_ref[...], sin_t_ref[...]).astype(bf16) * jnp.asarray(1.0 / HEAD_DIM, bf16)
        for h in range(4)
    ]
    pairs = [jnp.concatenate(turned[2 * j : 2 * j + 2], 0).astype(f32) for j in range(2)]
    q_ref[...] = jnp.where(side == 0, pairs[0], pairs[1]).astype(bf16)
    q_give_ref[...] = jnp.where(side == 0, pairs[1], pairs[0]).astype(bf16)


def to_columns(side, own_ref, other_ref, out_ref, first_row):
    for g in range(2):
        own = own_ref[64 * g : 64 * g + 64, :].astype(f32)
        other = other_ref[64 * g : 64 * g + 64, :].astype(f32)
        zero = jnp.where(side == 0, own, other)
        one = jnp.where(side == 0, other, own)
        low = lanes_of(own.shape) < 64
        out_ref[first_row : first_row + 64, 128 * g : 128 * g + 128] = jnp.where(
            low, zero, swap_halves(one)
        ).astype(bf16)
        out_ref[first_row : first_row + 64, 256 + 128 * g : 384 + 128 * g] = jnp.where(
            low, swap_halves(zero), one
        ).astype(bf16)


def from_columns(side, columns, g):
    a = columns[:, 128 * g : 128 * g + 128]
    b = columns[:, 256 + 128 * g : 384 + 128 * g]
    low = lanes_of(a.shape) < 64
    zero = jnp.where(low, a, swap_halves(b))
    one = jnp.where(low, swap_halves(a), b)
    return jnp.where(side == 0, zero, one), jnp.where(side == 0, one, zero)


def masked_early(scores, base, c):
    rows = lax.broadcasted_iota(jnp.int32, scores.shape, 0) + base * 64
    columns = lanes_of(scores.shape)
    block = (c & 29) + ((columns >> 6) & 1) * 2
    return jnp.where(rows <= block * 64 + (columns & 63), scores, -1e30)


def masked_late(scores, base, c):
    rows = lax.broadcasted_iota(jnp.int32, scores.shape, 0)
    columns = lanes_of(scores.shape)
    block = (c & 29) + ((columns >> 6) & 1) * 2
    key_at = (63 - base - (rows >> 6)) * 64 + (rows & 63)
    return jnp.where(key_at <= (63 - block) * 64 + (columns & 63), scores, -1e30)


def attend_kernel(
    at_ref, own_ref, other_ref, kv_ref,
    mine_ref, give_ref, o_ref, lse_ref,
    q_ref, m_ref, l_ref, acc_ref,
):
    c, side = at_ref[3], at_ref[2]
    to_columns(side, own_ref, other_ref, q_ref, 0)
    q_ref[64:128, :] = jnp.zeros((64, 512), bf16)
    m_ref[...] = jnp.full(m_ref.shape, -1e30, f32)
    l_ref[...] = jnp.zeros(l_ref.shape, f32)
    acc_ref[...] = jnp.zeros(acc_ref.shape, f32)

    def step(base, keys_half, cols, mask):
        kv = kv_ref[base : base + CHUNK, keys_half, :].reshape(CHUNK * 64, 128)
        s = dot(kv, q_ref[:, cols])
        if mask is not None:
            s = mask(s, base, c)
        m_old = m_ref[:, cols]
        m_new = jnp.maximum(m_old, jnp.max(s, 0, keepdims=True))
        p = jnp.exp(s - m_new)
        factor = jnp.exp(m_old - m_new)
        m_ref[:, cols] = m_new
        l_ref[:, cols] = l_ref[:, cols] * factor + jnp.sum(p, 0, keepdims=True)
        acc_ref[:, cols] = acc_ref[:, cols] * factor + dot_tn(kv, p.astype(bf16))

    early, late = slice(0, 64), slice(64, 128)
    first, second = slice(0, 256), slice(256, 512)
    for base in range(0, 32, CHUNK):
        step(base, early, second, None)

        @pl.when(base <= (c | 2))
        def _():
            step(base, early, first, masked_early)

        @pl.when(base + CHUNK > (c & 29))
        def _():
            step(base, late, second, masked_late)

    total = l_ref[...]
    o_ref[...] = acc_ref[64:128, :] / total
    lse_ref[...] = m_ref[...] + jnp.log(total)
    for g in range(2):
        own, other = from_columns(side, o_ref[...], g)
        mine_ref[64 * g : 64 * g + 64, :] = own.astype(bf16)
        give_ref[64 * g : 64 * g + 64, :] = other.astype(bf16)


def reverse_kernel(
    at_ref, own_ref, other_ref, kv_ref, do_own_ref, do_other_ref, o_ref, lse_ref,
    cos_ref, sin_ref, cos2_ref, sin2_ref,
    dq_ref, dq_give_ref, dkv_ref,
    q_ref, do_ref, delta_ref, acc_ref,
):
    c, side = at_ref[3], at_ref[2]
    to_columns(side, own_ref, other_ref, q_ref, 0)
    q_ref[64:128, :] = jnp.zeros((64, 512), bf16)
    to_columns(side, do_own_ref, do_other_ref, do_ref, 64)
    do_ref[0:64, :] = jnp.zeros((64, 512), bf16)
    delta_ref[...] = jnp.sum(do_ref[64:128, :].astype(f32) * o_ref[...], 0, keepdims=True)
    acc_ref[...] = jnp.zeros(acc_ref.shape, f32)

    def step(base, keys_half, cols, mask, add):
        kv = kv_ref[base : base + CHUNK, keys_half, :].reshape(CHUNK * 64, 128)
        q = q_ref[:, cols]
        do = do_ref[:, cols]
        s = dot(kv, q)
        if mask is not None:
            s = mask(s, base, c)
        p = jnp.exp(s - lse_ref[:, cols])
        dp = dot(kv, do)
        ds = (p * (dp - delta_ref[:, cols])).astype(bf16)
        acc_ref[:, cols] += dot_tn(kv, ds)
        dkv = (dot_nt(ds, q) + dot_nt(p.astype(bf16), do)).reshape(CHUNK, 64, 128)
        if add:
            dkv += dkv_ref[base : base + CHUNK, keys_half, :].astype(f32)
        dkv_ref[base : base + CHUNK, keys_half, :] = dkv.astype(bf16)

    early, late = slice(0, 64), slice(64, 128)
    first, second = slice(0, 256), slice(256, 512)
    for base in range(0, 32, CHUNK):
        step(base, early, second, None, False)

        @pl.when(base <= (c | 2))
        def _():
            step(base, early, first, masked_early, True)

        @pl.when(base + CHUNK > (c & 29))
        def _():
            step(base, late, second, masked_late, False)

        @pl.when(base + CHUNK <= (c & 29))
        def _():
            dkv_ref[base : base + CHUNK, late, :] = jnp.zeros((CHUNK, 64, 128), bf16)

    for g in range(2):
        own, other = from_columns(side, acc_ref[0:64, :] * (1.0 / HEAD_DIM), g)
        here = slice(64 * g, 64 * g + 64)
        dq_ref[here, :] = turn_rows(own, cos_ref[...], -sin_ref[...]).astype(bf16)
        dq_give_ref[here, :] = turn_rows(other, cos2_ref[...], -sin2_ref[...]).astype(bf16)


def mix_kernel(at_ref, mine_ref, got_ref, w_out_ref, context_ref, keep_ref, give_ref):
    core, side = at_ref[1], at_ref[2]
    mine, got = mine_ref[...].astype(f32), got_ref[...].astype(f32)
    context_ref[0:128, :] = jnp.where(side == 0, mine, got).astype(bf16)
    context_ref[128:256, :] = jnp.where(side == 0, got, mine).astype(bf16)
    mixed = dot_tn(context_ref[...], w_out_ref[...])
    top, bottom = mixed[0:64], mixed[64:128]
    keep_ref[...] = jnp.where(core == 0, top, bottom).astype(bf16)
    give_ref[...] = jnp.where(core == 0, bottom, top).astype(bf16)


def selection(rank_ref, first, count):
    slot = lax.broadcasted_iota(jnp.int32, (64, 128), 0).astype(f32)
    return jnp.concatenate([(slot == rank_ref[e : e + 1, :]).astype(f32) for e in range(first, first + count)], 0)


def route_kernel(
    at_ref, tokens_ref, mine_ref, theirs_ref, gain_ref, router_ref, rank_ref, cot_ref,
    middle_ref, normed_ref, gates_ref, out_ref,
):
    wa, core = at_ref[0], at_ref[1]
    for half in range(2):
        here = slice(64 * half, 64 * half + 64)
        mixed = jnp.where(core == half, mine_ref[...].astype(f32), theirs_ref[...].astype(f32))
        middle = tokens_ref[here, :].astype(f32) + mixed
        middle_ref[here, :] = middle
        root = lax.rsqrt(jnp.mean(middle * middle, -1, keepdims=True) + epsilon)
        normed_ref[here, :] = (middle * root * gain_ref[...]).astype(bf16)
    logits = dot_nt(router_ref[...], normed_ref[...])
    member = rank_ref[...] >= 0.0
    top = jnp.max(jnp.where(member, logits, -1e30), 0, keepdims=True)
    raised = jnp.where(member, jnp.exp(jnp.where(member, logits - top, 0.0)), 0.0)
    gates_ref[...] = raised / jnp.sum(raised, 0, keepdims=True)
    quarter = normed_ref[:, pl.ds(pl.multiple_of(wa * 256, 256), 256)]
    for first in range(0, 32, 4):
        chosen = selection(rank_ref, first, 4)
        weights = jnp.concatenate(
            [
                jnp.sum(chosen[64 * n : 64 * n + 64] * gates_ref[first + n : first + n + 1, :], 1, keepdims=True)
                for n in range(4)
            ],
            0,
        )
        chosen = chosen.astype(bf16)
        here = slice(64 * first, 64 * first + 256)
        out_ref[here, 0:256] = dot(chosen, quarter).astype(bf16)
        out_ref[here, 256:512] = (weights * dot(chosen, cot_ref[...])).astype(bf16)


def expert_kernel(
    in_ref, w0_ref, w1_ref, w2_ref, w3_ref,
    out_ref, act_ref, dgate_ref, dup_ref,
    gate_ref, up_ref, down_ref,
):
    for p, w in enumerate((w0_ref, w1_ref, w2_ref, w3_ref)):
        here = slice(128 * p, 128 * p + 128)
        gate_ref[:, here] = w[0]
        up_ref[:, here] = w[1]
        for n in range(8):
            down_ref[here, 128 * n : 128 * n + 128] = w[2, 128 * n : 128 * n + 128, :]
    gate_pre = jnp.zeros((512, 512), f32)
    up_pre = jnp.zeros((512, 512), f32)
    d_act = jnp.zeros((512, 512), f32)
    for q in range(4):
        here = slice(256 * q, 256 * q + 256)
        x = in_ref[:, q, :, 0:256].reshape(512, 256)
        gate_pre += dot(x, gate_ref[here, :])
        up_pre += dot(x, up_ref[here, :])
        d_act += dot_nt(in_ref[:, q, :, 256:512].reshape(512, 256), down_ref[:, here])
    sigma = jax.nn.sigmoid(gate_pre)
    act_ref[...] = (gate_pre * sigma * up_pre).astype(bf16)
    dgate_ref[...] = (d_act * up_pre * sigma * (1.0 + gate_pre * (1.0 - sigma))).astype(bf16)
    dup_ref[...] = (d_act * gate_pre * sigma).astype(bf16)
    for q in range(4):
        here = slice(256 * q, 256 * q + 256)
        part = dot(act_ref[...], down_ref[:, here])
        out_ref[:, q, :, 0:256] = part.astype(bf16).reshape(32, 16, 256)
        d_x = dot_nt(dgate_ref[...], gate_ref[here, :]) + dot_nt(dup_ref[...], up_ref[here, :])
        out_ref[:, q, :, 256:512] = d_x.astype(bf16).reshape(32, 16, 256)


def expert_grad_kernel(in_ref, act_ref, dgate_ref, dup_ref, near_ref, far_ref):
    for q in range(4):
        here = slice(256 * q, 256 * q + 256)
        x = in_ref[:, q, :, 0:256].reshape(512, 256)
        d = in_ref[:, q, :, 256:512].reshape(512, 256)
        g_gate = dot_tn(x, dgate_ref[...]).astype(bf16)
        g_up = dot_tn(x, dup_ref[...]).astype(bf16)
        g_down = dot_tn(act_ref[...], d).astype(bf16)
        for p in range(4):
            to = near_ref if p < 2 else far_ref
            to[p % 2, 0, here, :] = g_gate[:, 128 * p : 128 * p + 128]
            to[p % 2, 1, here, :] = g_up[:, 128 * p : 128 * p + 128]
            for n in range(2):
                at = 256 * q + 128 * n
                to[p % 2, 2, at : at + 128, :] = g_down[128 * p : 128 * p + 128, 128 * n : 128 * n + 128]


def combine_kernel(back_ref, rank_ref, gates_ref, cot_ref, sent_ref, moe_ref, dgates_ref):
    d_normed = jnp.zeros((128, 256), f32)
    moe = jnp.zeros((128, 256), f32)
    for first in range(0, 32, 4):
        here = slice(64 * first, 64 * first + 256)
        chosen = selection(rank_ref, first, 4)
        gated = jnp.concatenate(
            [chosen[64 * n : 64 * n + 64] * gates_ref[first + n : first + n + 1, :] for n in range(4)], 0
        )
        high = gated.astype(bf16)
        low = (gated - high.astype(f32)).astype(bf16)
        picked = chosen.astype(bf16)
        part = back_ref[here, 0:256]
        d_normed += dot_tn(picked, back_ref[here, 256:512])
        moe += dot_tn(high, part) + dot_tn(low, part)
        along = jnp.sum(dot(picked, cot_ref[...]) * part.astype(f32), 1, keepdims=True)
        placed = chosen * along
        for n in range(4):
            dgates_ref[first + n : first + n + 1, :] = jnp.sum(
                placed[64 * n : 64 * n + 64], 0, keepdims=True
            )
    moe_ref[...] = moe.astype(bf16)
    sent_ref[0:128, :] = d_normed.astype(bf16)
    sent_ref[128:144, 0:128] = dgates_ref[0:16, :].astype(bf16)
    sent_ref[128:144, 128:256] = dgates_ref[16:32, :].astype(bf16)


def second_norm_kernel(
    at_ref, own_ref, across_ref, beside_ref, diagonal_ref, gates_ref, middle_ref, normed_ref, cot_ref,
    gain_ref, router_ref, w_out_ref, context_ref,
    dmiddle_ref, dmine_ref, dgive_ref, parts_ref, dnormed_ref, extra_ref,
):
    wa, side = at_ref[0], at_ref[2]
    pieces = [(own_ref, 0), (across_ref, 2), (beside_ref, 1), (diagonal_ref, 3)]
    for ref, flip in pieces:
        at = pl.multiple_of((wa ^ flip) * 256, 256)
        dnormed_ref[:, pl.ds(at, 256)] = ref[0:128, :].astype(f32)
    terms = [
        jnp.concatenate([ref[128:144, 0:128], ref[128:144, 128:256]], 0).astype(f32) for ref, _ in pieces
    ]
    d_gates = (terms[0] + terms[1]) + (terms[2] + terms[3])
    gates = gates_ref[...]
    d_logits = (gates * (d_gates - jnp.sum(gates * d_gates, 0, keepdims=True))).astype(bf16)
    gain = gain_ref[...]
    d_normed = dnormed_ref[...] + dot_tn(d_logits, router_ref[...])
    middle = middle_ref[...]
    root = lax.rsqrt(jnp.mean(middle * middle, -1, keepdims=True) + epsilon)
    unit = middle * root
    scaled = d_normed * gain
    gain_grad = jnp.sum(d_normed * unit, 0, keepdims=True)
    d_middle = cot_ref[...].astype(f32) + root * (
        scaled - unit * jnp.mean(scaled * unit, -1, keepdims=True)
    )
    dmiddle_ref[...] = d_middle
    d_mixed = d_middle.astype(bf16)
    d_context = dot_nt(w_out_ref[...], d_mixed)
    dmine_ref[...] = jnp.where(side == 0, d_context[0:128], d_context[128:256]).astype(bf16)
    dgive_ref[...] = jnp.where(side == 0, d_context[128:256], d_context[0:128]).astype(bf16)
    router_grad = dot(d_logits, normed_ref[...])
    extra_ref[...] = jnp.zeros(extra_ref.shape, f32)
    for q in range(4):
        here = slice(256 * q, 256 * q + 256)
        extra_ref[:, q, :] = router_grad[:, here]
        extra_ref[:, 4 + q, :] = jnp.broadcast_to(gain_grad[:, here], (32, 256))
        parts_ref[8 * q : 8 * q + 8, 0:32, :] = (
            dot(context_ref[...], d_mixed[:, here]).astype(bf16).reshape(8, 32, 256)
        )
    parts_ref[:, 32:48, :] = extra_ref[...].astype(bf16)


def late_kernel(
    at_ref, back_ref, cos_ref, sin_ref, normed_ref, wk_ref, wv_ref, first_ref, query_ref, early_ref,
    parts_ref, keep_ref, give_ref,
):
    core = at_ref[1]
    parts_ref[:, 0:32, :] = query_ref[...]
    parts_ref[:, 32:80, :] = early_ref[...]
    heads = []
    for j in range(2):
        total = jnp.zeros((128, 128), f32)
        for d in range(32):
            if (d >> 1) & 1 == j:
                total += back_ref[d].astype(f32)
        heads.append(turn_lanes(total, cos_ref[...], -sin_ref[...]))
    low = lanes_of((128, 128)) < 64
    d_k = jnp.where(low, heads[0], swap_halves(heads[1])).astype(bf16)
    d_v = jnp.where(low, swap_halves(heads[0]), heads[1]).astype(bf16)
    parts_ref[:, 80:112, 0:128] = dot_tn(normed_ref[...], d_k).astype(bf16).reshape(32, 32, 128)
    parts_ref[:, 80:112, 128:256] = dot_tn(normed_ref[...], d_v).astype(bf16).reshape(32, 32, 128)
    first = first_ref[...] + dot_nt(d_k, wk_ref[...]) + dot_nt(d_v, wv_ref[...])
    keep_ref[...] = jnp.where(core == 0, first[0:64], first[64:128]).astype(bf16)
    give_ref[...] = jnp.where(core == 0, first[64:128], first[0:64]).astype(bf16)


def share_kernel(in_ref, gain_ref, out_ref, gain2_ref, total_ref):
    total_ref[...] = jnp.sum(in_ref[...].astype(f32), 0)
    gain2_ref[...] = total_ref[68:72, :]
    total_ref[68:72, :] = gain_ref[...].astype(f32)
    out_ref[...] = jnp.broadcast_to(total_ref[...].astype(bf16)[None], (32, 112, 256))


def sum_over_wa(keep, give):
    got = lax.ppermute(give, "wa", CORE_SWAP)
    pair = (keep.astype(f32) + got.astype(f32)).astype(bf16)
    other = lax.ppermute(pair, "wa", CHIP_SWAP)
    mine = (pair.astype(f32) + other.astype(f32)).astype(bf16)
    return mine, lax.ppermute(mine, "wa", CORE_SWAP)


def pieces_over_wa(part):
    across = lax.ppermute(part, "wa", CHIP_SWAP)
    beside = lax.ppermute(part, "wa", CORE_SWAP)
    return across, beside, lax.ppermute(across, "wa", CORE_SWAP)


def local(
    tokens,
    norm1_gain,
    w_query,
    key_weight,
    value_weight,
    w_out,
    norm2_gain,
    w_router,
    w_gate,
    w_up,
    w_down,
    routes,
    cotangent,
):
    ctx = lax.axis_index("ctx").astype(jnp.int32)
    wa = lax.axis_index("wa").astype(jnp.int32)
    core, chip, side = wa % 2, wa // 2, (ctx >> 1) & 1
    at = jnp.stack([wa, core, side, ctx])
    rows, width, experts = 128, 1024, 32

    angles = angles_of(ctx)
    cosine, sine = jnp.cos(angles), jnp.sin(angles)
    one, zero = jnp.ones((rows, 64), f32), jnp.zeros((rows, 64), f32)
    cos_lanes = jnp.concatenate([cosine, cosine, one], 1)
    sin_lanes = jnp.concatenate([-sine, sine, zero], 1)
    cos_rows, sin_rows = cosine.T, sine.T
    gain1 = norm1_gain.reshape(1, width)
    kv_send, normed1, q_own, q_give = on_device(
        prelude_kernel,
        "prelude",
        [SMEM] + [VMEM] * 9,
        (shape((32, rows, 128)), shape((rows, width)), shape((rows, 128)), shape((rows, 128))),
    )(
        at, tokens, gain1, w_query, key_weight, value_weight, cos_lanes, sin_lanes, cos_rows, sin_rows
    )
    kv = exchange(kv_send, "ctx")
    q_other = lax.ppermute(q_give, "ctx", PARTNER)

    member = jnp.any(
        routes[:, :, None] == jnp.arange(experts, dtype=jnp.int32)[None, None, :], axis=1
    )
    lower = (jnp.arange(rows)[:, None] >= jnp.arange(rows)[None, :]).astype(bf16)
    rank = jnp.where(member, dot(lower, member.astype(bf16)) - 1.0, -1.0).T
    cot_quarter = lax.dynamic_slice_in_dim(cotangent, wa * 256, 256, 1)
    router_t = w_router.T
    gain2 = norm2_gain.reshape(1, width)
    down_lanes = w_down[0].reshape(128, 8, 128).transpose(1, 0, 2).reshape(width, 128)
    weights = jnp.stack([w_gate[0], w_up[0], down_lanes])

    kv, weights, rank, q_other = lax.optimization_barrier((kv, weights, rank, q_other))
    w_across, w_beside, w_diagonal = pieces_over_wa(weights)
    ctx_mine, ctx_give, context_o, lse = on_device(
        attend_kernel,
        "attend",
        [SMEM] + [VMEM] * 3,
        (shape((rows, 128)), shape((rows, 128)), shape((64, 512), f32), shape((1, 512), f32)),
        [
            pltpu.VMEM((128, 512), bf16),
            pltpu.VMEM((1, 512), f32),
            pltpu.VMEM((1, 512), f32),
            pltpu.VMEM((128, 512), f32),
        ],
    )(at, q_own, q_other, kv)
    ctx_got = lax.ppermute(ctx_give, "ctx", PARTNER)
    context_t, mix_keep, mix_give = on_device(
        mix_kernel,
        "mix",
        [SMEM] + [VMEM] * 3,
        (shape((256, rows)), shape((64, width)), shape((64, width))),
    )(at, ctx_mine, ctx_got, w_out)
    mine, theirs = sum_over_wa(mix_keep, mix_give)
    middle, normed2, gates, outgoing = on_device(
        route_kernel,
        "route",
        [SMEM] + [VMEM] * 7,
        (
            shape((rows, width), f32),
            shape((rows, width)),
            shape((experts, rows), f32),
            shape((2048, 512)),
        ),
    )(at, tokens, mine, theirs, gain2, router_t, rank, cot_quarter)

    outgoing, w_across, w_beside, w_diagonal = lax.optimization_barrier(
        (outgoing, w_across, w_beside, w_diagonal)
    )
    arrived = exchange(outgoing.reshape(128, 16, 512), ("ctx", "wa")).reshape(32, 4, 16, 512)
    returning, active, d_gate, d_up = on_device(
        expert_kernel,
        "experts",
        [VMEM] * 5,
        (shape((32, 4, 16, 512)), shape((512, 512)), shape((512, 512)), shape((512, 512))),
        [pltpu.VMEM((width, 512), bf16), pltpu.VMEM((width, 512), bf16), pltpu.VMEM((512, width), bf16)],
        megabytes=24,
    )(arrived, weights, w_across, w_beside, w_diagonal)
    back = exchange(returning.reshape(128, 16, 512), ("ctx", "wa")).reshape(2048, 512)
    near, far = on_device(
        expert_grad_kernel,
        "expert_grads",
        [VMEM] * 4,
        (shape((2, 3, width, 128)), shape((2, 3, width, 128))),
        flops=3_000_000_000,
    )(arrived, active, d_gate, d_up)
    far = lax.ppermute(far, "wa", CORE_SWAP)
    near = near.astype(f32) + far.astype(f32)
    near_own, near_give = near[0], near[1].astype(bf16)
    back, near_own, near_give = lax.optimization_barrier((back, near_own, near_give))
    sent, moe = on_device(
        combine_kernel,
        "combine",
        [VMEM] * 4,
        (shape((144, 256)), shape((rows, 256))),
        [pltpu.VMEM((32, 128), f32)],
    )(back, rank, gates, cot_quarter)

    pieces = pieces_over_wa(sent)
    pieces, moe, near_give = lax.optimization_barrier((pieces, moe, near_give))
    near_got = lax.ppermute(near_give, "wa", CHIP_SWAP)
    d_middle, do_own, do_give, parts = on_device(
        second_norm_kernel,
        "second_norm",
        [SMEM] + [VMEM] * 12,
        (
            shape((rows, width), f32),
            shape((rows, 128)),
            shape((rows, 128)),
            shape((32, 48, 256)),
        ),
        [pltpu.VMEM((rows, width), f32), pltpu.VMEM((32, 16, 256), f32)],
    )(
        at, sent, *pieces, gates, middle, normed2, cotangent, gain2, router_t, w_out, context_t
    )
    do_other = lax.ppermute(do_give, "ctx", PARTNER)

    angles2 = angles_of(ctx ^ 2)
    dq_own, dq_give, dkv = on_device(
        reverse_kernel,
        "reverse",
        [SMEM] + [VMEM] * 11,
        (shape((rows, 128)), shape((rows, 128)), shape((32, rows, 128))),
        [
            pltpu.VMEM((128, 512), bf16),
            pltpu.VMEM((128, 512), bf16),
            pltpu.VMEM((1, 512), f32),
            pltpu.VMEM((128, 512), f32),
        ],
    )(
        at, q_own, q_other, kv, do_own, do_other, context_o, lse,
        cos_rows, sin_rows, jnp.cos(angles2).T, jnp.sin(angles2).T,
    )
    dkv, near_got = lax.optimization_barrier((dkv, near_got))
    kv_back = exchange(dkv, "ctx")

    dq_got = lax.ppermute(dq_give, "ctx", PARTNER)
    d_query = jnp.where(
        side == 0, jnp.concatenate([dq_own, dq_got], 0), jnp.concatenate([dq_got, dq_own], 0)
    ).T
    parts_query = dot_tn(normed1, d_query).astype(bf16).reshape(32, 32, 256)
    first_query = dot_nt(d_query, w_query)
    kv_back, parts_query, first_query = lax.optimization_barrier((kv_back, parts_query, first_query))

    parts_all, first_keep, first_give = on_device(
        late_kernel,
        "late",
        [SMEM] + [VMEM] * 9,
        (shape((32, 112, 256)), shape((64, width)), shape((64, width))),
    )(
        at, kv_back, cos_lanes, sin_lanes, normed1, key_weight, value_weight, first_query,
        parts_query, parts,
    )
    parts_all, moe = lax.optimization_barrier((parts_all, moe))
    summed = exchange(parts_all, "ctx")
    moe_all = jnp.stack((moe,) + pieces_over_wa(moe))
    moe_all = moe_all.reshape(2, 2, rows, 256)
    moe_all = jnp.where(core == 0, moe_all, moe_all[::-1])
    moe_all = jnp.where(chip == 0, moe_all, moe_all[:, ::-1])
    moe_sum = moe_all.transpose(2, 1, 0, 3).reshape(rows, width).astype(f32)
    output = (middle + moe_sum).astype(bf16)
    near_all = near_own + near_got.astype(f32)
    g_down = near_all[2].reshape(8, 128, 128).transpose(1, 0, 2).reshape(128, width)
    first_mine, first_theirs = sum_over_wa(first_keep, first_give)
    d_first = jnp.where(
        core == 0, jnp.stack([first_mine, first_theirs]), jnp.stack([first_theirs, first_mine])
    ).reshape(rows, width).astype(f32)
    widened = tokens.astype(f32)
    root_first = lax.rsqrt(jnp.mean(widened * widened, -1, keepdims=True) + epsilon)
    unit_first = widened * root_first
    scaled_first = d_first * norm1_gain
    grad_gain_first = jnp.sum(d_first * unit_first, 0).astype(bf16).reshape(4, 256)
    grad_tokens = (
        d_middle
        + root_first
        * (scaled_first - unit_first * jnp.mean(scaled_first * unit_first, -1, keepdims=True))
    ).astype(bf16)
    shared, out_gain2 = on_device(
        share_kernel,
        "share",
        [VMEM] * 2,
        (shape((32, 112, 256)), shape((4, 256), f32)),
        [pltpu.VMEM((112, 256), f32)],
    )(summed, grad_gain_first)
    spread_out = exchange(shared, "ctx").astype(f32)

    out_query = spread_out[:, 0:32].reshape(width, 256)
    out_out = spread_out[:, 32:64].reshape(4, 256, 256).transpose(1, 0, 2).reshape(256, width)
    out_router = spread_out[:, 64:68].reshape(experts, width).T
    return (
        output,
        grad_tokens,
        jnp.sum(spread_out[:, 68:72], 0).reshape(width),
        out_query,
        spread_out[:, 80:112, :128].reshape(width, 128),
        spread_out[:, 80:112, 128:].reshape(width, 128),
        out_out,
        out_gain2.reshape(width),
        out_router,
        near_all[0][None],
        near_all[1][None],
        g_down[None],
    )


def solution(mesh):
    in_specs = (
        P("ctx", None),
        P(),
        P(None, "wa"),
        P(None, "wa"),
        P(None, "wa"),
        P("wa", None),
        P(),
        P(),
        P("ctx", None, "wa"),
        P("ctx", None, "wa"),
        P("ctx", "wa", None),
        P("ctx", None),
        P("ctx", None),
    )
    out_specs = (
        P("ctx", None),
        P("ctx", None),
        P(),
        P(None, "wa"),
        P(None, "wa"),
        P(None, "wa"),
        P("wa", None),
        P(),
        P(),
        P("ctx", None, "wa"),
        P("ctx", None, "wa"),
        P("ctx", "wa", None),
    )
    return jax.shard_map(local, mesh=mesh, in_specs=in_specs, out_specs=out_specs, check_vma=False)
```

time: 1120 us -> 293 us (0.26)
  waiting for transfers between devices: 704 us -> 129 us
  blocking collectives: 229 us -> 35.6 us
  matrix products: 57 us -> 2.22 us
  starting transfers between devices: 10.7 us -> 43.1 us
  Pallas kernels: 0 us -> 29.7 us
  local copies, waits for them, and re-layouts: 65.1 us -> 41 us
  other arithmetic: 30.8 us -> 9.22 us
  between operations: 15.1 us -> 1.41 us
    psum x4 -> x0, waiting for transfers between devices: 344 us -> none  [the longest x1 257 us: local(): lax.psum(grad_query.astype(jnp.bfloat16), 'ctx').astype(jnp.float32)]
    reduce_scatter x1 -> x0, waiting for transfers between devices: 184 us -> none  [local(): lax.psum_scatter(d_blocks.reshape(all_rows, 2 * key_width).astype(jnp.bfl...]
    psum x2 -> x0, blocking collectives: 102 us -> none  [the longest x1 96.7 us: local(): lax.psum(grad_gain_first.astype(jnp.bfloat16), 'ctx').astype(jnp.float32)]
    all_to_all x2 -> x1, blocking collectives: 126 us -> 35.6 us  [exchange(): return lax.all_to_all(value, axes, split_axis=0, concat_axis=0, tiled=True)]
    all_gather x1 -> x0, waiting for transfers between devices: 74.1 us -> none  [local(): gathered = lax.all_gather(keys_values, 'ctx', axis=0, tiled=True)]
    ppermute x0 -> x21, waiting for transfers between devices: none -> 64.9 us  [the longest x2 25.7 us: sum_over_wa(): other = lax.ppermute(pair, 'wa', CHIP_SWAP)]
    dot_general x54 -> x3, matrix products: 57 us -> 2.22 us  [the longest x1 1.15 us: dot_nt(): lax.dot_general(a, b, (((1,), (1,)), ((), ())), preferred_element_type=f32)]
    all_to_all x2 -> x5, waiting for transfers between devices: 103 us -> 63.9 us  [exchange(): return lax.all_to_all(value, axes, split_axis=0, concat_axis=0, tiled=True)]
  transfers between devices with their start and end apart: 8 -> 26, of which waited for: 8 -> 17; matrix products, arithmetic and copies ran while one was open for 3% -> 5% of each run, Pallas kernels for 0% -> 6%
where the time goes in v1:
time: 293 us; the launch traced here: 291 us
  waiting for transfers between devices  129 us (44%)
  starting transfers between devices  43.1 us (15%)
  local copies, waits for them, and re-layouts  41 us (14%)
  blocking collectives  35.6 us (12%)
  Pallas kernels  29.7 us (10%)
  other arithmetic  9.22 us (3%)
    all_to_all x5, waiting for transfers between devices, exchange(): return lax.all_to_all(value, axes, split_axis=0, concat_axis=0, tiled=True)  63.9 us
    all_to_all x1, blocking collectives, exchange(): return lax.all_to_all(value, axes, split_axis=0, concat_axis=0, tiled=True)  35.6 us
    all_to_all x5, starting transfers between devices, exchange(): return lax.all_to_all(value, axes, split_axis=0, concat_axis=0, tiled=True)  32.3 us
    unnamed x154, local copies, waits for them, and re-layouts  28 us
    ppermute x2, waiting for transfers between devices, sum_over_wa(): other = lax.ppermute(pair, 'wa', CHIP_SWAP)  25.7 us
    ppermute x1, waiting for transfers between devices, local(): dq_got = lax.ppermute(dq_give, 'ctx', PARTNER)  9.39 us
    ppermute x1, waiting for transfers between devices, local(): q_other = lax.ppermute(q_give, 'ctx', PARTNER)  7.63 us
    pallas_call x1, Pallas kernels, local(): on_device(reverse_kernel, 'reverse', [SMEM] + [VMEM] * 11, (shape((rows,...  6.99 us
  transfers between devices with their start and end apart: 26, of which 17 were waited for; matrix products, arithmetic and copies ran while one was open for 5% of the time, Pallas kernels for 6%

profile of v1, /device:TPU:0, one launch (start us, length us, event | category | flops | bytes accessed | tf_op | source)
XLA Modules:
  0.0 291.1 jit_solution(1879812902439377616)
XLA Ops:
  1.2 0.8 multiply_sine_fusion.1
  2.2 0.9 copy-done
  3.1 1.0 copy-done.8
  4.2 0.9 copy-done.15
  5.1 0.9 copy-done.17
  6.8 2.2 prelude.1
  10.3 11.0 %all-to-all-start = ((bf16[32,128,128]{2,1,0:T(8,128)(2,1)}), bf16[32,128,128]{2,1,0:T(8,128)(2,1)S(1)}, u32[]{:S(2)}, u32[]{:S(2)}) async-start(bf16[32,128,128]{2,1,0:T(8,128)(2,1)} %get-tuple-element.71), calls=%async_computation | async-start | bytes 2097152 | tf_op jit(solution)/shard_map/all_to_all | solution.py:34
  21.3 1.9 collective-permute-start
  24.1 1.1 pad_maximum_fusion.w0_ref
  25.1 7.6 %collective-permute-done.other_ref = bf16[128,128]{1,0:T(8,128)(2,1)S(1)} collective-permute-done((bf16[128,128]{1,0:T(8,128)(2,1)S(1)}, bf16[128,128]{1,0:T(8,128)(2,1)S(1)}, u32[]{:S(2)}, u32[]{:S(2)}) %collective-permute-start) | collective-permute-done | bytes 32800 | tf_op jit(solution)/shard_map/ppermute | solution.py:509
  33.4 7.2 %all-to-all-done.kv_ref = bf16[32,128,128]{2,1,0:T(8,128)(2,1)S(1)} async-done(((bf16[32,128,128]{2,1,0:T(8,128)(2,1)}), bf16[32,128,128]{2,1,0:T(8,128)(2,1)S(1)}, u32[]{:S(2)}, u32[]{:S(2)}) %all-to-all-start) | async-done | bytes 1048608 | tf_op jit(solution)/shard_map/all_to_all | solution.py:34
  43.4 5.3 %attend.1 = (bf16[128,128]{1,0:T(8,128)(2,1)S(1)}, bf16[128,128]{1,0:T(8,128)(2,1)S(1)}, f32[64,512]{1,0:T(8,128)S(1)}, f32[1,512]{1,0:T(1,128)S(1)}) custom-call(s32[4]{0:T(128)S(1)} %copy-done.57, bf16[128,128]{1,0:T(8,128)(2,1)S(1)} %copy-done.37, bf16[128,128]{1,0:T(8,128)(2,1)S(1)} %copy-done.40, bf16[32,128,128]{2,1,0:T(8,128)(2,1)S(1)} %all-to-all-done.kv_ref), custom_call_target="tpu_custom_call" | custom-call | tf_op jit(solution)/shard_map/attend/pallas_call | solution.py:524
  50.6 3.3 %collective-permute-done.1.got_ref = bf16[128,128]{1,0:T(8,128)(2,1)S(1)} collective-permute-done((bf16[128,128]{1,0:T(8,128)(2,1)S(1)}, bf16[128,128]{1,0:T(8,128)(2,1)S(1)}, u32[]{:S(2)}, u32[]{:S(2)}) %collective-permute-start.1) | collective-permute-done | bytes 32800 | tf_op jit(solution)/shard_map/ppermute | solution.py:536
  54.6 0.8 mix.1
  56.0 2.4 collective-permute-done.5.w1_ref
  59.2 5.3 %collective-permute-done.3 = bf16[64,1024]{1,0:T(8,128)(2,1)S(1)} collective-permute-done((bf16[64,1024]{1,0:T(8,128)(2,1)S(1)}, bf16[64,1024]{1,0:T(8,128)(2,1)S(1)}, u32[]{:S(2)}, u32[]{:S(2)}) %collective-permute-start.3) | collective-permute-done | bytes 131104 | tf_op jit(solution)/shard_map/ppermute | solution.py:461
  64.6 0.8 constant_dynamic-slice_fusion.cot_ref
  65.9 0.8 copy-done.28
  68.8 1.6 route.1
  70.5 35.6 %all_to_all.30 = bf16[128,16,512]{2,1,0:T(8,128)(2,1)S(1)} all-to-all(bf16[128,16,512]{2,1,0:T(8,128)(2,1)S(1)} %bitcast.64), channel_id=1, replica_groups=mesh['ctx'=32,'wa'=4] {'ctx','wa'}, dimensions={0} | all-to-all | bytes 4194304 | tf_op jit(solution)/shard_map/all_to_all | solution.py:34
  106.2 5.5 %experts.1 = (bf16[32,4,16,512]{3,2,1,0:T(8,128)(2,1)S(1)}, bf16[512,512]{1,0:T(8,128)(2,1)S(1)}, bf16[512,512]{1,0:T(8,128)(2,1)S(1)}, bf16[512,512]{1,0:T(8,128)(2,1)S(1)}) custom-call(bf16[32,4,16,512]{3,2,1,0:T(8,128)(2,1)S(1)} %bitcast.61, bf16[3,1024,128]{2,1,0:T(8,128)(2,1)S(1)} %pad_maximum_fusion.w0_ref, ...), custom_call_target="tpu_custom_call" | custom-call | tf_op jit(solution)/shard_map/experts/pallas_call | solution.py:560
  111.7 3.0 %expert_grads.1 = (bf16[2,3,1024,128]{3,2,1,0:T(8,128)(2,1)S(1)}, bf16[2,3,1024,128]{3,2,1,0:T(8,128)(2,1)}) custom-call(bf16[32,4,16,512]{3,2,1,0:T(8,128)(2,1)S(1)} %bitcast.62, bf16[512,512]{1,0:T(8,128)(2,1)S(1)} %get-tuple-element.88.act_ref, bf16[512,512]{1,0:T(8,128)(2,1)S(1)} %get-tuple-element.89.dgate_ref, ...), custom_call_target="tpu_custom_call" | custom-call | flops 3000000000 | bytes 8000000 | tf_op jit(solution)/shard_map/expert_grads/pallas_call | solution.py:569
  114.7 1.2 copy-done.12
  115.8 4.6 %all-to-all-start.2 = ((bf16[128,16,512]{2,1,0:T(8,128)(2,1)}), bf16[128,16,512]{2,1,0:T(8,128)(2,1)S(1)}, u32[]{:S(2)}, u32[]{:S(2)}) async-start(bf16[128,16,512]{2,1,0:T(8,128)(2,1)} %bitcast.63), calls=%async_computation.2 | async-start | bytes 4194304 | tf_op jit(solution)/shard_map/all_to_all | solution.py:34
  120.5 2.2 convert_add_fusion
  122.7 1.0 fusion.1
  123.7 1.3 slice_bitcast_fusion
  125.0 25.9 %all-to-all-done.2 = bf16[128,16,512]{2,1,0:T(8,128)(2,1)S(1)} async-done(((bf16[128,16,512]{2,1,0:T(8,128)(2,1)}), bf16[128,16,512]{2,1,0:T(8,128)(2,1)S(1)}, u32[]{:S(2)}, u32[]{:S(2)}) %all-to-all-start.2) | async-done | bytes 2097184 | tf_op jit(solution)/shard_map/all_to_all | solution.py:34
  150.9 0.9 copy-done.22
  153.4 1.0 combine.1
  155.6 3.8 %collective-permute-done.9.across_ref = bf16[144,256]{1,0:T(8,128)(2,1)S(1)} collective-permute-done((bf16[144,256]{1,0:T(8,128)(2,1)S(1)}, bf16[144,256]{1,0:T(8,128)(2,1)S(1)}, u32[]{:S(2)}, u32[]{:S(2)}) %collective-permute-start.9) | collective-permute-done | bytes 73760 | tf_op jit(solution)/shard_map/ppermute | solution.py:467
  159.4 1.3 collective-permute-done.11.diagonal_ref
  161.3 1.6 second_norm.1
  162.9 0.9 copy-done.19
  163.8 3.9 %collective-permute-done.12.do_other_ref = bf16[128,128]{1,0:T(8,128)(2,1)S(1)} collective-permute-done((bf16[128,128]{1,0:T(8,128)(2,1)S(1)}, bf16[128,128]{1,0:T(8,128)(2,1)S(1)}, u32[]{:S(2)}, u32[]{:S(2)}) %collective-permute-start.12) | collective-permute-done | bytes 32800 | tf_op jit(solution)/shard_map/ppermute | solution.py:605
  167.7 7.0 %reverse.1 = (bf16[128,128]{1,0:T(8,128)(2,1)S(1)}, bf16[128,128]{1,0:T(8,128)(2,1)S(1)}, bf16[32,128,128]{2,1,0:T(8,128)(2,1)}) custom-call(s32[4]{0:T(128)S(1)} %copy-done.60, bf16[128,128]{1,0:T(8,128)(2,1)S(1)} %copy-done.38, bf16[128,128]{1,0:T(8,128)(2,1)S(1)} %copy-done.41, bf16[32,128,128]{2,1,0:T(8,128)(2,1)S(1)} %all-to-all-done.kv_ref, ...), custom_call_target="tpu_custom_call" | custom-call | tf_op jit(solution)/shard_map/reverse/pallas_call | solution.py:608
  174.7 5.7 %collective-permute-done.13 = bf16[3,1024,128]{2,1,0:T(8,128)(2,1)S(1)} collective-permute-done((bf16[3,1024,128]{2,1,0:T(8,128)(2,1)}, bf16[3,1024,128]{2,1,0:T(8,128)(2,1)S(1)}, u32[]{:S(2)}, u32[]{:S(2)}) %collective-permute-start.13) | collective-permute-done | bytes 786464 | tf_op jit(solution)/shard_map/ppermute | solution.py:590
  180.5 0.9 copy-done.69
  181.3 4.1 %all-to-all-start.3 = ((bf16[32,128,128]{2,1,0:T(8,128)(2,1)}), bf16[32,128,128]{2,1,0:T(8,128)(2,1)S(1)}, u32[]{:S(2)}, u32[]{:S(2)}) async-start(bf16[32,128,128]{2,1,0:T(8,128)(2,1)} %get-tuple-element.109), calls=%async_computation.3 | async-start | bytes 2097152 | tf_op jit(solution)/shard_map/all_to_all | solution.py:34
  185.4 1.8 collective-permute-start.14
  187.2 9.4 %collective-permute-done.14 = bf16[128,128]{1,0:T(8,128)(2,1)S(1)} collective-permute-done((bf16[128,128]{1,0:T(8,128)(2,1)S(1)}, bf16[128,128]{1,0:T(8,128)(2,1)S(1)}, u32[]{:S(2)}, u32[]{:S(2)}) %collective-permute-start.14) | collective-permute-done | bytes 32800 | tf_op jit(solution)/shard_map/ppermute | solution.py:626
  197.5 1.1 fusion.13.first_ref
  198.7 5.9 %all-to-all-done.3.back_ref = bf16[32,128,128]{2,1,0:T(8,128)(2,1)S(1)} async-done(((bf16[32,128,128]{2,1,0:T(8,128)(2,1)}), bf16[32,128,128]{2,1,0:T(8,128)(2,1)S(1)}, u32[]{:S(2)}, u32[]{:S(2)}) %all-to-all-start.3) | async-done | bytes 1048608 | tf_op jit(solution)/shard_map/all_to_all | solution.py:34
  204.5 0.9 copy-done.18
  205.5 1.1 copy-done.20
  206.6 1.3 late.1
  207.9 1.2 copy-done.10
  210.4 6.1 %all-to-all-start.4 = ((bf16[32,112,256]{2,1,0:T(8,128)(2,1)}), bf16[32,112,256]{2,1,0:T(8,128)(2,1)S(1)}, u32[]{:S(2)}, u32[]{:S(2)}) async-start(bf16[32,112,256]{2,1,0:T(8,128)(2,1)} %copy-done.10), calls=%async_computation.4 | async-start | bytes 3670016 | tf_op jit(solution)/shard_map/all_to_all | solution.py:34
  216.6 1.3 collective-permute-done.18
  218.8 20.4 %collective-permute-done.19 = bf16[64,1024]{1,0:T(8,128)(2,1)S(1)} collective-permute-done((bf16[64,1024]{1,0:T(8,128)(2,1)S(1)}, bf16[64,1024]{1,0:T(8,128)(2,1)S(1)}, u32[]{:S(2)}, u32[]{:S(2)}) %collective-permute-start.19) | collective-permute-done | bytes 131104 | tf_op jit(solution)/shard_map/ppermute | solution.py:461
  239.3 1.9 collective-permute-start.15
  241.6 3.3 %all-to-all-done.4.in_ref = bf16[32,112,256]{2,1,0:T(8,128)(2,1)S(1)} async-done(((bf16[32,112,256]{2,1,0:T(8,128)(2,1)}), bf16[32,112,256]{2,1,0:T(8,128)(2,1)S(1)}, u32[]{:S(2)}, u32[]{:S(2)}) %all-to-all-start.4) | async-done | bytes 1835040 | tf_op jit(solution)/shard_map/all_to_all | solution.py:34
  245.3 1.2 copy-done.11
  246.6 6.6 %all-to-all-start.5 = ((bf16[32,112,256]{2,1,0:T(8,128)(2,1)}), bf16[32,112,256]{2,1,0:T(8,128)(2,1)}, u32[]{:S(2)}, u32[]{:S(2)}) async-start(bf16[32,112,256]{2,1,0:T(8,128)(2,1)} %copy-done.11), calls=%async_computation.5 | async-start | bytes 3670016 | tf_op jit(solution)/shard_map/all_to_all | solution.py:34
  253.9 1.1 fusion.20
  255.3 0.9 broadcast_in_dim_reshape.3
  257.3 0.8 add_convert_fusion
  258.1 0.9 fusion.7
  259.6 21.6 %all-to-all-done.5 = bf16[32,112,256]{2,1,0:T(8,128)(2,1)} async-done(((bf16[32,112,256]{2,1,0:T(8,128)(2,1)}), bf16[32,112,256]{2,1,0:T(8,128)(2,1)}, u32[]{:S(2)}, u32[]{:S(2)}) %all-to-all-start.5) | async-done | bytes 1835040 | tf_op jit(solution)/shard_map/all_to_all | solution.py:34
  281.2 0.9 slice.52
  282.8 2.4 fusion.18
  285.3 1.1 copy.39
  286.4 1.9 convert_element_type.130
  289.0 2.1 fusion.19
  (202 shorter events, 24.9 us)
Async XLA Ops:
  2.0 8.3 %copy-start.30 = (f32[32,128]{1,0:T(8,128)}, f32[32,128]{1,0:T(8,128)S(1)}, u32[]{:S(2)}) copy-start(f32[32,128]{1,0:T(8,128)S(1)} %get-tuple-element.145.sin_t_ref.sin_ref) | copy-start | bytes 49156
  2.1 6.9 %copy-start.56 = (s32[4]{0:T(128)}, s32[4]{0:T(128)S(1)}, u32[]{:S(2)}) copy-start(s32[4]{0:T(128)S(1)} %pad_add_fusion.at_ref) | copy-start | bytes 52
  2.1 21.1 %copy-start.71 = (bf16[1,128,1024]{2,1,0:T(8,128)(2,1)S(1)}, bf16[1,128,1024]{2,1,0:T(8,128)(2,1)}, u32[]{:S(2)}) copy-start(bf16[1,128,1024]{2,1,0:T(8,128)(2,1)} %param.23) | copy-start | bytes 786436
  10.2 13.0 %copy-start.74 = (s32[128,8]{0,1:T(8,128)S(1)}, s32[128,8]{0,1:T(8,128)}, u32[]{:S(2)}) copy-start(s32[128,8]{0,1:T(8,128)} %param.24) | copy-start | bytes 12292
  10.3 13.8 %copy-start.72 = (bf16[1,1024,128]{2,1,0:T(8,128)(2,1)S(1)}, bf16[1,1024,128]{2,1,0:T(8,128)(2,1)}, u32[]{:S(2)}) copy-start(bf16[1,1024,128]{2,1,0:T(8,128)(2,1)} %param.22) | copy-start | bytes 786436
  10.3 30.4 %all-to-all-start = ((bf16[32,128,128]{2,1,0:T(8,128)(2,1)}), bf16[32,128,128]{2,1,0:T(8,128)(2,1)S(1)}, u32[]{:S(2)}, u32[]{:S(2)}) async-start(bf16[32,128,128]{2,1,0:T(8,128)(2,1)} %get-tuple-element.71), calls=%async_computation | async-start | bytes 2097152 | tf_op jit(solution)/shard_map/all_to_all | solution.py:34
  21.3 11.5 %collective-permute-start = (bf16[128,128]{1,0:T(8,128)(2,1)S(1)}, bf16[128,128]{1,0:T(8,128)(2,1)S(1)}, u32[]{:S(2)}, u32[]{:S(2)}) collective-permute-start(bf16[128,128]{1,0:T(8,128)(2,1)S(1)} %get-tuple-element.72), channel_id=1, source_target_pairs={{0,8},{4,12},{8,0},{12,4},{16,24},{20,28},{24,16},{28,20},{32,40},... | collective-permute-start | bytes 98312 | tf_op jit(solution)/shard_map/ppermute | solution.py:509
  23.1 30.8 %copy-start.2 = (bf16[256,1024]{1,0:T(8,128)(2,1)S(1)}, bf16[256,1024]{1,0:T(8,128)(2,1)}, u32[]{:S(2)}) copy-start(bf16[256,1024]{1,0:T(8,128)(2,1)} %w_out_ref.3) | copy-start | bytes 1572868
  24.1 41.9 %copy-start.1 = (bf16[128,1024]{1,0:T(8,128)(2,1)S(1)}, bf16[128,1024]{1,0:T(8,128)(2,1)}, u32[]{:S(2)}) copy-start(bf16[128,1024]{1,0:T(8,128)(2,1)} %tokens_ref.3) | copy-start | bytes 786436
  40.6 17.8 %collective-permute-start.5 = (bf16[3,1024,128]{2,1,0:T(8,128)(2,1)S(1)}, bf16[3,1024,128]{2,1,0:T(8,128)(2,1)S(1)}, u32[]{:S(2)}, u32[]{:S(2)}) collective-permute-start(bf16[3,1024,128]{2,1,0:T(8,128)(2,1)S(1)} %pad_maximum_fusion.w0_ref), channel_id=1, source_target_pairs={{0,2},{2,0},{1,3},{3,1},{4,6},{6,4},{5,7},{7,5},{8,10},{10,8},{9,1... | collective-permute-start | bytes 2359304 | tf_op jit(solution)/shard_map/ppermute | solution.py:467
  50.0 3.9 %collective-permute-start.1 = (bf16[128,128]{1,0:T(8,128)(2,1)S(1)}, bf16[128,128]{1,0:T(8,128)(2,1)S(1)}, u32[]{:S(2)}, u32[]{:S(2)}) collective-permute-start(bf16[128,128]{1,0:T(8,128)(2,1)S(1)} %get-tuple-element.76), channel_id=1, source_target_pairs={{0,8},{4,12},{8,0},{12,4},{16,24},{20,28},{24,16},{28,20},{32,40},... | collective-permute-start | bytes 98312 | tf_op jit(solution)/shard_map/ppermute | solution.py:536
  55.4 9.0 %copy-start.50 = (bf16[256,128]{1,0:T(8,128)(2,1)}, bf16[256,128]{1,0:T(8,128)(2,1)S(1)}, u32[]{:S(2)}) copy-start(bf16[256,128]{1,0:T(8,128)(2,1)S(1)} %get-tuple-element.102.context_ref) | copy-start | bytes 196612
  55.4 3.0 %collective-permute-start.2 = (bf16[64,1024]{1,0:T(8,128)(2,1)S(1)}, bf16[64,1024]{1,0:T(8,128)(2,1)S(1)}, u32[]{:S(2)}, u32[]{:S(2)}) collective-permute-start(bf16[64,1024]{1,0:T(8,128)(2,1)S(1)} %get-tuple-element.78), channel_id=1, source_target_pairs={{0,1},{1,0},{2,3},{3,2},{4,5},{5,4},{6,7},{7,6},{8,9},{9,8},{10,11... | collective-permute-start | bytes 393224 | tf_op jit(solution)/shard_map/ppermute | solution.py:459
  55.5 15.0 %collective-permute-start.6 = (bf16[3,1024,128]{2,1,0:T(8,128)(2,1)S(1)}, bf16[3,1024,128]{2,1,0:T(8,128)(2,1)}, u32[]{:S(2)}, u32[]{:S(2)}) collective-permute-start(bf16[3,1024,128]{2,1,0:T(8,128)(2,1)S(1)} %pad_maximum_fusion.w0_ref), channel_id=1, source_target_pairs={{0,1},{1,0},{2,3},{3,2},{4,5},{5,4},{6,7},{7,6},{8,9},{9,8},{10,11... | collective-permute-start | bytes 2359304 | tf_op jit(solution)/shard_map/ppermute | solution.py:468
  58.4 12.1 %collective-permute-start.7 = (bf16[3,1024,128]{2,1,0:T(8,128)(2,1)S(1)}, bf16[3,1024,128]{2,1,0:T(8,128)(2,1)}, u32[]{:S(2)}, u32[]{:S(2)}) collective-permute-start(bf16[3,1024,128]{2,1,0:T(8,128)(2,1)S(1)} %collective-permute-done.5.w1_ref), channel_id=1, source_target_pairs={{0,1},{1,0},{2,3},{3,2},{4,5},{5,4},{6,7},{7,6},{8,9},{9,8},{10,11... | collective-permute-start | bytes 2359304 | tf_op jit(solution)/shard_map/ppermute | solution.py:469
  58.5 6.0 %collective-permute-start.3 = (bf16[64,1024]{1,0:T(8,128)(2,1)S(1)}, bf16[64,1024]{1,0:T(8,128)(2,1)S(1)}, u32[]{:S(2)}, u32[]{:S(2)}) collective-permute-start(bf16[64,1024]{1,0:T(8,128)(2,1)S(1)} %add_convert_fusion.4), channel_id=1, source_target_pairs={{0,2},{2,0},{1,3},{3,1},{4,6},{6,4},{5,7},{7,5},{8,10},{10,8},{9,1... | collective-permute-start | bytes 393224 | tf_op jit(solution)/shard_map/ppermute | solution.py:461
  64.5 1.4 collective-permute-start.4
  65.4 40.7 %copy-start.21 = (bf16[128,256]{1,0:T(8,128)(2,1)}, bf16[128,256]{1,0:T(8,128)(2,1)S(1)}, u32[]{:S(2)}) copy-start(bf16[128,256]{1,0:T(8,128)(2,1)S(1)} %constant_dynamic-slice_fusion.cot_ref) | copy-start | bytes 196612
  70.5 35.6 %copy-start.4 = (f32[128,1024]{1,0:T(8,128)}, f32[128,1024]{1,0:T(8,128)S(1)}, u32[]{:S(2)}) copy-start(f32[128,1024]{1,0:T(8,128)S(1)} %get-tuple-element.80.middle_ref) | copy-start | bytes 1572868
  70.5 35.6 %copy-start.26 = (bf16[128,1024]{1,0:T(8,128)(2,1)}, bf16[128,1024]{1,0:T(8,128)(2,1)S(1)}, u32[]{:S(2)}) copy-start(bf16[128,1024]{1,0:T(8,128)(2,1)S(1)} %get-tuple-element.101.normed_ref) | copy-start | bytes 786436
  70.5 35.6 %copy-start.43 = (f32[32,128]{1,0:T(8,128)}, f32[32,128]{1,0:T(8,128)S(1)}, u32[]{:S(2)}) copy-start(f32[32,128]{1,0:T(8,128)S(1)} %get-tuple-element.94.gates_ref) | copy-start | bytes 49156
  115.8 4.7 %collective-permute-start.8 = (bf16[2,3,1024,128]{3,2,1,0:T(8,128)(2,1)}, bf16[2,3,1024,128]{3,2,1,0:T(8,128)(2,1)}, u32[]{:S(2)}, u32[]{:S(2)}) collective-permute-start(bf16[2,3,1024,128]{3,2,1,0:T(8,128)(2,1)} %get-tuple-element.92), channel_id=1, source_target_pairs={{0,1},{1,0},{2,3},{3,2},{4,5},{5,4},{6,7},{7,6},{8,9},{9,8},{10,11... | collective-permute-start | bytes 4718600 | tf_op jit(solution)/shard_map/ppermute | solution.py:576
  115.8 35.0 %all-to-all-start.2 = ((bf16[128,16,512]{2,1,0:T(8,128)(2,1)}), bf16[128,16,512]{2,1,0:T(8,128)(2,1)S(1)}, u32[]{:S(2)}, u32[]{:S(2)}) async-start(bf16[128,16,512]{2,1,0:T(8,128)(2,1)} %bitcast.63), calls=%async_computation.2 | async-start | bytes 4194304 | tf_op jit(solution)/shard_map/all_to_all | solution.py:34
  150.9 10.3 %copy-start.3 = (bf16[256,1024]{1,0:T(8,128)(2,1)S(1)}, bf16[256,1024]{1,0:T(8,128)(2,1)}, u32[]{:S(2)}) copy-start(bf16[256,1024]{1,0:T(8,128)(2,1)} %w_out_ref.3) | copy-start | bytes 1572868
  150.9 10.3 %copy-start.5 = (f32[128,1024]{1,0:T(8,128)S(1)}, f32[128,1024]{1,0:T(8,128)}, u32[]{:S(2)}) copy-start(f32[128,1024]{1,0:T(8,128)} %copy-done.4) | copy-start | bytes 1572868
  153.3 8.0 %copy-start.25 = (bf16[128,1024]{1,0:T(8,128)(2,1)S(1)}, bf16[128,1024]{1,0:T(8,128)(2,1)}, u32[]{:S(2)}) copy-start(bf16[128,1024]{1,0:T(8,128)(2,1)} %cot_ref.1) | copy-start | bytes 786436
  153.3 8.0 %copy-start.27 = (bf16[128,1024]{1,0:T(8,128)(2,1)S(1)}, bf16[128,1024]{1,0:T(8,128)(2,1)}, u32[]{:S(2)}) copy-start(bf16[128,1024]{1,0:T(8,128)(2,1)} %copy-done.26) | copy-start | bytes 786436
  153.3 8.0 %copy-start.29 = (bf16[1024,32]{0,1:T(8,128)(2,1)S(1)}, bf16[1024,32]{0,1:T(8,128)(2,1)}, u32[]{:S(2)}) copy-start(bf16[1024,32]{0,1:T(8,128)(2,1)} %param.20) | copy-start | bytes 196612
  153.3 8.0 %copy-start.45 = (f32[32,128]{1,0:T(8,128)S(1)}, f32[32,128]{1,0:T(8,128)}, u32[]{:S(2)}) copy-start(f32[32,128]{1,0:T(8,128)} %copy-done.43) | copy-start | bytes 49156
  153.3 8.0 %copy-start.51 = (bf16[256,128]{1,0:T(8,128)(2,1)S(1)}, bf16[256,128]{1,0:T(8,128)(2,1)}, u32[]{:S(2)}) copy-start(bf16[256,128]{1,0:T(8,128)(2,1)} %copy-done.50) | copy-start | bytes 196612
  153.3 8.0 %copy-start.60 = (s32[4]{0:T(128)S(1)}, s32[4]{0:T(128)}, u32[]{:S(2)}) copy-start(s32[4]{0:T(128)} %copy-done.56) | copy-start | bytes 52
  153.3 8.0 %copy-start.63 = (f32[1024]{0:T(1024)S(1)}, f32[1024]{0:T(1024)}, u32[]{:S(2)}) copy-start(f32[1024]{0:T(1024)} %param.19) | copy-start | bytes 12292
  153.3 14.4 %copy-start.31 = (f32[32,128]{1,0:T(8,128)S(1)}, f32[32,128]{1,0:T(8,128)}, u32[]{:S(2)}) copy-start(f32[32,128]{1,0:T(8,128)} %copy-done.30) | copy-start | bytes 49156
  153.3 14.4 %copy-start.33 = (f32[64,512]{1,0:T(8,128)S(1)}, f32[64,512]{1,0:T(8,128)}, u32[]{:S(2)}) copy-start(f32[64,512]{1,0:T(8,128)} %copy-done.32) | copy-start | bytes 393220
  153.3 14.4 %copy-start.38 = (bf16[128,128]{1,0:T(8,128)(2,1)S(1)}, bf16[128,128]{1,0:T(8,128)(2,1)}, u32[]{:S(2)}) copy-start(bf16[128,128]{1,0:T(8,128)(2,1)} %copy-done.36) | copy-start | bytes 98308
  153.3 14.3 %copy-start.41 = (bf16[128,128]{1,0:T(8,128)(2,1)S(1)}, bf16[128,128]{1,0:T(8,128)(2,1)}, u32[]{:S(2)}) copy-start(bf16[128,128]{1,0:T(8,128)(2,1)} %copy-done.39) | copy-start | bytes 98308
  153.3 14.3 %copy-start.48 = (f32[32,128]{1,0:T(8,128)S(1)}, f32[32,128]{1,0:T(8,128)}, u32[]{:S(2)}) copy-start(f32[32,128]{1,0:T(8,128)} %get-tuple-element.137.sin2_ref) | copy-start | bytes 49156
  153.4 14.3 %copy-start.49 = (f32[32,128]{1,0:T(8,128)S(1)}, f32[32,128]{1,0:T(8,128)}, u32[]{:S(2)}) copy-start(f32[32,128]{1,0:T(8,128)} %get-tuple-element.138.cos2_ref) | copy-start | bytes 49156
  153.4 14.3 %copy-start.65 = (f32[1,512]{1,0:T(1,128)S(1)}, f32[1,512]{1,0:T(1,128)}, u32[]{:S(2)}) copy-start(f32[1,512]{1,0:T(1,128)} %copy-done.64) | copy-start | bytes 6148
  155.0 4.4 %collective-permute-start.9 = (bf16[144,256]{1,0:T(8,128)(2,1)S(1)}, bf16[144,256]{1,0:T(8,128)(2,1)S(1)}, u32[]{:S(2)}, u32[]{:S(2)}) collective-permute-start(bf16[144,256]{1,0:T(8,128)(2,1)S(1)} %get-tuple-element.95.own_ref), channel_id=1, source_target_pairs={{0,2},{2,0},{1,3},{3,1},{4,6},{6,4},{5,7},{7,5},{8,10},{10,8},{9,1... | collective-permute-start | bytes 221192 | tf_op jit(solution)/shard_map/ppermute | solution.py:467
  155.6 3.8 %collective-permute-start.10 = (bf16[144,256]{1,0:T(8,128)(2,1)S(1)}, bf16[144,256]{1,0:T(8,128)(2,1)S(1)}, u32[]{:S(2)}, u32[]{:S(2)}) collective-permute-start(bf16[144,256]{1,0:T(8,128)(2,1)S(1)} %get-tuple-element.95.own_ref), channel_id=1, source_target_pairs={{0,1},{1,0},{2,3},{3,2},{4,5},{5,4},{6,7},{7,6},{8,9},{9,8},{10,11... | collective-permute-start | bytes 221192 | tf_op jit(solution)/shard_map/ppermute | solution.py:468
  159.4 1.3 collective-permute-start.11
  160.6 19.8 %collective-permute-start.13 = (bf16[3,1024,128]{2,1,0:T(8,128)(2,1)}, bf16[3,1024,128]{2,1,0:T(8,128)(2,1)S(1)}, u32[]{:S(2)}, u32[]{:S(2)}) collective-permute-start(bf16[3,1024,128]{2,1,0:T(8,128)(2,1)} %fusion.1), channel_id=1, source_target_pairs={{0,2},{2,0},{1,3},{3,1},{4,6},{6,4},{5,7},{7,5},{8,10},{10,8},{9,1... | collective-permute-start | bytes 2359304 | tf_op jit(solution)/shard_map/ppermute | solution.py:590
  163.8 16.7 %copy-start.23 = (f32[128,1024]{1,0:T(8,128)}, f32[128,1024]{1,0:T(8,128)S(1)}, u32[]{:S(2)}) copy-start(f32[128,1024]{1,0:T(8,128)S(1)} %get-tuple-element.120) | copy-start | bytes 1572868
  163.8 33.4 %copy-start.14 = (bf16[128,1024]{1,0:T(8,128)(2,1)S(1)}, bf16[128,1024]{1,0:T(8,128)(2,1)}, u32[]{:S(2)}) copy-start(bf16[128,1024]{1,0:T(8,128)(2,1)} %copy-done.13) | copy-start | bytes 786436
  163.8 3.9 %collective-permute-start.12 = (bf16[128,128]{1,0:T(8,128)(2,1)S(1)}, bf16[128,128]{1,0:T(8,128)(2,1)S(1)}, u32[]{:S(2)}, u32[]{:S(2)}) collective-permute-start(bf16[128,128]{1,0:T(8,128)(2,1)S(1)} %get-tuple-element.104), channel_id=1, source_target_pairs={{0,8},{4,12},{8,0},{12,4},{16,24},{20,28},{24,16},{28,20},{32,40},... | collective-permute-start | bytes 98312 | tf_op jit(solution)/shard_map/ppermute | solution.py:605
  167.7 29.8 %copy-start.9 = (bf16[1024,256]{1,0:T(8,128)(2,1)S(1)}, bf16[1024,256]{1,0:T(8,128)(2,1)}, u32[]{:S(2)}) copy-start(bf16[1024,256]{1,0:T(8,128)(2,1)} %wq_ref.1) | copy-start | bytes 1572868
  174.7 21.8 %copy-start.42 = (bf16[128,128]{1,0:T(8,128)(2,1)}, bf16[128,128]{1,0:T(8,128)(2,1)S(1)}, u32[]{:S(2)}) copy-start(bf16[128,128]{1,0:T(8,128)(2,1)S(1)} %get-tuple-element.111) | copy-start | bytes 98308
  181.3 23.2 %copy-start.16 = (bf16[1024,128]{1,0:T(8,128)(2,1)S(1)}, bf16[1024,128]{1,0:T(8,128)(2,1)}, u32[]{:S(2)}) copy-start(bf16[1024,128]{1,0:T(8,128)(2,1)} %wk_ref.3) | copy-start | bytes 786436
  181.3 23.2 %copy-start.61 = (s32[4]{0:T(128)S(1)}, s32[4]{0:T(128)}, u32[]{:S(2)}) copy-start(s32[4]{0:T(128)} %copy-done.56) | copy-start | bytes 52
  181.3 23.2 %all-to-all-start.3 = ((bf16[32,128,128]{2,1,0:T(8,128)(2,1)}), bf16[32,128,128]{2,1,0:T(8,128)(2,1)S(1)}, u32[]{:S(2)}, u32[]{:S(2)}) async-start(bf16[32,128,128]{2,1,0:T(8,128)(2,1)} %get-tuple-element.109), calls=%async_computation.3 | async-start | bytes 2097152 | tf_op jit(solution)/shard_map/all_to_all | solution.py:34
  185.4 11.2 %collective-permute-start.14 = (bf16[128,128]{1,0:T(8,128)(2,1)S(1)}, bf16[128,128]{1,0:T(8,128)(2,1)S(1)}, u32[]{:S(2)}, u32[]{:S(2)}) collective-permute-start(bf16[128,128]{1,0:T(8,128)(2,1)S(1)} %get-tuple-element.112), channel_id=1, source_target_pairs={{0,8},{4,12},{8,0},{12,4},{16,24},{20,28},{24,16},{28,20},{32,40},... | collective-permute-start | bytes 98312 | tf_op jit(solution)/shard_map/ppermute | solution.py:626
  210.4 7.5 %copy-start.35 = (bf16[64,1024]{1,0:T(8,128)(2,1)S(1)}, bf16[64,1024]{1,0:T(8,128)(2,1)}, u32[]{:S(2)}) copy-start(bf16[64,1024]{1,0:T(8,128)(2,1)} %copy-done.34) | copy-start | bytes 393220
  210.4 28.9 %copy-start.53 = (bf16[128,256]{1,0:T(8,128)(2,1)S(1)}, bf16[128,256]{1,0:T(8,128)(2,1)}, u32[]{:S(2)}) copy-start(bf16[128,256]{1,0:T(8,128)(2,1)} %copy-done.52) | copy-start | bytes 196612
  210.4 30.9 %copy-start.55 = (f32[1024]{0:T(1024)S(1)}, f32[1024]{0:T(1024)}, u32[]{:S(2)}) copy-start(f32[1024]{0:T(1024)} %param.14) | copy-start | bytes 12292
  210.4 34.5 %all-to-all-start.4 = ((bf16[32,112,256]{2,1,0:T(8,128)(2,1)}), bf16[32,112,256]{2,1,0:T(8,128)(2,1)S(1)}, u32[]{:S(2)}, u32[]{:S(2)}) async-start(bf16[32,112,256]{2,1,0:T(8,128)(2,1)} %copy-done.10), calls=%async_computation.4 | async-start | bytes 3670016 | tf_op jit(solution)/shard_map/all_to_all | solution.py:34
  216.5 1.4 collective-permute-start.18
  218.0 21.2 %collective-permute-start.19 = (bf16[64,1024]{1,0:T(8,128)(2,1)S(1)}, bf16[64,1024]{1,0:T(8,128)(2,1)S(1)}, u32[]{:S(2)}, u32[]{:S(2)}) collective-permute-start(bf16[64,1024]{1,0:T(8,128)(2,1)S(1)} %add_convert_fusion.2), channel_id=1, source_target_pairs={{0,2},{2,0},{1,3},{3,1},{4,6},{6,4},{5,7},{7,5},{8,10},{10,8},{9,1... | collective-permute-start | bytes 393224 | tf_op jit(solution)/shard_map/ppermute | solution.py:461
  239.2 2.1 collective-permute-start.20
  239.3 14.1 %collective-permute-start.15 = (bf16[128,256]{1,0:T(8,128)(2,1)S(1)}, bf16[128,256]{1,0:T(8,128)(2,1)S(1)}, u32[]{:S(2)}, u32[]{:S(2)}) collective-permute-start(bf16[128,256]{1,0:T(8,128)(2,1)S(1)} %copy-done.53), channel_id=1, source_target_pairs={{0,2},{2,0},{1,3},{3,1},{4,6},{6,4},{5,7},{7,5},{8,10},{10,8},{9,1... | collective-permute-start | bytes 196616 | tf_op jit(solution)/shard_map/ppermute | solution.py:467
  246.6 6.6 %copy-start.70 = (bf16[3,1024,128]{2,1,0:T(8,128)(2,1)S(1)}, bf16[3,1024,128]{2,1,0:T(8,128)(2,1)}, u32[]{:S(2)}) copy-start(bf16[3,1024,128]{2,1,0:T(8,128)(2,1)} %copy-done.69) | copy-start | bytes 2359300
  246.6 34.6 %all-to-all-start.5 = ((bf16[32,112,256]{2,1,0:T(8,128)(2,1)}), bf16[32,112,256]{2,1,0:T(8,128)(2,1)}, u32[]{:S(2)}, u32[]{:S(2)}) async-start(bf16[32,112,256]{2,1,0:T(8,128)(2,1)} %copy-done.11), calls=%async_computation.5 | async-start | bytes 3670016 | tf_op jit(solution)/shard_map/all_to_all | solution.py:34
  253.3 2.9 collective-permute-start.16
  253.5 2.8 collective-permute-start.17
  (37 other events, 44.3 us)

commit v2 on v1

--- a/solution.py
+++ b/solution.py
@@ -14,10 +14,6 @@
 CORE_SWAP = [(0, 1), (1, 0), (2, 3), (3, 2)]
 CHIP_SWAP = [(0, 2), (2, 0), (1, 3), (3, 1)]
 PARTNER = [(i, i ^ 2) for i in range(32)]
-VMEM = pl.BlockSpec(memory_space=pltpu.VMEM)
-SMEM = pl.BlockSpec(memory_space=pltpu.SMEM)
-
-
 def dot(a, b):
     return jnp.dot(a, b, preferred_element_type=f32)
 
@@ -38,17 +34,83 @@
     return jax.ShapeDtypeStruct(dims, dtype)
 
 
-def on_device(kernel, name, in_specs, outs, scratch=(), megabytes=16, flops=0):
-    return pl.pallas_call(
-        kernel,
-        out_shape=outs,
-        in_specs=in_specs,
-        out_specs=tuple(VMEM for _ in outs),
-        scratch_shapes=list(scratch),
-        cost_estimate=pl.CostEstimate(flops=flops, bytes_accessed=8_000_000, transcendentals=0) if flops else None,
-        compiler_params=pltpu.CompilerParams(vmem_limit_bytes=megabytes * 1024 * 1024),
-        name=name,
-    )
+def on_device(kernel, name, ins, outs, scratch=(), megabytes=16, us=1.0, lazy=False, aliases=None):
+    spaces = {"V": pltpu.VMEM, "F": pltpu.HBM, "Q": pltpu.HBM, "H": pltpu.HBM, "S": pltpu.HBM}
+    fetched = [n for n, kind in enumerate(ins) if kind in "FQ"]
+    staged = [n for n, (kind, _) in enumerate(outs) if kind == "S"]
+
+    def call(*operands):
+        def held(n):
+            dims = operands[n].shape
+            return pltpu.VMEM((dims[0], 256) if ins[n] == "Q" else dims, operands[n].dtype)
+
+        buffers = [held(n) for n in fetched]
+        stages = [pltpu.VMEM(outs[n][1].shape, outs[n][1].dtype) for n in staged]
+
+        def body(*refs):
+            refs = list(refs)
+            in_refs, refs = refs[: len(ins)], refs[len(ins) :]
+            out_refs, refs = refs[: len(outs)], refs[len(outs) :]
+            own, refs = refs[: len(scratch)], refs[len(scratch) :]
+            held_refs, refs = refs[: len(buffers)], refs[len(buffers) :]
+            stage_refs, sems = refs[: len(stages)], refs[len(stages)]
+            copies = []
+            for k, n in enumerate(fetched):
+                source = in_refs[n]
+                if ins[n] == "Q":
+                    quarter = lax.axis_index("wa").astype(jnp.int32) * 256
+                    source = source.at[:, pl.ds(pl.multiple_of(quarter, 256), 256)]
+                copies.append(pltpu.make_async_copy(source, held_refs[k], sems.at[k]))
+                in_refs[n] = held_refs[k]
+            for copy in copies:
+                copy.start()
+            pending = {}
+            for k, n in enumerate(staged):
+                pending[n] = pltpu.make_async_copy(stage_refs[k], out_refs[n], sems.at[len(buffers) + k])
+                out_refs[n] = stage_refs[k]
+            sent = set()
+
+            def send(n):
+                if n in pending:
+                    pending[n].start()
+                    sent.add(n)
+
+            if lazy:
+                kernel(*in_refs, *out_refs, *own, send=send, ready=lambda n: copies[fetched.index(n)].wait())
+            else:
+                for copy in copies:
+                    copy.wait()
+                kernel(*in_refs, *out_refs, *own, send=send)
+            for n in staged:
+                if n not in sent:
+                    send(n)
+            for n in staged:
+                pending[n].wait()
+
+        return pl.pallas_call(
+            body,
+            out_shape=tuple(o for _, o in outs),
+            in_specs=[pl.BlockSpec(memory_space=spaces[kind]) for kind in ins],
+            out_specs=tuple(pl.BlockSpec(memory_space=spaces[kind]) for kind, _ in outs),
+            scratch_shapes=[
+                *scratch,
+                *buffers,
+                *stages,
+                pltpu.SemaphoreType.DMA((max(1, len(buffers) + len(stages)),)),
+            ],
+            compiler_params=pltpu.CompilerParams(vmem_limit_bytes=megabytes * 1024 * 1024),
+            cost_estimate=pl.CostEstimate(flops=int(us * 1.1e9), bytes_accessed=0, transcendentals=0),
+            name=name,
+            input_output_aliases=aliases or {},
+        )(*operands)
+
+    return call
+
+
+def places():
+    ctx = lax.axis_index("ctx").astype(jnp.int32)
+    wa = lax.axis_index("wa").astype(jnp.int32)
+    return ctx, (ctx >> 1) & 1, wa, wa & 1
 
 
 def local_positions(first_row, row_count, device_rows, group_count):
@@ -88,15 +150,20 @@
 
 
 def prelude_kernel(
-    at_ref, tokens_ref, gain_ref, wq_ref, wk_ref, wv_ref, cos_ref, sin_ref, cos_t_ref, sin_t_ref,
-    kv_ref, normed_ref, q_ref, q_give_ref,
-):
-    side = at_ref[2]
+    tokens_ref, gain_ref, wq_ref, wk_ref, wv_ref, cos_ref, sin_ref, cos_t_ref, sin_t_ref,
+    kv_ref, normed_ref, q_ref, q_give_ref, *, send, ready
+):
+    _, side, _, _ = places()
+    ready(0)
+    ready(1)
     x = tokens_ref[...].astype(f32)
     root = lax.rsqrt(jnp.mean(x * x, -1, keepdims=True) + epsilon)
     normed = (x * root * gain_ref[...]).astype(bf16)
     normed_ref[...] = normed
+    send(1)
+    ready(3)
     k = dot(normed, wk_ref[...])
+    ready(4)
     v = dot(normed, wv_ref[...])
     low = lanes_of(k.shape) < 64
     heads = (
@@ -106,6 +173,8 @@
     heads = [turn_lanes(y, cos_ref[...], sin_ref[...]).astype(bf16) for y in heads]
     for d in range(32):
         kv_ref[d] = heads[(d >> 1) & 1]
+    send(0)
+    ready(2)
     qt = dot(normed, wq_ref[...]).T
     turned = [
         turn_rows(qt[64 * h : 64 * h + 64], cos_t_ref[...], sin_t_ref[...]).astype(bf16) * jnp.asarray(1.0 / HEAD_DIM, bf16)
@@ -156,11 +225,11 @@
 
 
 def attend_kernel(
-    at_ref, own_ref, other_ref, kv_ref,
-    mine_ref, give_ref, o_ref, lse_ref,
-    q_ref, m_ref, l_ref, acc_ref,
-):
-    c, side = at_ref[3], at_ref[2]
+    own_ref, other_ref, kv_ref,
+    mine_ref, give_ref, o_ref,
+    q_ref, m_ref, l_ref, acc_ref, *, send
+):
+    c, side, _, _ = places()
     to_columns(side, own_ref, other_ref, q_ref, 0)
     q_ref[64:128, :] = jnp.zeros((64, 512), bf16)
     m_ref[...] = jnp.full(m_ref.shape, -1e30, f32)
@@ -194,26 +263,27 @@
             step(base, late, second, masked_late)
 
     total = l_ref[...]
-    o_ref[...] = acc_ref[64:128, :] / total
-    lse_ref[...] = m_ref[...] + jnp.log(total)
+    o_ref[0:64, :] = acc_ref[64:128, :] / total
+    o_ref[64:72, :] = jnp.broadcast_to(m_ref[...] + jnp.log(total), (8, 512))
+    send(2)
     for g in range(2):
-        own, other = from_columns(side, o_ref[...], g)
+        own, other = from_columns(side, o_ref[0:64, :], g)
         mine_ref[64 * g : 64 * g + 64, :] = own.astype(bf16)
         give_ref[64 * g : 64 * g + 64, :] = other.astype(bf16)
 
 
 def reverse_kernel(
-    at_ref, own_ref, other_ref, kv_ref, do_own_ref, do_other_ref, o_ref, lse_ref,
+    own_ref, other_ref, kv_ref, do_own_ref, do_other_ref, o_ref,
     cos_ref, sin_ref, cos2_ref, sin2_ref,
     dq_ref, dq_give_ref, dkv_ref,
-    q_ref, do_ref, delta_ref, acc_ref,
-):
-    c, side = at_ref[3], at_ref[2]
+    q_ref, do_ref, delta_ref, acc_ref, *, send
+):
+    c, side, _, _ = places()
     to_columns(side, own_ref, other_ref, q_ref, 0)
     q_ref[64:128, :] = jnp.zeros((64, 512), bf16)
     to_columns(side, do_own_ref, do_other_ref, do_ref, 64)
     do_ref[0:64, :] = jnp.zeros((64, 512), bf16)
-    delta_ref[...] = jnp.sum(do_ref[64:128, :].astype(f32) * o_ref[...], 0, keepdims=True)
+    delta_ref[...] = jnp.sum(do_ref[64:128, :].astype(f32) * o_ref[0:64, :], 0, keepdims=True)
     acc_ref[...] = jnp.zeros(acc_ref.shape, f32)
 
     def step(base, keys_half, cols, mask, add):
@@ -223,7 +293,7 @@
         s = dot(kv, q)
         if mask is not None:
             s = mask(s, base, c)
-        p = jnp.exp(s - lse_ref[:, cols])
+        p = jnp.exp(s - o_ref[64:65, cols])
         dp = dot(kv, do)
         ds = (p * (dp - delta_ref[:, cols])).astype(bf16)
         acc_ref[:, cols] += dot_tn(kv, ds)
@@ -256,11 +326,13 @@
         dq_give_ref[here, :] = turn_rows(other, cos2_ref[...], -sin2_ref[...]).astype(bf16)
 
 
-def mix_kernel(at_ref, mine_ref, got_ref, w_out_ref, context_ref, keep_ref, give_ref):
-    core, side = at_ref[1], at_ref[2]
+def mix_kernel(mine_ref, got_ref, w_out_ref, context_ref, keep_ref, give_ref, *, send
+):
+    _, side, _, core = places()
     mine, got = mine_ref[...].astype(f32), got_ref[...].astype(f32)
     context_ref[0:128, :] = jnp.where(side == 0, mine, got).astype(bf16)
     context_ref[128:256, :] = jnp.where(side == 0, got, mine).astype(bf16)
+    send(0)
     mixed = dot_tn(context_ref[...], w_out_ref[...])
     top, bottom = mixed[0:64], mixed[64:128]
     keep_ref[...] = jnp.where(core == 0, top, bottom).astype(bf16)
@@ -273,10 +345,10 @@
 
 
 def route_kernel(
-    at_ref, tokens_ref, mine_ref, theirs_ref, gain_ref, router_ref, rank_ref, cot_ref,
-    middle_ref, normed_ref, gates_ref, out_ref,
-):
-    wa, core = at_ref[0], at_ref[1]
+    tokens_ref, mine_ref, theirs_ref, gain_ref, router_ref, rank_ref, cot_ref,
+    middle_ref, normed_ref, gates_ref, out_ref, *, send
+):
+    _, _, wa, core = places()
     for half in range(2):
         here = slice(64 * half, 64 * half + 64)
         mixed = jnp.where(core == half, mine_ref[...].astype(f32), theirs_ref[...].astype(f32))
@@ -284,11 +356,15 @@
         middle_ref[here, :] = middle
         root = lax.rsqrt(jnp.mean(middle * middle, -1, keepdims=True) + epsilon)
         normed_ref[here, :] = (middle * root * gain_ref[...]).astype(bf16)
+    send(0)
+    send(1)
     logits = dot_nt(router_ref[...], normed_ref[...])
     member = rank_ref[...] >= 0.0
     top = jnp.max(jnp.where(member, logits, -1e30), 0, keepdims=True)
     raised = jnp.where(member, jnp.exp(jnp.where(member, logits - top, 0.0)), 0.0)
-    gates_ref[...] = raised / jnp.sum(raised, 0, keepdims=True)
+    gates_ref[0:32, :] = raised / jnp.sum(raised, 0, keepdims=True)
+    gates_ref[32:64, :] = rank_ref[...]
+    send(2)
     quarter = normed_ref[:, pl.ds(pl.multiple_of(wa * 256, 256), 256)]
     for first in range(0, 32, 4):
         chosen = selection(rank_ref, first, 4)
@@ -306,16 +382,18 @@
 
 
 def expert_kernel(
-    in_ref, w0_ref, w1_ref, w2_ref, w3_ref,
-    out_ref, act_ref, dgate_ref, dup_ref,
-    gate_ref, up_ref, down_ref,
-):
+    in_ref, w0_ref, w1_ref, w2_ref, w3_ref, d0_ref, d1_ref, d2_ref, d3_ref,
+    out_ref, hidden_ref,
+    gate_ref, up_ref, down_ref, *, send
+):
+    downs = (d0_ref, d1_ref, d2_ref, d3_ref)
     for p, w in enumerate((w0_ref, w1_ref, w2_ref, w3_ref)):
         here = slice(128 * p, 128 * p + 128)
         gate_ref[:, here] = w[0]
         up_ref[:, here] = w[1]
         for n in range(8):
-            down_ref[here, 128 * n : 128 * n + 128] = w[2, 128 * n : 128 * n + 128, :]
+            down_ref[here, 128 * n : 128 * n + 128] = downs[p][128 * n : 128 * n + 128, :]
+    act_ref, dgate_ref, dup_ref = (hidden_ref.at[:, 512 * n : 512 * n + 512] for n in range(3))
     gate_pre = jnp.zeros((512, 512), f32)
     up_pre = jnp.zeros((512, 512), f32)
     d_act = jnp.zeros((512, 512), f32)
@@ -337,7 +415,8 @@
         out_ref[:, q, :, 256:512] = d_x.astype(bf16).reshape(32, 16, 256)
 
 
-def expert_grad_kernel(in_ref, act_ref, dgate_ref, dup_ref, near_ref, far_ref):
+def expert_grad_kernel(in_ref, hidden_ref, near_ref, far_ref, *, send):
+    act_ref, dgate_ref, dup_ref = (hidden_ref.at[:, 512 * n : 512 * n + 512] for n in range(3))
     for q in range(4):
         here = slice(256 * q, 256 * q + 256)
         x = in_ref[:, q, :, 0:256].reshape(512, 256)
@@ -354,7 +433,9 @@
                 to[p % 2, 2, at : at + 128, :] = g_down[128 * p : 128 * p + 128, 128 * n : 128 * n + 128]
 
 
-def combine_kernel(back_ref, rank_ref, gates_ref, cot_ref, sent_ref, moe_ref, dgates_ref):
+def combine_kernel(back_ref, gates_ref, cot_ref, sent_ref, dgates_ref, *, send
+):
+    rank_ref = gates_ref.at[32:64, :]
     d_normed = jnp.zeros((128, 256), f32)
     moe = jnp.zeros((128, 256), f32)
     for first in range(0, 32, 4):
@@ -375,27 +456,30 @@
             dgates_ref[first + n : first + n + 1, :] = jnp.sum(
                 placed[64 * n : 64 * n + 64], 0, keepdims=True
             )
-    moe_ref[...] = moe.astype(bf16)
+    sent_ref[144:272, :] = moe.astype(bf16)
     sent_ref[0:128, :] = d_normed.astype(bf16)
     sent_ref[128:144, 0:128] = dgates_ref[0:16, :].astype(bf16)
     sent_ref[128:144, 128:256] = dgates_ref[16:32, :].astype(bf16)
 
 
 def second_norm_kernel(
-    at_ref, own_ref, across_ref, beside_ref, diagonal_ref, gates_ref, middle_ref, normed_ref, cot_ref,
+    own_ref, across_ref, beside_ref, diagonal_ref, gates_ref, middle_ref, normed_ref, cot_ref,
     gain_ref, router_ref, w_out_ref, context_ref,
-    dmiddle_ref, dmine_ref, dgive_ref, parts_ref, dnormed_ref, extra_ref,
-):
-    wa, side = at_ref[0], at_ref[2]
+    dmiddle_ref, dmine_ref, dgive_ref, parts_ref, output_ref, dnormed_ref, extra_ref, *, send
+):
+    _, side, wa, _ = places()
     pieces = [(own_ref, 0), (across_ref, 2), (beside_ref, 1), (diagonal_ref, 3)]
     for ref, flip in pieces:
         at = pl.multiple_of((wa ^ flip) * 256, 256)
         dnormed_ref[:, pl.ds(at, 256)] = ref[0:128, :].astype(f32)
+        output_ref[:, pl.ds(at, 256)] = (
+            middle_ref[:, pl.ds(at, 256)] + ref[144:272, :].astype(f32)
+        ).astype(bf16)
     terms = [
         jnp.concatenate([ref[128:144, 0:128], ref[128:144, 128:256]], 0).astype(f32) for ref, _ in pieces
     ]
     d_gates = (terms[0] + terms[1]) + (terms[2] + terms[3])
-    gates = gates_ref[...]
+    gates = gates_ref[0:32, :]
     d_logits = (gates * (d_gates - jnp.sum(gates * d_gates, 0, keepdims=True))).astype(bf16)
     gain = gain_ref[...]
     d_normed = dnormed_ref[...] + dot_tn(d_logits, router_ref[...])
@@ -408,6 +492,7 @@
         scaled - unit * jnp.mean(scaled * unit, -1, keepdims=True)
     )
     dmiddle_ref[...] = d_middle
+    send(0)
     d_mixed = d_middle.astype(bf16)
     d_context = dot_nt(w_out_ref[...], d_mixed)
     dmine_ref[...] = jnp.where(side == 0, d_context[0:128], d_context[128:256]).astype(bf16)
@@ -425,12 +510,15 @@
 
 
 def late_kernel(
-    at_ref, back_ref, cos_ref, sin_ref, normed_ref, wk_ref, wv_ref, first_ref, query_ref, early_ref,
+    back_ref, cos_ref, sin_ref, normed_ref, wk_ref, wv_ref, first_ref, filled_ref,
     parts_ref, keep_ref, give_ref,
-):
-    core = at_ref[1]
-    parts_ref[:, 0:32, :] = query_ref[...]
-    parts_ref[:, 32:80, :] = early_ref[...]
+    kv_ref, sems, *, send, ready
+):
+    _, _, _, core = places()
+    move = pltpu.make_async_copy(kv_ref, parts_ref.at[:, 80:112, :], sems.at[0])
+    ready(0)
+    ready(1)
+    ready(2)
     heads = []
     for j in range(2):
         total = jnp.zeros((128, 128), f32)
@@ -441,18 +529,43 @@
     low = lanes_of((128, 128)) < 64
     d_k = jnp.where(low, heads[0], swap_halves(heads[1])).astype(bf16)
     d_v = jnp.where(low, swap_halves(heads[0]), heads[1]).astype(bf16)
-    parts_ref[:, 80:112, 0:128] = dot_tn(normed_ref[...], d_k).astype(bf16).reshape(32, 32, 128)
-    parts_ref[:, 80:112, 128:256] = dot_tn(normed_ref[...], d_v).astype(bf16).reshape(32, 32, 128)
+    ready(3)
+    kv_ref[:, :, 0:128] = dot_tn(normed_ref[...], d_k).astype(bf16).reshape(32, 32, 128)
+    kv_ref[:, :, 128:256] = dot_tn(normed_ref[...], d_v).astype(bf16).reshape(32, 32, 128)
+    move.start()
+    ready(4)
+    ready(5)
+    ready(6)
     first = first_ref[...] + dot_nt(d_k, wk_ref[...]) + dot_nt(d_v, wv_ref[...])
     keep_ref[...] = jnp.where(core == 0, first[0:64], first[64:128]).astype(bf16)
     give_ref[...] = jnp.where(core == 0, first[64:128], first[0:64]).astype(bf16)
-
-
-def share_kernel(in_ref, gain_ref, out_ref, gain2_ref, total_ref):
+    move.wait()
+
+
+def share_kernel(in_ref, gain_ref, out_ref, gain2_ref, total_ref, *, send):
     total_ref[...] = jnp.sum(in_ref[...].astype(f32), 0)
-    gain2_ref[...] = total_ref[68:72, :]
+    for q in range(4):
+        gain2_ref[:, 256 * q : 256 * q + 256] = total_ref[68 + q : 69 + q, :]
     total_ref[68:72, :] = gain_ref[...].astype(f32)
     out_ref[...] = jnp.broadcast_to(total_ref[...].astype(bf16)[None], (32, 112, 256))
+
+
+def final_kernel(in_ref, query_ref, key_ref, value_ref, out_ref, router_ref, gain_ref, extra_ref, *, send):
+    query_ref[...] = in_ref[:, 0:32, :].astype(f32).reshape(1024, 256)
+    send(0)
+    for q in range(4):
+        here = slice(256 * q, 256 * q + 256)
+        out_ref[:, here] = in_ref[8 * q : 8 * q + 8, 32:64, :].astype(f32).reshape(256, 256)
+    send(3)
+    key_ref[...] = in_ref[:, 80:112, 0:128].astype(f32).reshape(1024, 128)
+    send(1)
+    value_ref[...] = in_ref[:, 80:112, 128:256].astype(f32).reshape(1024, 128)
+    send(2)
+    extra_ref[...] = in_ref[:, 64:80, :].astype(f32)
+    for q in range(4):
+        router_ref[:, 256 * q : 256 * q + 256] = extra_ref[:, q, :]
+    for q in range(4):
+        gain_ref[:, 256 * q : 256 * q + 256] = jnp.sum(extra_ref[:, 4 + q, :], 0, keepdims=True)
 
 
 def sum_over_wa(keep, give):
@@ -487,7 +600,6 @@
     ctx = lax.axis_index("ctx").astype(jnp.int32)
     wa = lax.axis_index("wa").astype(jnp.int32)
     core, chip, side = wa % 2, wa // 2, (ctx >> 1) & 1
-    at = jnp.stack([wa, core, side, ctx])
     rows, width, experts = 128, 1024, 32
 
     angles = angles_of(ctx)
@@ -500,11 +612,17 @@
     kv_send, normed1, q_own, q_give = on_device(
         prelude_kernel,
         "prelude",
-        [SMEM] + [VMEM] * 9,
-        (shape((32, rows, 128)), shape((rows, width)), shape((rows, 128)), shape((rows, 128))),
-    )(
-        at, tokens, gain1, w_query, key_weight, value_weight, cos_lanes, sin_lanes, cos_rows, sin_rows
-    )
+        "FFFFFVVVV",
+        (
+            ("S", shape((32, rows, 128))),
+            ("S", shape((rows, width))),
+            ("S", shape((rows, 128))),
+            ("V", shape((rows, 128))),
+        ),
+        megabytes=56,
+        us=2,
+        lazy=True,
+    )(tokens, gain1, w_query, key_weight, value_weight, cos_lanes, sin_lanes, cos_rows, sin_rows)
     kv = exchange(kv_send, "ctx")
     q_other = lax.ppermute(q_give, "ctx", PARTNER)
 
@@ -513,143 +631,153 @@
     )
     lower = (jnp.arange(rows)[:, None] >= jnp.arange(rows)[None, :]).astype(bf16)
     rank = jnp.where(member, dot(lower, member.astype(bf16)) - 1.0, -1.0).T
-    cot_quarter = lax.dynamic_slice_in_dim(cotangent, wa * 256, 256, 1)
     router_t = w_router.T
     gain2 = norm2_gain.reshape(1, width)
+
+    cot_quarter = lax.dynamic_slice_in_dim(cotangent, wa * 256, 256, 1)
     down_lanes = w_down[0].reshape(128, 8, 128).transpose(1, 0, 2).reshape(width, 128)
-    weights = jnp.stack([w_gate[0], w_up[0], down_lanes])
-
-    kv, weights, rank, q_other = lax.optimization_barrier((kv, weights, rank, q_other))
+    weights = jnp.stack([w_gate[0], w_up[0]])
+    down_across = lax.ppermute(down_lanes, "wa", CHIP_SWAP)
+    kv, rank, q_other, weights, cot_quarter, down_across = lax.optimization_barrier(
+        (kv, rank, q_other, weights, cot_quarter, down_across)
+    )
     w_across, w_beside, w_diagonal = pieces_over_wa(weights)
-    ctx_mine, ctx_give, context_o, lse = on_device(
+    down_beside = lax.ppermute(down_lanes, "wa", CORE_SWAP)
+    down_diagonal = lax.ppermute(down_across, "wa", CORE_SWAP)
+    ctx_mine, ctx_give, context_o = on_device(
         attend_kernel,
         "attend",
-        [SMEM] + [VMEM] * 3,
-        (shape((rows, 128)), shape((rows, 128)), shape((64, 512), f32), shape((1, 512), f32)),
+        "VVV",
+        (("V", shape((rows, 128))), ("V", shape((rows, 128))), ("V", shape((72, 512), f32))),
         [
             pltpu.VMEM((128, 512), bf16),
             pltpu.VMEM((1, 512), f32),
             pltpu.VMEM((1, 512), f32),
             pltpu.VMEM((128, 512), f32),
         ],
-    )(at, q_own, q_other, kv)
+        us=0.5,
+    )(q_own, q_other, kv)
     ctx_got = lax.ppermute(ctx_give, "ctx", PARTNER)
     context_t, mix_keep, mix_give = on_device(
         mix_kernel,
         "mix",
-        [SMEM] + [VMEM] * 3,
-        (shape((256, rows)), shape((64, width)), shape((64, width))),
-    )(at, ctx_mine, ctx_got, w_out)
+        "VVV",
+        (("V", shape((256, rows))), ("V", shape((64, width))), ("V", shape((64, width)))),
+        us=0.8,
+    )(ctx_mine, ctx_got, w_out)
     mine, theirs = sum_over_wa(mix_keep, mix_give)
     middle, normed2, gates, outgoing = on_device(
         route_kernel,
         "route",
-        [SMEM] + [VMEM] * 7,
+        "VVVVVVV",
         (
-            shape((rows, width), f32),
-            shape((rows, width)),
-            shape((experts, rows), f32),
-            shape((2048, 512)),
+            ("V", shape((rows, width), f32)),
+            ("V", shape((rows, width))),
+            ("V", shape((2 * experts, rows), f32)),
+            ("V", shape((2048, 512))),
         ),
-    )(at, tokens, mine, theirs, gain2, router_t, rank, cot_quarter)
-
-    outgoing, w_across, w_beside, w_diagonal = lax.optimization_barrier(
-        (outgoing, w_across, w_beside, w_diagonal)
+        us=1.6,
+    )(tokens, mine, theirs, gain2, router_t, rank, cot_quarter)
+
+    outgoing, w_across, w_beside, w_diagonal, down_beside, down_diagonal = lax.optimization_barrier(
+        (outgoing, w_across, w_beside, w_diagonal, down_beside, down_diagonal)
     )
     arrived = exchange(outgoing.reshape(128, 16, 512), ("ctx", "wa")).reshape(32, 4, 16, 512)
-    returning, active, d_gate, d_up = on_device(
+    returning, hidden = on_device(
         expert_kernel,
         "experts",
-        [VMEM] * 5,
-        (shape((32, 4, 16, 512)), shape((512, 512)), shape((512, 512)), shape((512, 512))),
+        "VVVVVVVVV",
+        (("V", shape((32, 4, 16, 512))), ("V", shape((512, 1536)))),
         [pltpu.VMEM((width, 512), bf16), pltpu.VMEM((width, 512), bf16), pltpu.VMEM((512, width), bf16)],
         megabytes=24,
-    )(arrived, weights, w_across, w_beside, w_diagonal)
+        us=5,
+    )(
+        arrived, weights, w_across, w_beside, w_diagonal,
+        down_lanes, down_across, down_beside, down_diagonal,
+    )
     back = exchange(returning.reshape(128, 16, 512), ("ctx", "wa")).reshape(2048, 512)
     near, far = on_device(
         expert_grad_kernel,
         "expert_grads",
-        [VMEM] * 4,
-        (shape((2, 3, width, 128)), shape((2, 3, width, 128))),
-        flops=3_000_000_000,
-    )(arrived, active, d_gate, d_up)
+        "VV",
+        (("V", shape((2, 3, width, 128))), ("V", shape((2, 3, width, 128)))),
+        us=3,
+    )(arrived, hidden)
     far = lax.ppermute(far, "wa", CORE_SWAP)
-    near = near.astype(f32) + far.astype(f32)
-    near_own, near_give = near[0], near[1].astype(bf16)
+    near_sum = near.astype(f32) + far.astype(f32)
+    near_own, near_give = near_sum[0], near_sum[1].astype(bf16)
     back, near_own, near_give = lax.optimization_barrier((back, near_own, near_give))
-    sent, moe = on_device(
+    (sent,) = on_device(
         combine_kernel,
         "combine",
-        [VMEM] * 4,
-        (shape((144, 256)), shape((rows, 256))),
+        "VVV",
+        (("V", shape((272, 256))),),
         [pltpu.VMEM((32, 128), f32)],
-    )(back, rank, gates, cot_quarter)
+        us=1,
+    )(back, gates, cot_quarter)
 
     pieces = pieces_over_wa(sent)
-    pieces, moe, near_give = lax.optimization_barrier((pieces, moe, near_give))
-    near_got = lax.ppermute(near_give, "wa", CHIP_SWAP)
-    d_middle, do_own, do_give, parts = on_device(
+    pieces, near_two = lax.optimization_barrier((pieces, near_give[:2]))
+    near_got = lax.ppermute(near_two, "wa", CHIP_SWAP)
+    d_middle, do_own, do_give, parts, output = on_device(
         second_norm_kernel,
         "second_norm",
-        [SMEM] + [VMEM] * 12,
+        "VVVVVVVVVVVV",
         (
-            shape((rows, width), f32),
-            shape((rows, 128)),
-            shape((rows, 128)),
-            shape((32, 48, 256)),
+            ("V", shape((rows, width), f32)),
+            ("V", shape((rows, 128))),
+            ("V", shape((rows, 128))),
+            ("V", shape((32, 48, 256))),
+            ("V", shape((rows, width))),
         ),
         [pltpu.VMEM((rows, width), f32), pltpu.VMEM((32, 16, 256), f32)],
-    )(
-        at, sent, *pieces, gates, middle, normed2, cotangent, gain2, router_t, w_out, context_t
-    )
+        us=1.6,
+    )(sent, *pieces, gates, middle, normed2, cotangent, gain2, router_t, w_out, context_t)
     do_other = lax.ppermute(do_give, "ctx", PARTNER)
 
     angles2 = angles_of(ctx ^ 2)
     dq_own, dq_give, dkv = on_device(
         reverse_kernel,
         "reverse",
-        [SMEM] + [VMEM] * 11,
-        (shape((rows, 128)), shape((rows, 128)), shape((32, rows, 128))),
+        "VVVVVVVVVV",
+        (("V", shape((rows, 128))), ("V", shape((rows, 128))), ("V", shape((32, rows, 128)))),
         [
             pltpu.VMEM((128, 512), bf16),
             pltpu.VMEM((128, 512), bf16),
             pltpu.VMEM((1, 512), f32),
             pltpu.VMEM((128, 512), f32),
         ],
+        us=1,
     )(
-        at, q_own, q_other, kv, do_own, do_other, context_o, lse,
+        q_own, q_other, kv, do_own, do_other, context_o,
         cos_rows, sin_rows, jnp.cos(angles2).T, jnp.sin(angles2).T,
     )
-    dkv, near_got = lax.optimization_barrier((dkv, near_got))
+    dkv, near_got, near_last = lax.optimization_barrier((dkv, near_got, near_give[2]))
     kv_back = exchange(dkv, "ctx")
+    near_last = lax.ppermute(near_last, "wa", CHIP_SWAP)
 
     dq_got = lax.ppermute(dq_give, "ctx", PARTNER)
+    dq_got, near_last = lax.optimization_barrier((dq_got, near_last))
     d_query = jnp.where(
         side == 0, jnp.concatenate([dq_own, dq_got], 0), jnp.concatenate([dq_got, dq_own], 0)
     ).T
     parts_query = dot_tn(normed1, d_query).astype(bf16).reshape(32, 32, 256)
     first_query = dot_nt(d_query, w_query)
-    kv_back, parts_query, first_query = lax.optimization_barrier((kv_back, parts_query, first_query))
-
+    filled = jnp.concatenate([parts_query, parts, jnp.zeros((32, 32, 256), bf16)], 1)
+    kv_back, filled, first_query = lax.optimization_barrier((kv_back, filled, first_query))
     parts_all, first_keep, first_give = on_device(
         late_kernel,
         "late",
-        [SMEM] + [VMEM] * 9,
-        (shape((32, 112, 256)), shape((64, width)), shape((64, width))),
-    )(
-        at, kv_back, cos_lanes, sin_lanes, normed1, key_weight, value_weight, first_query,
-        parts_query, parts,
-    )
-    parts_all, moe = lax.optimization_barrier((parts_all, moe))
+        "FFFFFFFH",
+        (("H", shape((32, 112, 256))), ("V", shape((64, width))), ("V", shape((64, width)))),
+        [pltpu.VMEM((32, 32, 256), bf16), pltpu.SemaphoreType.DMA((1,))],
+        megabytes=56,
+        us=1.3,
+        lazy=True,
+        aliases={7: 0},
+    )(kv_back, cos_lanes, sin_lanes, normed1, key_weight, value_weight, first_query, filled)
     summed = exchange(parts_all, "ctx")
-    moe_all = jnp.stack((moe,) + pieces_over_wa(moe))
-    moe_all = moe_all.reshape(2, 2, rows, 256)
-    moe_all = jnp.where(core == 0, moe_all, moe_all[::-1])
-    moe_all = jnp.where(chip == 0, moe_all, moe_all[:, ::-1])
-    moe_sum = moe_all.transpose(2, 1, 0, 3).reshape(rows, width).astype(f32)
-    output = (middle + moe_sum).astype(bf16)
-    near_all = near_own + near_got.astype(f32)
-    g_down = near_all[2].reshape(8, 128, 128).transpose(1, 0, 2).reshape(128, width)
+
     first_mine, first_theirs = sum_over_wa(first_keep, first_give)
     d_first = jnp.where(
         core == 0, jnp.stack([first_mine, first_theirs]), jnp.stack([first_theirs, first_mine])
@@ -659,35 +787,56 @@
     unit_first = widened * root_first
     scaled_first = d_first * norm1_gain
     grad_gain_first = jnp.sum(d_first * unit_first, 0).astype(bf16).reshape(4, 256)
+    shared, out_gain2 = on_device(
+        share_kernel,
+        "share",
+        "VV",
+        (("V", shape((32, 112, 256))), ("V", shape((1, width), f32))),
+        [pltpu.VMEM((112, 256), f32)],
+        us=0.5,
+    )(summed, grad_gain_first)
+    shared, d_first = lax.optimization_barrier((shared, d_first))
+    spread_out = exchange(shared, "ctx")
+
     grad_tokens = (
         d_middle
         + root_first
         * (scaled_first - unit_first * jnp.mean(scaled_first * unit_first, -1, keepdims=True))
     ).astype(bf16)
-    shared, out_gain2 = on_device(
-        share_kernel,
-        "share",
-        [VMEM] * 2,
-        (shape((32, 112, 256)), shape((4, 256), f32)),
-        [pltpu.VMEM((112, 256), f32)],
-    )(summed, grad_gain_first)
-    spread_out = exchange(shared, "ctx").astype(f32)
-
-    out_query = spread_out[:, 0:32].reshape(width, 256)
-    out_out = spread_out[:, 32:64].reshape(4, 256, 256).transpose(1, 0, 2).reshape(256, width)
-    out_router = spread_out[:, 64:68].reshape(experts, width).T
+    g_gate = near_own[0] + near_got[0].astype(f32)
+    g_up = near_own[1] + near_got[1].astype(f32)
+    g_down = (near_own[2] + near_last.astype(f32)).reshape(8, 128, 128)
+    g_down = g_down.transpose(1, 0, 2).reshape(128, width)
+    spread_out, output, grad_tokens, g_gate, g_up, g_down = lax.optimization_barrier(
+        (spread_out, output, grad_tokens, g_gate, g_up, g_down)
+    )
+    out_query, out_key, out_value, out_out, out_router, out_gain1 = on_device(
+        final_kernel,
+        "final",
+        "V",
+        (
+            ("S", shape((width, 256), f32)),
+            ("S", shape((width, 128), f32)),
+            ("S", shape((width, 128), f32)),
+            ("S", shape((256, width), f32)),
+            ("S", shape((experts, width), f32)),
+            ("S", shape((1, width), f32)),
+        ),
+        [pltpu.VMEM((32, 16, 256), f32)],
+        us=1.8,
+    )(spread_out)
     return (
         output,
         grad_tokens,
-        jnp.sum(spread_out[:, 68:72], 0).reshape(width),
+        out_gain1.reshape(width),
         out_query,
-        spread_out[:, 80:112, :128].reshape(width, 128),
-        spread_out[:, 80:112, 128:].reshape(width, 128),
+        out_key,
+        out_value,
         out_out,
         out_gain2.reshape(width),
-        out_router,
-        near_all[0][None],
-        near_all[1][None],
+        out_router.T,
+        g_gate[None],
+        g_up[None],
         g_down[None],
     )
 

time: 293 us -> 273 us (0.932)
  local copies, waits for them, and re-layouts: 41 us -> 10.8 us
  Pallas kernels: 29.7 us -> 34.7 us
  waiting for transfers between devices: 129 us -> 124 us
  blocking collectives: 35.6 us -> 40.1 us
  starting transfers between devices: 43.1 us -> 46.7 us
    unnamed x154 -> x73, local copies, waits for them, and re-layouts: 28 us -> 5.77 us
    all_to_all x5, waiting for transfers between devices: 63.9 us -> 57.2 us  [exchange(): return lax.all_to_all(value, axes, split_axis=0, concat_axis=0, tiled=True)]
    slice x4 -> x1, local copies, waits for them, and re-layouts: 6.55 us -> 0.03 us  [local(): pieces, near_two = lax.optimization_barrier((pieces, near_give[:2]))]
    pallas_call x11 -> x12, Pallas kernels: 29.7 us -> 34.7 us  [call(): pl.pallas_call(body, out_shape=tuple((o for _, o in outs)), in_specs=[pl....]
    all_to_all x1, blocking collectives: 35.6 us -> 40.1 us  [exchange(): return lax.all_to_all(value, axes, split_axis=0, concat_axis=0, tiled=True)]
    ppermute x3 -> x2, waiting for transfers between devices: 6.17 us -> 10.6 us  [pieces_over_wa(): across = lax.ppermute(part, 'wa', CHIP_SWAP)]
    ppermute x2, waiting for transfers between devices: 25.7 us -> 21.6 us  [sum_over_wa(): other = lax.ppermute(pair, 'wa', CHIP_SWAP)]
    all_to_all x5, starting transfers between devices: 32.3 us -> 36 us  [exchange(): return lax.all_to_all(value, axes, split_axis=0, concat_axis=0, tiled=True)]
  transfers between devices with their start and end apart: 26 -> 27, of which waited for: 17 -> 20; matrix products, arithmetic and copies ran while one was open for 5% -> 6% of each run, Pallas kernels for 6% -> 4%
where the time goes in v2:
time: 273 us; the launch traced here: 272 us
  waiting for transfers between devices  124 us (45%)
  starting transfers between devices  46.7 us (17%)
  blocking collectives  40.1 us (15%)
  Pallas kernels  34.7 us (13%)
  other arithmetic  12.1 us (4%)
  local copies, waits for them, and re-layouts  10.8 us (4%)
    all_to_all x5, waiting for transfers between devices, exchange(): return lax.all_to_all(value, axes, split_axis=0, concat_axis=0, tiled=True)  57.2 us
    all_to_all x1, blocking collectives, exchange(): return lax.all_to_all(value, axes, split_axis=0, concat_axis=0, tiled=True)  40.1 us
    all_to_all x5, starting transfers between devices, exchange(): return lax.all_to_all(value, axes, split_axis=0, concat_axis=0, tiled=True)  36 us
    pallas_call x12, Pallas kernels, call(): pl.pallas_call(body, out_shape=tuple((o for _, o in outs)), in_specs=[pl....  34.7 us
    ppermute x2, waiting for transfers between devices, sum_over_wa(): other = lax.ppermute(pair, 'wa', CHIP_SWAP)  21.6 us
    ppermute x2, waiting for transfers between devices, pieces_over_wa(): across = lax.ppermute(part, 'wa', CHIP_SWAP)  10.6 us
    ppermute x1, waiting for transfers between devices, local(): dq_got = lax.ppermute(dq_give, 'ctx', PARTNER)  8.96 us
    ppermute x1, waiting for transfers between devices, local(): q_other = lax.ppermute(q_give, 'ctx', PARTNER)  6.78 us
  transfers between devices with their start and end apart: 27, of which 20 were waited for; matrix products, arithmetic and copies ran while one was open for 6% of the time, Pallas kernels for 4%

profile of v2, /device:TPU:0, one launch (start us, length us, event | category | flops | bytes accessed | tf_op | source)
XLA Modules:
  0.0 272.2 jit_solution(3204812154922414892)
XLA Ops:
  1.2 0.8 multiply_sine_fusion.1
  2.0 0.8 maximum_maximum_fusion.1
  2.8 4.4 %prelude.1 = (bf16[32,128,128]{2,1,0:T(8,128)(2,1)}, bf16[128,1024]{1,0:T(8,128)(2,1)}, bf16[128,128]{1,0:T(8,128)(2,1)}, bf16[128,128]{1,0:T(8,128)(2,1)}) custom-call(bf16[128,1024]{1,0:T(8,128)(2,1)} %refs_0_.3, f32[1,1024]{1,0:T(1,128)} %bitcast.72, bf16[1024,256]{1,0:T(8,128)(2,1)} %refs_2_.2, bf16[1024,128]{1,0:T(8,128)(2,1)} %refs_4_.3, ...), custom_call_target="tpu_custom_call" | custom-call | flops 2200000000 | tf_op jit(solution)/shard_map/prelude/pallas_call | solution.py:90
  7.2 11.0 %all-to-all-start = ((bf16[32,128,128]{2,1,0:T(8,128)(2,1)}), bf16[32,128,128]{2,1,0:T(8,128)(2,1)S(1)}, u32[]{:S(2)}, u32[]{:S(2)}) async-start(bf16[32,128,128]{2,1,0:T(8,128)(2,1)} %get-tuple-element.84), calls=%async_computation | async-start | bytes 2097152 | tf_op jit(solution)/shard_map/all_to_all | solution.py:30
  18.3 1.9 collective-permute-start
  20.3 0.7 collective-permute-start.1
  21.1 1.0 pad_maximum_fusion.refs_1_
  22.1 0.9 constant_dynamic-slice_fusion.refs_6_.refs_2_
  23.0 6.8 %collective-permute-done.refs_1_ = bf16[128,128]{1,0:T(8,128)(2,1)S(1)} collective-permute-done((bf16[128,128]{1,0:T(8,128)(2,1)S(1)}, bf16[128,128]{1,0:T(8,128)(2,1)S(1)}, u32[]{:S(2)}, u32[]{:S(2)}) %collective-permute-start) | collective-permute-done | bytes 32800 | tf_op jit(solution)/shard_map/ppermute | solution.py:627
  29.7 6.3 %collective-permute-done.1.refs_6_ = bf16[1024,128]{1,0:T(8,128)(2,1)S(1)} collective-permute-done((bf16[1024,128]{1,0:T(8,128)(2,1)S(1)}, bf16[1024,128]{1,0:T(8,128)(2,1)S(1)}, u32[]{:S(2)}, u32[]{:S(2)}) %collective-permute-start.1) | collective-permute-done | bytes 262176 | tf_op jit(solution)/shard_map/ppermute | solution.py:640
  36.1 3.0 %all-to-all-done.refs_2_ = bf16[32,128,128]{2,1,0:T(8,128)(2,1)S(1)} async-done(((bf16[32,128,128]{2,1,0:T(8,128)(2,1)}), bf16[32,128,128]{2,1,0:T(8,128)(2,1)S(1)}, u32[]{:S(2)}, u32[]{:S(2)}) %all-to-all-start) | async-done | bytes 1048608 | tf_op jit(solution)/shard_map/all_to_all | solution.py:30
  39.1 4.8 %attend.1 = (bf16[128,128]{1,0:T(8,128)(2,1)S(1)}, bf16[128,128]{1,0:T(8,128)(2,1)S(1)}, f32[72,512]{1,0:T(8,128)S(1)}) custom-call(bf16[128,128]{1,0:T(8,128)(2,1)S(1)} %copy-done.15, bf16[128,128]{1,0:T(8,128)(2,1)S(1)} %collective-permute-done.refs_1_, bf16[32,128,128]{2,1,0:T(8,128)(2,1)S(1)} %all-to-all-done.refs_2_), custom_call_target="tpu_custom_call" | custom-call | flops 550000000 | tf_op jit(solution)/shard_map/attend/pallas_call | solution.py:90
  43.9 0.7 copy-done.13
  45.7 2.8 %collective-permute-done.2.refs_1_ = bf16[128,128]{1,0:T(8,128)(2,1)S(1)} collective-permute-done((bf16[128,128]{1,0:T(8,128)(2,1)S(1)}, bf16[128,128]{1,0:T(8,128)(2,1)S(1)}, u32[]{:S(2)}, u32[]{:S(2)}) %collective-permute-start.2) | collective-permute-done | bytes 32800 | tf_op jit(solution)/shard_map/ppermute | solution.py:660
  48.9 1.3 collective-permute-done.3
  50.3 0.7 collective-permute-start.4
  51.0 6.0 %collective-permute-done.6.refs_2_ = bf16[2,1024,128]{2,1,0:T(8,128)(2,1)S(1)} collective-permute-done((bf16[2,1024,128]{2,1,0:T(8,128)(2,1)S(1)}, bf16[2,1024,128]{2,1,0:T(8,128)(2,1)S(1)}, u32[]{:S(2)}, u32[]{:S(2)}) %collective-permute-start.6) | collective-permute-done | bytes 524320 | tf_op jit(solution)/shard_map/ppermute | solution.py:580
  57.0 1.4 collective-permute-done.4
  59.1 0.7 collective-permute-done.5.refs_2_
  59.8 1.1 route.1
  61.1 40.1 %all_to_all.30 = bf16[128,16,512]{2,1,0:T(8,128)(2,1)S(1)} all-to-all(bf16[128,16,512]{2,1,0:T(8,128)(2,1)S(1)} %bitcast.53), channel_id=1, replica_groups=mesh['ctx'=32,'wa'=4] {'ctx','wa'}, dimensions={0} | all-to-all | bytes 4194304 | tf_op jit(solution)/shard_map/all_to_all | solution.py:30
  101.2 5.5 %experts.1 = (bf16[32,4,16,512]{3,2,1,0:T(8,128)(2,1)}, bf16[512,1536]{1,0:T(8,128)(2,1)S(1)}) custom-call(bf16[32,4,16,512]{3,2,1,0:T(8,128)(2,1)S(1)} %bitcast.54, bf16[2,1024,128]{2,1,0:T(8,128)(2,1)S(1)} %pad_maximum_fusion.refs_1_, bf16[2,1024,128]{2,1,0:T(8,128)(2,1)S(1)} %collective-permute-done.6.refs_2_, ...), custom_call_target="tpu_custom_call" | custom-call | flops 5500000256 | tf_op jit(solution)/shard_map/experts/pallas_call | solution.py:90
  106.7 3.0 %expert_grads.1 = (bf16[2,3,1024,128]{3,2,1,0:T(8,128)(2,1)S(1)}, bf16[2,3,1024,128]{3,2,1,0:T(8,128)(2,1)}) custom-call(bf16[32,4,16,512]{3,2,1,0:T(8,128)(2,1)S(1)} %bitcast.55, bf16[512,1536]{1,0:T(8,128)(2,1)S(1)} %get-tuple-element.104.refs_1_), custom_call_target="tpu_custom_call" | custom-call | flops 3300000000 | tf_op jit(solution)/shard_map/expert_grads/pallas_call | solution.py:90
  109.7 1.1 copy-done.2
  110.8 4.6 %all-to-all-start.2 = ((bf16[128,16,512]{2,1,0:T(8,128)(2,1)}), bf16[128,16,512]{2,1,0:T(8,128)(2,1)S(1)}, u32[]{:S(2)}, u32[]{:S(2)}) async-start(bf16[128,16,512]{2,1,0:T(8,128)(2,1)} %bitcast.9), calls=%async_computation.2 | async-start | bytes 4194304 | tf_op jit(solution)/shard_map/all_to_all | solution.py:30
  115.5 2.2 convert_add_fusion
  117.7 1.0 fusion.1
  118.7 1.3 slice_bitcast_fusion
  120.0 25.9 %all-to-all-done.2 = bf16[128,16,512]{2,1,0:T(8,128)(2,1)S(1)} async-done(((bf16[128,16,512]{2,1,0:T(8,128)(2,1)}), bf16[128,16,512]{2,1,0:T(8,128)(2,1)S(1)}, u32[]{:S(2)}, u32[]{:S(2)}) %all-to-all-start.2) | async-done | bytes 2097184 | tf_op jit(solution)/shard_map/all_to_all | solution.py:30
  145.9 0.8 copy-done.22
  146.7 1.1 combine.1.refs_0_
  147.8 0.7 collective-permute-start.12
  148.5 4.6 %collective-permute-done.12.refs_1_ = bf16[272,256]{1,0:T(8,128)(2,1)S(1)} collective-permute-done((bf16[272,256]{1,0:T(8,128)(2,1)S(1)}, bf16[272,256]{1,0:T(8,128)(2,1)S(1)}, u32[]{:S(2)}, u32[]{:S(2)}) %collective-permute-start.12) | collective-permute-done | bytes 139296 | tf_op jit(solution)/shard_map/ppermute | solution.py:580
  153.1 1.3 collective-permute-done.14.refs_3_
  155.0 1.8 second_norm.1
  156.8 0.8 copy-done.3
  157.5 0.7 slice_bitcast_fusion.1
  158.3 3.2 %collective-permute-done.15.refs_4_ = bf16[128,128]{1,0:T(8,128)(2,1)S(1)} collective-permute-done((bf16[128,128]{1,0:T(8,128)(2,1)S(1)}, bf16[128,128]{1,0:T(8,128)(2,1)S(1)}, u32[]{:S(2)}, u32[]{:S(2)}) %collective-permute-start.15) | collective-permute-done | bytes 32800 | tf_op jit(solution)/shard_map/ppermute | solution.py:736
  161.5 6.5 %reverse.1 = (bf16[128,128]{1,0:T(8,128)(2,1)S(1)}, bf16[128,128]{1,0:T(8,128)(2,1)S(1)}, bf16[32,128,128]{2,1,0:T(8,128)(2,1)}) custom-call(bf16[128,128]{1,0:T(8,128)(2,1)S(1)} %copy-done.16, bf16[128,128]{1,0:T(8,128)(2,1)S(1)} %collective-permute-done.refs_1_, bf16[32,128,128]{2,1,0:T(8,128)(2,1)S(1)} %all-to-all-done.refs_2_, ...), custom_call_target="tpu_custom_call" | custom-call | flops 1100000000 | tf_op jit(solution)/shard_map/reverse/pallas_call | solution.py:90
  168.4 1.2 collective-permute-start.18
  169.6 3.9 %all-to-all-start.3 = ((bf16[32,128,128]{2,1,0:T(8,128)(2,1)}), bf16[32,128,128]{2,1,0:T(8,128)(2,1)S(1)}, u32[]{:S(2)}, u32[]{:S(2)}) async-start(bf16[32,128,128]{2,1,0:T(8,128)(2,1)} %get-tuple-element.121), calls=%async_computation.3 | async-start | bytes 2097152 | tf_op jit(solution)/shard_map/all_to_all | solution.py:30
  173.5 1.8 collective-permute-start.17
  175.4 9.0 %collective-permute-done.17 = bf16[128,128]{1,0:T(8,128)(2,1)S(1)} collective-permute-done((bf16[128,128]{1,0:T(8,128)(2,1)S(1)}, bf16[128,128]{1,0:T(8,128)(2,1)S(1)}, u32[]{:S(2)}, u32[]{:S(2)}) %collective-permute-start.17) | collective-permute-done | bytes 32800 | tf_op jit(solution)/shard_map/ppermute | solution.py:759
  184.4 1.3 convolution_convert_fusion
  185.7 1.1 fusion.14.refs_6_
  186.8 1.9 maximum_maximum_fusion.refs_7_
  188.7 3.4 %all-to-all-done.3.refs_0_ = bf16[32,128,128]{2,1,0:T(8,128)(2,1)S(1)} async-done(((bf16[32,128,128]{2,1,0:T(8,128)(2,1)}), bf16[32,128,128]{2,1,0:T(8,128)(2,1)S(1)}, u32[]{:S(2)}, u32[]{:S(2)}) %all-to-all-start.3) | async-done | bytes 1048608 | tf_op jit(solution)/shard_map/all_to_all | solution.py:30
  192.1 1.0 copy-done.27
  193.0 3.5 %late.1 = (bf16[32,112,256]{2,1,0:T(8,128)(2,1)}, bf16[64,1024]{1,0:T(8,128)(2,1)}, bf16[64,1024]{1,0:T(8,128)(2,1)}) custom-call(bf16[32,128,128]{2,1,0:T(8,128)(2,1)} %copy-done.27, f32[128,128]{1,0:T(8,128)} %get-tuple-element.167.refs_5_.refs_1_, f32[128,128]{1,0:T(8,128)} %get-tuple-element.168.refs_6_.refs_2_, ...), custom_call_target="tpu_custom_call", output_to_operand_aliasing={{0}: (7, {})} | custom-call | flops 1430000000 | tf_op jit(solution)/shard_map/late/pallas_call | solution.py:90
  196.5 8.2 %all-to-all-start.4 = ((bf16[32,112,256]{2,1,0:T(8,128)(2,1)}), bf16[32,112,256]{2,1,0:T(8,128)(2,1)S(1)}, u32[]{:S(2)}, u32[]{:S(2)}) async-start(bf16[32,112,256]{2,1,0:T(8,128)(2,1)} %get-tuple-element.131), calls=%async_computation.4 | async-start | bytes 3670016 | tf_op jit(solution)/shard_map/all_to_all | solution.py:30
  204.9 1.3 collective-permute-done.19
  206.3 1.2 collective-permute-start.20
  207.6 20.2 %collective-permute-done.20 = bf16[64,1024]{1,0:T(8,128)(2,1)S(1)} collective-permute-done((bf16[64,1024]{1,0:T(8,128)(2,1)S(1)}, bf16[64,1024]{1,0:T(8,128)(2,1)S(1)}, u32[]{:S(2)}, u32[]{:S(2)}) %collective-permute-start.20) | collective-permute-done | bytes 131104 | tf_op jit(solution)/shard_map/ppermute | solution.py:574
  227.9 1.3 collective-permute-done.21
  229.6 2.1 all-to-all-done.4.refs_0_
  231.7 1.0 share.1
  232.7 1.3 copy-done.1
  233.9 8.2 %all-to-all-start.5 = ((bf16[32,112,256]{2,1,0:T(8,128)(2,1)}), bf16[32,112,256]{2,1,0:T(8,128)(2,1)S(1)}, u32[]{:S(2)}, u32[]{:S(2)}) async-start(bf16[32,112,256]{2,1,0:T(8,128)(2,1)} %copy-done.1), calls=%async_computation.5 | async-start | bytes 3670016 | tf_op jit(solution)/shard_map/all_to_all | solution.py:30
  242.1 2.3 add_bitcast_fusion
  244.4 1.2 bitcast_add_fusion
  245.6 0.8 copy.37
  246.4 0.9 fusion.10
  247.4 22.8 %all-to-all-done.5.refs_0_ = bf16[32,112,256]{2,1,0:T(8,128)(2,1)S(1)} async-done(((bf16[32,112,256]{2,1,0:T(8,128)(2,1)}), bf16[32,112,256]{2,1,0:T(8,128)(2,1)S(1)}, u32[]{:S(2)}, u32[]{:S(2)}) %all-to-all-start.5) | async-done | bytes 1835040 | tf_op jit(solution)/shard_map/all_to_all | solution.py:30
  270.2 1.8 final.1
  (115 shorter events, 5.0 us)
Async XLA Ops:
  7.2 11.1 %copy-start.35 = (bf16[128,128]{1,0:T(8,128)(2,1)S(1)}, bf16[128,128]{1,0:T(8,128)(2,1)}, u32[]{:S(2)}) copy-start(bf16[128,128]{1,0:T(8,128)(2,1)} %get-tuple-element.85) | copy-start | bytes 98308
  7.2 13.0 %copy-start.29 = (bf16[1,128,1024]{2,1,0:T(8,128)(2,1)S(1)}, bf16[1,128,1024]{2,1,0:T(8,128)(2,1)}, u32[]{:S(2)}) copy-start(bf16[1,128,1024]{2,1,0:T(8,128)(2,1)} %param.23) | copy-start | bytes 786436
  7.2 13.7 %copy-start.33 = (s32[128,8]{0,1:T(8,128)S(1)}, s32[128,8]{0,1:T(8,128)}, u32[]{:S(2)}) copy-start(s32[128,8]{0,1:T(8,128)} %param.24) | copy-start | bytes 12292
  7.2 13.9 %copy-start.30 = (bf16[1,1024,128]{2,1,0:T(8,128)(2,1)S(1)}, bf16[1,1024,128]{2,1,0:T(8,128)(2,1)}, u32[]{:S(2)}) copy-start(bf16[1,1024,128]{2,1,0:T(8,128)(2,1)} %param.22) | copy-start | bytes 786436
  7.2 31.9 %copy-start.15 = (bf16[128,128]{1,0:T(8,128)(2,1)S(1)}, bf16[128,128]{1,0:T(8,128)(2,1)}, u32[]{:S(2)}) copy-start(bf16[128,128]{1,0:T(8,128)(2,1)} %get-tuple-element.83.refs_0_) | copy-start | bytes 98308
  7.2 31.8 %all-to-all-start = ((bf16[32,128,128]{2,1,0:T(8,128)(2,1)}), bf16[32,128,128]{2,1,0:T(8,128)(2,1)S(1)}, u32[]{:S(2)}, u32[]{:S(2)}) async-start(bf16[32,128,128]{2,1,0:T(8,128)(2,1)} %get-tuple-element.84), calls=%async_computation | async-start | bytes 2097152 | tf_op jit(solution)/shard_map/all_to_all | solution.py:30
  18.3 11.5 %collective-permute-start = (bf16[128,128]{1,0:T(8,128)(2,1)S(1)}, bf16[128,128]{1,0:T(8,128)(2,1)S(1)}, u32[]{:S(2)}, u32[]{:S(2)}) collective-permute-start(bf16[128,128]{1,0:T(8,128)(2,1)S(1)} %copy-done.35), channel_id=1, source_target_pairs={{0,8},{4,12},{8,0},{12,4},{16,24},{20,28},{24,16},{28,20},{32,40},... | collective-permute-start | bytes 98312 | tf_op jit(solution)/shard_map/ppermute | solution.py:627
  20.2 28.3 %copy-start.8 = (bf16[256,1024]{1,0:T(8,128)(2,1)S(1)}, bf16[256,1024]{1,0:T(8,128)(2,1)}, u32[]{:S(2)}) copy-start(bf16[256,1024]{1,0:T(8,128)(2,1)} %refs_10_.1) | copy-start | bytes 1572868
  20.3 15.8 %collective-permute-start.1 = (bf16[1024,128]{1,0:T(8,128)(2,1)S(1)}, bf16[1024,128]{1,0:T(8,128)(2,1)S(1)}, u32[]{:S(2)}, u32[]{:S(2)}) collective-permute-start(bf16[1024,128]{1,0:T(8,128)(2,1)S(1)} %bitcast.56), channel_id=1, source_target_pairs={{0,2},{2,0},{1,3},{3,1},{4,6},{6,4},{5,7},{7,5},{8,10},{10,8},{9,1... | collective-permute-start | bytes 786440 | tf_op jit(solution)/shard_map/ppermute | solution.py:640
  43.9 0.7 copy-start.13
  44.6 3.9 %collective-permute-start.2 = (bf16[128,128]{1,0:T(8,128)(2,1)S(1)}, bf16[128,128]{1,0:T(8,128)(2,1)S(1)}, u32[]{:S(2)}, u32[]{:S(2)}) collective-permute-start(bf16[128,128]{1,0:T(8,128)(2,1)S(1)} %get-tuple-element.89), channel_id=1, source_target_pairs={{0,8},{4,12},{8,0},{12,4},{16,24},{20,28},{24,16},{28,20},{32,40},... | collective-permute-start | bytes 98312 | tf_op jit(solution)/shard_map/ppermute | solution.py:660
  45.1 11.8 %collective-permute-start.6 = (bf16[2,1024,128]{2,1,0:T(8,128)(2,1)S(1)}, bf16[2,1024,128]{2,1,0:T(8,128)(2,1)S(1)}, u32[]{:S(2)}, u32[]{:S(2)}) collective-permute-start(bf16[2,1024,128]{2,1,0:T(8,128)(2,1)S(1)} %pad_maximum_fusion.refs_1_), channel_id=1, source_target_pairs={{0,2},{2,0},{1,3},{3,1},{4,6},{6,4},{5,7},{7,5},{8,10},{10,8},{9,1... | collective-permute-start | bytes 1572872 | tf_op jit(solution)/shard_map/ppermute | solution.py:580
  48.5 11.4 %copy-start = (bf16[128,1024]{1,0:T(8,128)(2,1)S(1)}, bf16[128,1024]{1,0:T(8,128)(2,1)}, u32[]{:S(2)}) copy-start(bf16[128,1024]{1,0:T(8,128)(2,1)} %refs_0_.3) | copy-start | bytes 786436
  48.5 11.4 %copy-start.10 = (bf16[1024,32]{0,1:T(8,128)(2,1)S(1)}, bf16[1024,32]{0,1:T(8,128)(2,1)}, u32[]{:S(2)}) copy-start(bf16[1024,32]{0,1:T(8,128)(2,1)} %param.20) | copy-start | bytes 196612
  48.5 11.4 %copy-start.12 = (f32[1024]{0:T(1024)S(1)}, f32[1024]{0:T(1024)}, u32[]{:S(2)}) copy-start(f32[1024]{0:T(1024)} %param.19) | copy-start | bytes 12292
  48.8 12.2 %copy-start.24 = (bf16[256,128]{1,0:T(8,128)(2,1)}, bf16[256,128]{1,0:T(8,128)(2,1)S(1)}, u32[]{:S(2)}) copy-start(bf16[256,128]{1,0:T(8,128)(2,1)S(1)} %get-tuple-element.115.refs_11_) | copy-start | bytes 196612
  48.8 1.4 collective-permute-start.3
  50.3 8.1 %collective-permute-start.4 = (bf16[64,1024]{1,0:T(8,128)(2,1)S(1)}, bf16[64,1024]{1,0:T(8,128)(2,1)S(1)}, u32[]{:S(2)}, u32[]{:S(2)}) collective-permute-start(bf16[64,1024]{1,0:T(8,128)(2,1)S(1)} %add_convert_fusion.3), channel_id=1, source_target_pairs={{0,2},{2,0},{1,3},{3,1},{4,6},{6,4},{5,7},{7,5},{8,10},{10,8},{9,1... | collective-permute-start | bytes 393224 | tf_op jit(solution)/shard_map/ppermute | solution.py:574
  51.0 10.1 %collective-permute-start.7 = (bf16[2,1024,128]{2,1,0:T(8,128)(2,1)S(1)}, bf16[2,1024,128]{2,1,0:T(8,128)(2,1)S(1)}, u32[]{:S(2)}, u32[]{:S(2)}) collective-permute-start(bf16[2,1024,128]{2,1,0:T(8,128)(2,1)S(1)} %pad_maximum_fusion.refs_1_), channel_id=1, source_target_pairs={{0,1},{1,0},{2,3},{3,2},{4,5},{5,4},{6,7},{7,6},{8,9},{9,8},{10,11... | collective-permute-start | bytes 1572872 | tf_op jit(solution)/shard_map/ppermute | solution.py:581
  57.0 4.1 %collective-permute-start.8 = (bf16[2,1024,128]{2,1,0:T(8,128)(2,1)S(1)}, bf16[2,1024,128]{2,1,0:T(8,128)(2,1)S(1)}, u32[]{:S(2)}, u32[]{:S(2)}) collective-permute-start(bf16[2,1024,128]{2,1,0:T(8,128)(2,1)S(1)} %collective-permute-done.6.refs_2_), channel_id=1, source_target_pairs={{0,1},{1,0},{2,3},{3,2},{4,5},{5,4},{6,7},{7,6},{8,9},{9,8},{10,11... | collective-permute-start | bytes 1572872 | tf_op jit(solution)/shard_map/ppermute | solution.py:582
  58.4 1.4 collective-permute-start.5
  58.5 2.5 collective-permute-start.9
  59.0 2.0 collective-permute-start.10
  61.0 40.2 %copy-start.17 = (f32[128,1024]{1,0:T(8,128)}, f32[128,1024]{1,0:T(8,128)S(1)}, u32[]{:S(2)}) copy-start(f32[128,1024]{1,0:T(8,128)S(1)} %get-tuple-element.113.refs_5_) | copy-start | bytes 1572868
  61.0 40.2 %copy-start.19 = (bf16[128,1024]{1,0:T(8,128)(2,1)}, bf16[128,1024]{1,0:T(8,128)(2,1)S(1)}, u32[]{:S(2)}) copy-start(bf16[128,1024]{1,0:T(8,128)(2,1)S(1)} %get-tuple-element.114.refs_6_) | copy-start | bytes 786436
  61.0 40.1 %copy-start.21 = (f32[64,128]{1,0:T(8,128)}, f32[64,128]{1,0:T(8,128)S(1)}, u32[]{:S(2)}) copy-start(f32[64,128]{1,0:T(8,128)S(1)} %get-tuple-element.108.refs_1_.refs_4_) | copy-start | bytes 98308
  109.7 1.1 copy-start.2
  110.8 4.7 %collective-permute-start.11 = (bf16[2,3,1024,128]{3,2,1,0:T(8,128)(2,1)}, bf16[2,3,1024,128]{3,2,1,0:T(8,128)(2,1)}, u32[]{:S(2)}, u32[]{:S(2)}) collective-permute-start(bf16[2,3,1024,128]{3,2,1,0:T(8,128)(2,1)} %get-tuple-element.106), channel_id=1, source_target_pairs={{0,1},{1,0},{2,3},{3,2},{4,5},{5,4},{6,7},{7,6},{8,9},{9,8},{10,11... | collective-permute-start | bytes 4718600 | tf_op jit(solution)/shard_map/ppermute | solution.py:706
  110.8 35.0 %all-to-all-start.2 = ((bf16[128,16,512]{2,1,0:T(8,128)(2,1)}), bf16[128,16,512]{2,1,0:T(8,128)(2,1)S(1)}, u32[]{:S(2)}, u32[]{:S(2)}) async-start(bf16[128,16,512]{2,1,0:T(8,128)(2,1)} %bitcast.9), calls=%async_computation.2 | async-start | bytes 4194304 | tf_op jit(solution)/shard_map/all_to_all | solution.py:30
  145.9 0.8 copy-start.22
  146.7 6.4 %copy-start.26 = (bf16[3,1024,128]{2,1,0:T(8,128)(2,1)S(1)}, bf16[3,1024,128]{2,1,0:T(8,128)(2,1)}, u32[]{:S(2)}) copy-start(bf16[3,1024,128]{2,1,0:T(8,128)(2,1)} %fusion.1) | copy-start | bytes 2359300
  146.7 8.2 %copy-start.5 = (bf16[128,1024]{1,0:T(8,128)(2,1)S(1)}, bf16[128,1024]{1,0:T(8,128)(2,1)}, u32[]{:S(2)}) copy-start(bf16[128,1024]{1,0:T(8,128)(2,1)} %refs_7_.1) | copy-start | bytes 786436
  146.7 8.2 %copy-start.9 = (bf16[256,1024]{1,0:T(8,128)(2,1)S(1)}, bf16[256,1024]{1,0:T(8,128)(2,1)}, u32[]{:S(2)}) copy-start(bf16[256,1024]{1,0:T(8,128)(2,1)} %refs_10_.1) | copy-start | bytes 1572868
  146.7 8.2 %copy-start.11 = (bf16[1024,32]{0,1:T(8,128)(2,1)S(1)}, bf16[1024,32]{0,1:T(8,128)(2,1)}, u32[]{:S(2)}) copy-start(bf16[1024,32]{0,1:T(8,128)(2,1)} %param.20) | copy-start | bytes 196612
  146.7 8.2 %copy-start.18 = (f32[128,1024]{1,0:T(8,128)S(1)}, f32[128,1024]{1,0:T(8,128)}, u32[]{:S(2)}) copy-start(f32[128,1024]{1,0:T(8,128)} %copy-done.17) | copy-start | bytes 1572868
  146.7 8.2 %copy-start.20 = (bf16[128,1024]{1,0:T(8,128)(2,1)S(1)}, bf16[128,1024]{1,0:T(8,128)(2,1)}, u32[]{:S(2)}) copy-start(bf16[128,1024]{1,0:T(8,128)(2,1)} %copy-done.19) | copy-start | bytes 786436
  146.7 8.2 %copy-start.23 = (f32[64,128]{1,0:T(8,128)S(1)}, f32[64,128]{1,0:T(8,128)}, u32[]{:S(2)}) copy-start(f32[64,128]{1,0:T(8,128)} %copy-done.21) | copy-start | bytes 98308
  146.7 8.2 %copy-start.25 = (bf16[256,128]{1,0:T(8,128)(2,1)S(1)}, bf16[256,128]{1,0:T(8,128)(2,1)}, u32[]{:S(2)}) copy-start(bf16[256,128]{1,0:T(8,128)(2,1)} %copy-done.24) | copy-start | bytes 196612
  147.8 5.2 %collective-permute-start.12 = (bf16[272,256]{1,0:T(8,128)(2,1)S(1)}, bf16[272,256]{1,0:T(8,128)(2,1)S(1)}, u32[]{:S(2)}, u32[]{:S(2)}) collective-permute-start(bf16[272,256]{1,0:T(8,128)(2,1)S(1)} %combine.1.refs_0_), channel_id=1, source_target_pairs={{0,2},{2,0},{1,3},{3,1},{4,6},{6,4},{5,7},{7,5},{8,10},{10,8},{9,1... | collective-permute-start | bytes 417800 | tf_op jit(solution)/shard_map/ppermute | solution.py:580
  148.5 4.6 %collective-permute-start.13 = (bf16[272,256]{1,0:T(8,128)(2,1)S(1)}, bf16[272,256]{1,0:T(8,128)(2,1)S(1)}, u32[]{:S(2)}, u32[]{:S(2)}) collective-permute-start(bf16[272,256]{1,0:T(8,128)(2,1)S(1)} %combine.1.refs_0_), channel_id=1, source_target_pairs={{0,1},{1,0},{2,3},{3,2},{4,5},{5,4},{6,7},{7,6},{8,9},{9,8},{10,11... | collective-permute-start | bytes 417800 | tf_op jit(solution)/shard_map/ppermute | solution.py:581
  153.0 1.4 collective-permute-start.14
  154.4 14.0 %collective-permute-start.16 = (bf16[2,1024,128]{2,1,0:T(8,128)(2,1)S(1)}, bf16[2,1024,128]{2,1,0:T(8,128)(2,1)S(1)}, u32[]{:S(2)}, u32[]{:S(2)}) collective-permute-start(bf16[2,1024,128]{2,1,0:T(8,128)(2,1)S(1)} %slice.30), channel_id=1, source_target_pairs={{0,2},{2,0},{1,3},{3,1},{4,6},{6,4},{5,7},{7,5},{8,10},{10,8},{9,1... | collective-permute-start | bytes 1572872 | tf_op jit(solution)/shard_map/ppermute | solution.py:721
  154.9 6.5 %copy-start.6 = (f32[32,128]{1,0:T(8,128)S(1)}, f32[32,128]{1,0:T(8,128)}, u32[]{:S(2)}) copy-start(f32[32,128]{1,0:T(8,128)} %get-tuple-element.165.refs_7_.refs_6_) | copy-start | bytes 49156
  154.9 6.5 %copy-start.7 = (f32[32,128]{1,0:T(8,128)S(1)}, f32[32,128]{1,0:T(8,128)}, u32[]{:S(2)}) copy-start(f32[32,128]{1,0:T(8,128)} %get-tuple-element.166.refs_8_.refs_7_) | copy-start | bytes 49156
  154.9 6.5 %copy-start.14 = (f32[72,512]{1,0:T(8,128)S(1)}, f32[72,512]{1,0:T(8,128)}, u32[]{:S(2)}) copy-start(f32[72,512]{1,0:T(8,128)} %copy-done.13) | copy-start | bytes 442372
  154.9 6.5 %copy-start.16 = (bf16[128,128]{1,0:T(8,128)(2,1)S(1)}, bf16[128,128]{1,0:T(8,128)(2,1)}, u32[]{:S(2)}) copy-start(bf16[128,128]{1,0:T(8,128)(2,1)} %get-tuple-element.83.refs_0_) | copy-start | bytes 98308
  156.7 0.8 copy-start.3
  157.5 3.9 %collective-permute-start.15 = (bf16[128,128]{1,0:T(8,128)(2,1)S(1)}, bf16[128,128]{1,0:T(8,128)(2,1)S(1)}, u32[]{:S(2)}, u32[]{:S(2)}) collective-permute-start(bf16[128,128]{1,0:T(8,128)(2,1)S(1)} %get-tuple-element.117), channel_id=1, source_target_pairs={{0,8},{4,12},{8,0},{12,4},{16,24},{20,28},{24,16},{28,20},{32,40},... | collective-permute-start | bytes 98312 | tf_op jit(solution)/shard_map/ppermute | solution.py:736
  167.9 17.7 %copy-start.28 = (bf16[1024,256]{1,0:T(8,128)(2,1)S(1)}, bf16[1024,256]{1,0:T(8,128)(2,1)}, u32[]{:S(2)}) copy-start(bf16[1024,256]{1,0:T(8,128)(2,1)} %refs_2_.2) | copy-start | bytes 1572868
  168.4 16.0 %collective-permute-start.18 = (bf16[1024,128]{1,0:T(8,128)(2,1)}, bf16[1024,128]{1,0:T(8,128)(2,1)}, u32[]{:S(2)}, u32[]{:S(2)}) collective-permute-start(bf16[1024,128]{1,0:T(8,128)(2,1)} %slice_bitcast_fusion.1), channel_id=1, source_target_pairs={{0,2},{2,0},{1,3},{3,1},{4,6},{6,4},{5,7},{7,5},{8,10},{10,8},{9,1... | collective-permute-start | bytes 786440 | tf_op jit(solution)/shard_map/ppermute | solution.py:757
  169.6 22.5 %all-to-all-start.3 = ((bf16[32,128,128]{2,1,0:T(8,128)(2,1)}), bf16[32,128,128]{2,1,0:T(8,128)(2,1)S(1)}, u32[]{:S(2)}, u32[]{:S(2)}) async-start(bf16[32,128,128]{2,1,0:T(8,128)(2,1)} %get-tuple-element.121), calls=%async_computation.3 | async-start | bytes 2097152 | tf_op jit(solution)/shard_map/all_to_all | solution.py:30
  173.5 10.9 %collective-permute-start.17 = (bf16[128,128]{1,0:T(8,128)(2,1)S(1)}, bf16[128,128]{1,0:T(8,128)(2,1)S(1)}, u32[]{:S(2)}, u32[]{:S(2)}) collective-permute-start(bf16[128,128]{1,0:T(8,128)(2,1)S(1)} %get-tuple-element.124), channel_id=1, source_target_pairs={{0,8},{4,12},{8,0},{12,4},{16,24},{20,28},{24,16},{28,20},{32,40},... | collective-permute-start | bytes 98312 | tf_op jit(solution)/shard_map/ppermute | solution.py:759
  192.1 1.0 copy-start.27
  196.5 8.3 %copy-start.34 = (bf16[64,1024]{1,0:T(8,128)(2,1)S(1)}, bf16[64,1024]{1,0:T(8,128)(2,1)}, u32[]{:S(2)}) copy-start(bf16[64,1024]{1,0:T(8,128)(2,1)} %get-tuple-element.133) | copy-start | bytes 393220
  196.5 9.7 %copy-start.31 = (bf16[64,1024]{1,0:T(8,128)(2,1)S(1)}, bf16[64,1024]{1,0:T(8,128)(2,1)}, u32[]{:S(2)}) copy-start(bf16[64,1024]{1,0:T(8,128)(2,1)} %get-tuple-element.132) | copy-start | bytes 393220
  196.5 32.8 %copy-start.32 = (f32[1024]{0:T(1024)S(1)}, f32[1024]{0:T(1024)}, u32[]{:S(2)}) copy-start(f32[1024]{0:T(1024)} %param.14) | copy-start | bytes 12292
  196.5 35.2 %all-to-all-start.4 = ((bf16[32,112,256]{2,1,0:T(8,128)(2,1)}), bf16[32,112,256]{2,1,0:T(8,128)(2,1)S(1)}, u32[]{:S(2)}, u32[]{:S(2)}) async-start(bf16[32,112,256]{2,1,0:T(8,128)(2,1)} %get-tuple-element.131), calls=%async_computation.4 | async-start | bytes 3670016 | tf_op jit(solution)/shard_map/all_to_all | solution.py:30
  204.8 1.4 collective-permute-start.19
  206.3 21.5 %collective-permute-start.20 = (bf16[64,1024]{1,0:T(8,128)(2,1)S(1)}, bf16[64,1024]{1,0:T(8,128)(2,1)S(1)}, u32[]{:S(2)}, u32[]{:S(2)}) collective-permute-start(bf16[64,1024]{1,0:T(8,128)(2,1)S(1)} %add_convert_fusion.1), channel_id=1, source_target_pairs={{0,2},{2,0},{1,3},{3,1},{4,6},{6,4},{5,7},{7,5},{8,10},{10,8},{9,1... | collective-permute-start | bytes 393224 | tf_op jit(solution)/shard_map/ppermute | solution.py:574
  227.8 1.4 collective-permute-start.21
  232.7 1.3 copy-start.1
  233.9 36.2 %all-to-all-start.5 = ((bf16[32,112,256]{2,1,0:T(8,128)(2,1)}), bf16[32,112,256]{2,1,0:T(8,128)(2,1)S(1)}, u32[]{:S(2)}, u32[]{:S(2)}) async-start(bf16[32,112,256]{2,1,0:T(8,128)(2,1)} %copy-done.1), calls=%async_computation.5 | async-start | bytes 3670016 | tf_op jit(solution)/shard_map/all_to_all | solution.py:30
  244.4 2.1 copy-start.4

commit v3 on v2

--- a/solution.py
+++ b/solution.py
@@ -415,7 +415,7 @@
         out_ref[:, q, :, 256:512] = d_x.astype(bf16).reshape(32, 16, 256)
 
 
-def expert_grad_kernel(in_ref, hidden_ref, near_ref, far_ref, *, send):
+def expert_grad_kernel(in_ref, hidden_ref, own_ref, give_ref, last_ref, far_ref, *, send):
     act_ref, dgate_ref, dup_ref = (hidden_ref.at[:, 512 * n : 512 * n + 512] for n in range(3))
     for q in range(4):
         here = slice(256 * q, 256 * q + 256)
@@ -424,13 +424,18 @@
         g_gate = dot_tn(x, dgate_ref[...]).astype(bf16)
         g_up = dot_tn(x, dup_ref[...]).astype(bf16)
         g_down = dot_tn(act_ref[...], d).astype(bf16)
-        for p in range(4):
-            to = near_ref if p < 2 else far_ref
-            to[p % 2, 0, here, :] = g_gate[:, 128 * p : 128 * p + 128]
-            to[p % 2, 1, here, :] = g_up[:, 128 * p : 128 * p + 128]
+        blocks = (
+            (own_ref.at[0], own_ref.at[1], own_ref.at[2]),
+            (give_ref.at[0], give_ref.at[1], last_ref),
+            (far_ref.at[0, 0], far_ref.at[0, 1], far_ref.at[0, 2]),
+            (far_ref.at[1, 0], far_ref.at[1, 1], far_ref.at[1, 2]),
+        )
+        for p, (gate, up, down) in enumerate(blocks):
+            gate[here, :] = g_gate[:, 128 * p : 128 * p + 128]
+            up[here, :] = g_up[:, 128 * p : 128 * p + 128]
             for n in range(2):
                 at = 256 * q + 128 * n
-                to[p % 2, 2, at : at + 128, :] = g_down[128 * p : 128 * p + 128, 128 * n : 128 * n + 128]
+                down[at : at + 128, :] = g_down[128 * p : 128 * p + 128, 128 * n : 128 * n + 128]
 
 
 def combine_kernel(back_ref, gates_ref, cot_ref, sent_ref, dgates_ref, *, send
@@ -510,13 +515,21 @@
 
 
 def late_kernel(
-    back_ref, cos_ref, sin_ref, normed_ref, wk_ref, wv_ref, first_ref, filled_ref,
+    back_ref, cos_ref, sin_ref, normed_ref, wk_ref, wv_ref, wq_ref, dq_ref, dq_got_ref, tokens_ref, filled_ref,
     parts_ref, keep_ref, give_ref,
-    kv_ref, sems, *, send, ready
+    q_ref, kv_ref, sems, *, send, ready
 ):
-    _, _, _, core = places()
-    move = pltpu.make_async_copy(kv_ref, parts_ref.at[:, 80:112, :], sems.at[0])
-    ready(0)
+    _, side, _, core = places()
+    move_q = pltpu.make_async_copy(q_ref, parts_ref.at[:, 0:32, :], sems.at[0])
+    move_kv = pltpu.make_async_copy(kv_ref, parts_ref.at[:, 80:112, :], sems.at[1])
+    ready(3)
+    ready(7)
+    ready(8)
+    own, got = dq_ref[...].astype(f32), dq_got_ref[...].astype(f32)
+    d_q = jnp.concatenate([jnp.where(side == 0, own, got), jnp.where(side == 0, got, own)], 0).T
+    d_q = d_q.astype(bf16)
+    q_ref[...] = dot_tn(normed_ref[...], d_q).astype(bf16).reshape(32, 32, 256)
+    move_q.start()
     ready(1)
     ready(2)
     heads = []
@@ -529,24 +542,30 @@
     low = lanes_of((128, 128)) < 64
     d_k = jnp.where(low, heads[0], swap_halves(heads[1])).astype(bf16)
     d_v = jnp.where(low, swap_halves(heads[0]), heads[1]).astype(bf16)
-    ready(3)
     kv_ref[:, :, 0:128] = dot_tn(normed_ref[...], d_k).astype(bf16).reshape(32, 32, 128)
     kv_ref[:, :, 128:256] = dot_tn(normed_ref[...], d_v).astype(bf16).reshape(32, 32, 128)
-    move.start()
+    move_kv.start()
     ready(4)
     ready(5)
     ready(6)
-    first = first_ref[...] + dot_nt(d_k, wk_ref[...]) + dot_nt(d_v, wv_ref[...])
-    keep_ref[...] = jnp.where(core == 0, first[0:64], first[64:128]).astype(bf16)
-    give_ref[...] = jnp.where(core == 0, first[64:128], first[0:64]).astype(bf16)
-    move.wait()
+    ready(9)
+    first = dot_nt(d_q, wq_ref[...]) + dot_nt(d_k, wk_ref[...]) + dot_nt(d_v, wv_ref[...])
+    x = tokens_ref[...].astype(f32)
+    unit = x * lax.rsqrt(jnp.mean(x * x, -1, keepdims=True) + epsilon)
+    gain = jnp.sum(first * unit, 0, keepdims=True)
+    for to, low_half in ((keep_ref, 0), (give_ref, 1)):
+        to[0:64, :] = jnp.where(core == low_half, first[0:64], first[64:128]).astype(bf16)
+        to[64:80, :] = jnp.broadcast_to(gain, (16, 1024)).astype(bf16)
+    move_q.wait()
+    move_kv.wait()
 
 
 def share_kernel(in_ref, gain_ref, out_ref, gain2_ref, total_ref, *, send):
     total_ref[...] = jnp.sum(in_ref[...].astype(f32), 0)
     for q in range(4):
-        gain2_ref[:, 256 * q : 256 * q + 256] = total_ref[68 + q : 69 + q, :]
-    total_ref[68:72, :] = gain_ref[...].astype(f32)
+        here = slice(256 * q, 256 * q + 256)
+        gain2_ref[:, here] = total_ref[68 + q : 69 + q, :]
+        total_ref[72 + q : 73 + q, :] = gain_ref[0:1, here].astype(f32)
     out_ref[...] = jnp.broadcast_to(total_ref[...].astype(bf16)[None], (32, 112, 256))
 
 
@@ -564,14 +583,17 @@
     extra_ref[...] = in_ref[:, 64:80, :].astype(f32)
     for q in range(4):
         router_ref[:, 256 * q : 256 * q + 256] = extra_ref[:, q, :]
-    for q in range(4):
-        gain_ref[:, 256 * q : 256 * q + 256] = jnp.sum(extra_ref[:, 4 + q, :], 0, keepdims=True)
-
-
-def sum_over_wa(keep, give):
+        gain_ref[:, 256 * q : 256 * q + 256] = jnp.sum(extra_ref[:, 8 + q, :], 0, keepdims=True)
+
+
+def pair_over_wa(keep, give):
     got = lax.ppermute(give, "wa", CORE_SWAP)
     pair = (keep.astype(f32) + got.astype(f32)).astype(bf16)
-    other = lax.ppermute(pair, "wa", CHIP_SWAP)
+    return pair, lax.ppermute(pair, "wa", CHIP_SWAP)
+
+
+def sum_over_wa(keep, give):
+    pair, other = pair_over_wa(keep, give)
     mine = (pair.astype(f32) + other.astype(f32)).astype(bf16)
     return mine, lax.ppermute(mine, "wa", CORE_SWAP)
 
@@ -665,6 +687,7 @@
         (("V", shape((256, rows))), ("V", shape((64, width))), ("V", shape((64, width)))),
         us=0.8,
     )(ctx_mine, ctx_got, w_out)
+    mix_keep, mix_give, w_across = lax.optimization_barrier((mix_keep, mix_give, w_across))
     mine, theirs = sum_over_wa(mix_keep, mix_give)
     middle, normed2, gates, outgoing = on_device(
         route_kernel,
@@ -696,17 +719,24 @@
         down_lanes, down_across, down_beside, down_diagonal,
     )
     back = exchange(returning.reshape(128, 16, 512), ("ctx", "wa")).reshape(2048, 512)
-    near, far = on_device(
+    near_own, near_two, near_last, far = on_device(
         expert_grad_kernel,
         "expert_grads",
         "VV",
-        (("V", shape((2, 3, width, 128))), ("V", shape((2, 3, width, 128)))),
+        (
+            ("V", shape((3, width, 128))),
+            ("V", shape((2, width, 128))),
+            ("V", shape((width, 128))),
+            ("V", shape((2, 3, width, 128))),
+        ),
         us=3,
     )(arrived, hidden)
     far = lax.ppermute(far, "wa", CORE_SWAP)
-    near_sum = near.astype(f32) + far.astype(f32)
-    near_own, near_give = near_sum[0], near_sum[1].astype(bf16)
-    back, near_own, near_give = lax.optimization_barrier((back, near_own, near_give))
+    far = far.astype(f32)
+    near_own = near_own.astype(f32) + far[0]
+    near_two = (near_two.astype(f32) + far[1, :2]).astype(bf16)
+    near_last = (near_last.astype(f32) + far[1, 2]).astype(bf16)
+    back, near_own, near_two, near_last = lax.optimization_barrier((back, near_own, near_two, near_last))
     (sent,) = on_device(
         combine_kernel,
         "combine",
@@ -717,7 +747,7 @@
     )(back, gates, cot_quarter)
 
     pieces = pieces_over_wa(sent)
-    pieces, near_two = lax.optimization_barrier((pieces, near_give[:2]))
+    pieces, near_two = lax.optimization_barrier((pieces, near_two))
     near_got = lax.ppermute(near_two, "wa", CHIP_SWAP)
     d_middle, do_own, do_give, parts, output = on_device(
         second_norm_kernel,
@@ -752,41 +782,37 @@
         q_own, q_other, kv, do_own, do_other, context_o,
         cos_rows, sin_rows, jnp.cos(angles2).T, jnp.sin(angles2).T,
     )
-    dkv, near_got, near_last = lax.optimization_barrier((dkv, near_got, near_give[2]))
+    dkv, near_got, near_last = lax.optimization_barrier((dkv, near_got, near_last))
     kv_back = exchange(dkv, "ctx")
     near_last = lax.ppermute(near_last, "wa", CHIP_SWAP)
 
     dq_got = lax.ppermute(dq_give, "ctx", PARTNER)
     dq_got, near_last = lax.optimization_barrier((dq_got, near_last))
-    d_query = jnp.where(
-        side == 0, jnp.concatenate([dq_own, dq_got], 0), jnp.concatenate([dq_got, dq_own], 0)
-    ).T
-    parts_query = dot_tn(normed1, d_query).astype(bf16).reshape(32, 32, 256)
-    first_query = dot_nt(d_query, w_query)
-    filled = jnp.concatenate([parts_query, parts, jnp.zeros((32, 32, 256), bf16)], 1)
-    kv_back, filled, first_query = lax.optimization_barrier((kv_back, filled, first_query))
+    filled = jnp.pad(parts, ((0, 0), (32, 32), (0, 0)))
+    kv_back, filled, dq_got = lax.optimization_barrier((kv_back, filled, dq_got))
     parts_all, first_keep, first_give = on_device(
         late_kernel,
         "late",
-        "FFFFFFFH",
-        (("H", shape((32, 112, 256))), ("V", shape((64, width))), ("V", shape((64, width)))),
-        [pltpu.VMEM((32, 32, 256), bf16), pltpu.SemaphoreType.DMA((1,))],
+        "VFFFFFFFFFH",
+        (("H", shape((32, 112, 256))), ("V", shape((80, width))), ("V", shape((80, width)))),
+        [
+            pltpu.VMEM((32, 32, 256), bf16),
+            pltpu.VMEM((32, 32, 256), bf16),
+            pltpu.SemaphoreType.DMA((2,)),
+        ],
         megabytes=56,
-        us=1.3,
+        us=2,
         lazy=True,
-        aliases={7: 0},
-    )(kv_back, cos_lanes, sin_lanes, normed1, key_weight, value_weight, first_query, filled)
+        aliases={10: 0},
+    )(
+        kv_back, cos_lanes, sin_lanes, normed1, key_weight, value_weight, w_query, dq_own, dq_got,
+        tokens, filled,
+    )
     summed = exchange(parts_all, "ctx")
 
-    first_mine, first_theirs = sum_over_wa(first_keep, first_give)
-    d_first = jnp.where(
-        core == 0, jnp.stack([first_mine, first_theirs]), jnp.stack([first_theirs, first_mine])
-    ).reshape(rows, width).astype(f32)
-    widened = tokens.astype(f32)
-    root_first = lax.rsqrt(jnp.mean(widened * widened, -1, keepdims=True) + epsilon)
-    unit_first = widened * root_first
-    scaled_first = d_first * norm1_gain
-    grad_gain_first = jnp.sum(d_first * unit_first, 0).astype(bf16).reshape(4, 256)
+    first_pair, first_other = pair_over_wa(first_keep, first_give)
+    summed, first_other = lax.optimization_barrier((summed, first_other))
+    first_mine = (first_pair.astype(f32) + first_other.astype(f32)).astype(bf16)
     shared, out_gain2 = on_device(
         share_kernel,
         "share",
@@ -794,10 +820,18 @@
         (("V", shape((32, 112, 256))), ("V", shape((1, width), f32))),
         [pltpu.VMEM((112, 256), f32)],
         us=0.5,
-    )(summed, grad_gain_first)
-    shared, d_first = lax.optimization_barrier((shared, d_first))
+    )(summed, first_mine[64:])
     spread_out = exchange(shared, "ctx")
 
+    first_half = first_mine[:64]
+    first_theirs = lax.ppermute(first_half, "wa", CORE_SWAP)
+    d_first = jnp.where(
+        core == 0, jnp.stack([first_half, first_theirs]), jnp.stack([first_theirs, first_half])
+    ).reshape(rows, width).astype(f32)
+    widened = tokens.astype(f32)
+    root_first = lax.rsqrt(jnp.mean(widened * widened, -1, keepdims=True) + epsilon)
+    unit_first = widened * root_first
+    scaled_first = d_first * norm1_gain
     grad_tokens = (
         d_middle
         + root_first

time: 273 us -> 267 us (0.978)
  starting transfers between devices: 46.7 us -> 40.7 us
    ppermute x1, waiting for transfers between devices: 0.01 us -> 6.43 us  [local(): near_last = lax.ppermute(near_last, 'wa', CHIP_SWAP)]
    ppermute x2, waiting for transfers between devices: 10.6 us -> 5.52 us  [pieces_over_wa(): across = lax.ppermute(part, 'wa', CHIP_SWAP)]
    all_to_all x5, starting transfers between devices: 36 us -> 31.2 us  [exchange(): return lax.all_to_all(value, axes, split_axis=0, concat_axis=0, tiled=True)]
    convert_element_type x2 -> x6, other arithmetic: 0.08 us -> 3.45 us  [the longest x1 1.67 us: local(): far = far.astype(f32)]
    ppermute x4 -> x5, waiting for transfers between devices: 24.3 us -> 27.1 us  [the longest x2 24.3 us: pair_over_wa(): return (pair, lax.ppermute(pair, 'wa', CHIP_SWAP))]
    unnamed x73 -> x87, local copies, waits for them, and re-layouts: 5.77 us -> 5.68 us
  transfers between devices with their start and end apart: 27 -> 27, of which waited for: 20 -> 20; matrix products, arithmetic and copies ran while one was open for 6% -> 5% of each run, Pallas kernels for 4% -> 5%
where the time goes in v3:
time: 267 us; the launch traced here: 266 us
  waiting for transfers between devices  126 us (47%)
  starting transfers between devices  40.7 us (15%)
  blocking collectives  39.5 us (15%)
  Pallas kernels  36.3 us (14%)
  other arithmetic  12.5 us (5%)
  local copies, waits for them, and re-layouts  8.95 us (3%)
    all_to_all x5, waiting for transfers between devices, exchange(): return lax.all_to_all(value, axes, split_axis=0, concat_axis=0, tiled=True)  57.3 us
    all_to_all x1, blocking collectives, exchange(): return lax.all_to_all(value, axes, split_axis=0, concat_axis=0, tiled=True)  39.5 us
    pallas_call x12, Pallas kernels, call(): pl.pallas_call(body, out_shape=tuple((o for _, o in outs)), in_specs=[pl....  36.3 us
    all_to_all x5, starting transfers between devices, exchange(): return lax.all_to_all(value, axes, split_axis=0, concat_axis=0, tiled=True)  31.2 us
    ppermute x2, waiting for transfers between devices, pair_over_wa(): return (pair, lax.ppermute(pair, 'wa', CHIP_SWAP))  24.3 us
    ppermute x1, waiting for transfers between devices, local(): dq_got = lax.ppermute(dq_give, 'ctx', PARTNER)  7.12 us
    ppermute x1, waiting for transfers between devices, local(): q_other = lax.ppermute(q_give, 'ctx', PARTNER)  6.78 us
    ppermute x1, waiting for transfers between devices, local(): near_last = lax.ppermute(near_last, 'wa', CHIP_SWAP)  6.43 us
  transfers between devices with their start and end apart: 27, of which 20 were waited for; matrix products, arithmetic and copies ran while one was open for 5% of the time, Pallas kernels for 5%

profile of v3, /device:TPU:0, one launch (start us, length us, event | category | flops | bytes accessed | tf_op | source)
XLA Modules:
  0.0 265.9 jit_solution(7047866232904294835)
XLA Ops:
  1.2 0.8 multiply_sine_fusion.1
  2.0 0.8 maximum_maximum_fusion
  2.8 4.4 %prelude.1 = (bf16[32,128,128]{2,1,0:T(8,128)(2,1)}, bf16[128,1024]{1,0:T(8,128)(2,1)}, bf16[128,128]{1,0:T(8,128)(2,1)}, bf16[128,128]{1,0:T(8,128)(2,1)}) custom-call(bf16[128,1024]{1,0:T(8,128)(2,1)} %refs_9_.1, f32[1,1024]{1,0:T(1,128)} %bitcast.76, bf16[1024,256]{1,0:T(8,128)(2,1)} %refs_6_.1, bf16[1024,128]{1,0:T(8,128)(2,1)} %refs_4_.3, ...), custom_call_target="tpu_custom_call" | custom-call | flops 2200000000 | tf_op jit(solution)/shard_map/prelude/pallas_call | solution.py:90
  7.2 11.0 %all-to-all-start = ((bf16[32,128,128]{2,1,0:T(8,128)(2,1)}), bf16[32,128,128]{2,1,0:T(8,128)(2,1)S(1)}, u32[]{:S(2)}, u32[]{:S(2)}) async-start(bf16[32,128,128]{2,1,0:T(8,128)(2,1)} %get-tuple-element.91), calls=%async_computation | async-start | bytes 2097152 | tf_op jit(solution)/shard_map/all_to_all | solution.py:30
  18.3 1.9 collective-permute-start
  20.2 0.7 collective-permute-start.1
  21.1 1.0 pad_maximum_fusion.refs_1_
  22.1 0.9 constant_dynamic-slice_fusion.refs_6_.refs_2_
  23.0 6.8 %collective-permute-done.refs_1_ = bf16[128,128]{1,0:T(8,128)(2,1)S(1)} collective-permute-done((bf16[128,128]{1,0:T(8,128)(2,1)S(1)}, bf16[128,128]{1,0:T(8,128)(2,1)S(1)}, u32[]{:S(2)}, u32[]{:S(2)}) %collective-permute-start) | collective-permute-done | bytes 32800 | tf_op jit(solution)/shard_map/ppermute | solution.py:649
  29.7 6.3 %collective-permute-done.1.refs_6_ = bf16[1024,128]{1,0:T(8,128)(2,1)S(1)} collective-permute-done((bf16[1024,128]{1,0:T(8,128)(2,1)S(1)}, bf16[1024,128]{1,0:T(8,128)(2,1)S(1)}, u32[]{:S(2)}, u32[]{:S(2)}) %collective-permute-start.1) | collective-permute-done | bytes 262176 | tf_op jit(solution)/shard_map/ppermute | solution.py:662
  36.1 3.0 %all-to-all-done.refs_2_ = bf16[32,128,128]{2,1,0:T(8,128)(2,1)S(1)} async-done(((bf16[32,128,128]{2,1,0:T(8,128)(2,1)}), bf16[32,128,128]{2,1,0:T(8,128)(2,1)S(1)}, u32[]{:S(2)}, u32[]{:S(2)}) %all-to-all-start) | async-done | bytes 1048608 | tf_op jit(solution)/shard_map/all_to_all | solution.py:30
  39.1 0.6 collective-permute-start.3
  39.7 4.8 %attend.1 = (bf16[128,128]{1,0:T(8,128)(2,1)S(1)}, bf16[128,128]{1,0:T(8,128)(2,1)S(1)}, f32[72,512]{1,0:T(8,128)S(1)}) custom-call(bf16[128,128]{1,0:T(8,128)(2,1)S(1)} %copy-done.19, bf16[128,128]{1,0:T(8,128)(2,1)S(1)} %collective-permute-done.refs_1_, bf16[32,128,128]{2,1,0:T(8,128)(2,1)S(1)} %all-to-all-done.refs_2_), custom_call_target="tpu_custom_call" | custom-call | flops 550000000 | tf_op jit(solution)/shard_map/attend/pallas_call | solution.py:90
  44.5 0.7 collective-permute-start.2
  45.2 3.3 %collective-permute-done.2.refs_1_ = bf16[128,128]{1,0:T(8,128)(2,1)S(1)} collective-permute-done((bf16[128,128]{1,0:T(8,128)(2,1)S(1)}, bf16[128,128]{1,0:T(8,128)(2,1)S(1)}, u32[]{:S(2)}, u32[]{:S(2)}) %collective-permute-start.2) | collective-permute-done | bytes 32800 | tf_op jit(solution)/shard_map/ppermute | solution.py:682
  48.8 0.9 collective-permute-done.3.refs_2_
  49.8 1.3 collective-permute-done.4
  51.2 0.7 collective-permute-start.5
  51.9 0.5 collective-permute-start.8
  52.4 4.4 %collective-permute-done.5 = bf16[64,1024]{1,0:T(8,128)(2,1)S(1)} collective-permute-done((bf16[64,1024]{1,0:T(8,128)(2,1)S(1)}, bf16[64,1024]{1,0:T(8,128)(2,1)S(1)}, u32[]{:S(2)}, u32[]{:S(2)}) %collective-permute-start.5) | collective-permute-done | bytes 131104 | tf_op jit(solution)/shard_map/ppermute | solution.py:592
  57.5 0.7 collective-permute-done.6.refs_2_
  58.3 1.1 route.1
  59.5 39.5 %all_to_all.30 = bf16[128,16,512]{2,1,0:T(8,128)(2,1)S(1)} all-to-all(bf16[128,16,512]{2,1,0:T(8,128)(2,1)S(1)} %bitcast.59), channel_id=1, replica_groups=mesh['ctx'=32,'wa'=4] {'ctx','wa'}, dimensions={0} | all-to-all | bytes 4194304 | tf_op jit(solution)/shard_map/all_to_all | solution.py:30
  99.0 5.5 %experts.1 = (bf16[32,4,16,512]{3,2,1,0:T(8,128)(2,1)}, bf16[512,1536]{1,0:T(8,128)(2,1)S(1)}) custom-call(bf16[32,4,16,512]{3,2,1,0:T(8,128)(2,1)S(1)} %bitcast.60, bf16[2,1024,128]{2,1,0:T(8,128)(2,1)S(1)} %pad_maximum_fusion.refs_1_, bf16[2,1024,128]{2,1,0:T(8,128)(2,1)S(1)} %collective-permute-done.3.refs_2_, ...), custom_call_target="tpu_custom_call" | custom-call | flops 5500000256 | tf_op jit(solution)/shard_map/experts/pallas_call | solution.py:90
  104.5 3.0 %expert_grads.1 = (bf16[3,1024,128]{2,1,0:T(8,128)(2,1)S(1)}, bf16[2,1024,128]{2,1,0:T(8,128)(2,1)S(1)}, bf16[1024,128]{1,0:T(8,128)(2,1)S(1)}, bf16[2,3,1024,128]{3,2,1,0:T(8,128)(2,1)}) custom-call(bf16[32,4,16,512]{3,2,1,0:T(8,128)(2,1)S(1)} %bitcast.61, bf16[512,1536]{1,0:T(8,128)(2,1)S(1)} %get-tuple-element.114.refs_1_), custom_call_target="tpu_custom_call" | custom-call | flops 3300000000 | tf_op jit(solution)/shard_map/expert_grads/pallas_call | solution.py:90
  107.5 0.9 copy-done.3
  108.4 0.8 copy-done.7
  109.2 4.6 %all-to-all-start.2 = ((bf16[128,16,512]{2,1,0:T(8,128)(2,1)}), bf16[128,16,512]{2,1,0:T(8,128)(2,1)S(1)}, u32[]{:S(2)}, u32[]{:S(2)}) async-start(bf16[128,16,512]{2,1,0:T(8,128)(2,1)} %bitcast.9), calls=%async_computation.2 | async-start | bytes 4194304 | tf_op jit(solution)/shard_map/all_to_all | solution.py:30
  113.8 1.7 convert_element_type.103
  115.5 0.8 fusion.13
  116.3 0.9 fusion.3
  117.2 1.3 fusion
  118.5 25.7 %all-to-all-done.2 = bf16[128,16,512]{2,1,0:T(8,128)(2,1)S(1)} async-done(((bf16[128,16,512]{2,1,0:T(8,128)(2,1)}), bf16[128,16,512]{2,1,0:T(8,128)(2,1)S(1)}, u32[]{:S(2)}, u32[]{:S(2)}) %all-to-all-start.2) | async-done | bytes 2097184 | tf_op jit(solution)/shard_map/all_to_all | solution.py:30
  144.3 1.0 combine.1.refs_0_
  145.3 0.7 collective-permute-start.12
  145.9 4.6 %collective-permute-done.12.refs_1_ = bf16[272,256]{1,0:T(8,128)(2,1)S(1)} collective-permute-done((bf16[272,256]{1,0:T(8,128)(2,1)S(1)}, bf16[272,256]{1,0:T(8,128)(2,1)S(1)}, u32[]{:S(2)}, u32[]{:S(2)}) %collective-permute-start.12) | collective-permute-done | bytes 139296 | tf_op jit(solution)/shard_map/ppermute | solution.py:602
  150.5 1.4 collective-permute-done.14.refs_3_
  152.4 1.8 second_norm.1
  154.2 0.8 copy-done.5
  155.0 3.9 %collective-permute-done.15.refs_4_ = bf16[128,128]{1,0:T(8,128)(2,1)S(1)} collective-permute-done((bf16[128,128]{1,0:T(8,128)(2,1)S(1)}, bf16[128,128]{1,0:T(8,128)(2,1)S(1)}, u32[]{:S(2)}, u32[]{:S(2)}) %collective-permute-start.15) | collective-permute-done | bytes 32800 | tf_op jit(solution)/shard_map/ppermute | solution.py:766
  159.0 6.5 %reverse.1 = (bf16[128,128]{1,0:T(8,128)(2,1)S(1)}, bf16[128,128]{1,0:T(8,128)(2,1)S(1)}, bf16[32,128,128]{2,1,0:T(8,128)(2,1)}) custom-call(bf16[128,128]{1,0:T(8,128)(2,1)S(1)} %copy-done.20, bf16[128,128]{1,0:T(8,128)(2,1)S(1)} %collective-permute-done.refs_1_, bf16[32,128,128]{2,1,0:T(8,128)(2,1)S(1)} %all-to-all-done.refs_2_, ...), custom_call_target="tpu_custom_call" | custom-call | flops 1100000000 | tf_op jit(solution)/shard_map/reverse/pallas_call | solution.py:90
  165.9 0.8 copy-done.31
  166.6 4.4 %all-to-all-start.3 = ((bf16[32,128,128]{2,1,0:T(8,128)(2,1)}), bf16[32,128,128]{2,1,0:T(8,128)(2,1)S(1)}, u32[]{:S(2)}, u32[]{:S(2)}) async-start(bf16[32,128,128]{2,1,0:T(8,128)(2,1)} %get-tuple-element.134), calls=%async_computation.3 | async-start | bytes 2097152 | tf_op jit(solution)/shard_map/all_to_all | solution.py:30
  171.1 0.7 collective-permute-start.18
  171.8 1.7 collective-permute-start.17
  173.5 1.4 pad.4.refs_10_
  174.9 7.1 %collective-permute-done.17.refs_8_ = bf16[128,128]{1,0:T(8,128)(2,1)S(1)} collective-permute-done((bf16[128,128]{1,0:T(8,128)(2,1)S(1)}, bf16[128,128]{1,0:T(8,128)(2,1)S(1)}, u32[]{:S(2)}, u32[]{:S(2)}) %collective-permute-start.17) | collective-permute-done | bytes 32800 | tf_op jit(solution)/shard_map/ppermute | solution.py:789
  182.0 6.4 %collective-permute-done.18 = bf16[1024,128]{1,0:T(8,128)(2,1)S(1)} collective-permute-done((bf16[1024,128]{1,0:T(8,128)(2,1)S(1)}, bf16[1024,128]{1,0:T(8,128)(2,1)S(1)}, u32[]{:S(2)}, u32[]{:S(2)}) %collective-permute-start.18) | collective-permute-done | bytes 262176 | tf_op jit(solution)/shard_map/ppermute | solution.py:787
  188.4 3.5 %all-to-all-done.3.refs_0_ = bf16[32,128,128]{2,1,0:T(8,128)(2,1)S(1)} async-done(((bf16[32,128,128]{2,1,0:T(8,128)(2,1)}), bf16[32,128,128]{2,1,0:T(8,128)(2,1)S(1)}, u32[]{:S(2)}, u32[]{:S(2)}) %all-to-all-start.3) | async-done | bytes 1048608 | tf_op jit(solution)/shard_map/all_to_all | solution.py:30
  191.9 1.0 copy-done.30
  192.9 5.2 %late.1 = (bf16[32,112,256]{2,1,0:T(8,128)(2,1)}, bf16[80,1024]{1,0:T(8,128)(2,1)}, bf16[80,1024]{1,0:T(8,128)(2,1)}) custom-call(bf16[32,128,128]{2,1,0:T(8,128)(2,1)} %copy-done.30, f32[128,128]{1,0:T(8,128)} %get-tuple-element.181.refs_5_.refs_1_, f32[128,128]{1,0:T(8,128)} %get-tuple-element.182.refs_6_.refs_2_, ...), custom_call_target="tpu_custom_call", output_to_operand_aliasing={{0}: (10, {})} | custom-call | flops 2200000000 | tf_op jit(solution)/shard_map/late/pallas_call | solution.py:90
  198.1 6.9 %all-to-all-start.4 = ((bf16[32,112,256]{2,1,0:T(8,128)(2,1)}), bf16[32,112,256]{2,1,0:T(8,128)(2,1)S(1)}, u32[]{:S(2)}, u32[]{:S(2)}) async-start(bf16[32,112,256]{2,1,0:T(8,128)(2,1)} %get-tuple-element.144), calls=%async_computation.4 | async-start | bytes 3670016 | tf_op jit(solution)/shard_map/all_to_all | solution.py:30
  205.1 1.4 collective-permute-done.19
  206.7 19.9 %collective-permute-done.20 = bf16[80,1024]{1,0:T(8,128)(2,1)S(1)} collective-permute-done((bf16[80,1024]{1,0:T(8,128)(2,1)S(1)}, bf16[80,1024]{1,0:T(8,128)(2,1)S(1)}, u32[]{:S(2)}, u32[]{:S(2)}) %collective-permute-start.20) | collective-permute-done | bytes 163872 | tf_op jit(solution)/shard_map/ppermute | solution.py:592
  226.6 6.2 %all-to-all-done.4.refs_0_ = bf16[32,112,256]{2,1,0:T(8,128)(2,1)S(1)} async-done(((bf16[32,112,256]{2,1,0:T(8,128)(2,1)}), bf16[32,112,256]{2,1,0:T(8,128)(2,1)S(1)}, u32[]{:S(2)}, u32[]{:S(2)}) %all-to-all-start.4) | async-done | bytes 1835040 | tf_op jit(solution)/shard_map/all_to_all | solution.py:30
  232.9 0.9 share.1
  233.8 1.2 copy-done.2
  235.0 4.2 %all-to-all-start.5 = ((bf16[32,112,256]{2,1,0:T(8,128)(2,1)}), bf16[32,112,256]{2,1,0:T(8,128)(2,1)S(1)}, u32[]{:S(2)}, u32[]{:S(2)}) async-start(bf16[32,112,256]{2,1,0:T(8,128)(2,1)} %copy-done.2), calls=%async_computation.5 | async-start | bytes 3670016 | tf_op jit(solution)/shard_map/all_to_all | solution.py:30
  239.4 2.3 add_bitcast_fusion
  241.8 1.1 bitcast_add_fusion
  242.9 0.8 copy.37
  244.0 0.9 fusion.10
  245.0 18.9 %all-to-all-done.5.refs_0_ = bf16[32,112,256]{2,1,0:T(8,128)(2,1)S(1)} async-done(((bf16[32,112,256]{2,1,0:T(8,128)(2,1)}), bf16[32,112,256]{2,1,0:T(8,128)(2,1)S(1)}, u32[]{:S(2)}, u32[]{:S(2)}) %all-to-all-start.5) | async-done | bytes 1835040 | tf_op jit(solution)/shard_map/all_to_all | solution.py:30
  263.9 1.8 final.1
  (125 shorter events, 3.7 us)
Async XLA Ops:
  7.2 11.1 %copy-start.41 = (bf16[128,128]{1,0:T(8,128)(2,1)S(1)}, bf16[128,128]{1,0:T(8,128)(2,1)}, u32[]{:S(2)}) copy-start(bf16[128,128]{1,0:T(8,128)(2,1)} %get-tuple-element.92) | copy-start | bytes 98308
  7.2 13.0 %copy-start.34 = (bf16[1,128,1024]{2,1,0:T(8,128)(2,1)S(1)}, bf16[1,128,1024]{2,1,0:T(8,128)(2,1)}, u32[]{:S(2)}) copy-start(bf16[1,128,1024]{2,1,0:T(8,128)(2,1)} %param.23) | copy-start | bytes 786436
  7.2 13.7 %copy-start.39 = (s32[128,8]{0,1:T(8,128)S(1)}, s32[128,8]{0,1:T(8,128)}, u32[]{:S(2)}) copy-start(s32[128,8]{0,1:T(8,128)} %param.24) | copy-start | bytes 12292
  7.2 13.9 %copy-start.35 = (bf16[1,1024,128]{2,1,0:T(8,128)(2,1)S(1)}, bf16[1,1024,128]{2,1,0:T(8,128)(2,1)}, u32[]{:S(2)}) copy-start(bf16[1,1024,128]{2,1,0:T(8,128)(2,1)} %param.22) | copy-start | bytes 786436
  7.2 32.4 %copy-start.19 = (bf16[128,128]{1,0:T(8,128)(2,1)S(1)}, bf16[128,128]{1,0:T(8,128)(2,1)}, u32[]{:S(2)}) copy-start(bf16[128,128]{1,0:T(8,128)(2,1)} %get-tuple-element.90.refs_0_) | copy-start | bytes 98308
  7.2 31.8 %all-to-all-start = ((bf16[32,128,128]{2,1,0:T(8,128)(2,1)}), bf16[32,128,128]{2,1,0:T(8,128)(2,1)S(1)}, u32[]{:S(2)}, u32[]{:S(2)}) async-start(bf16[32,128,128]{2,1,0:T(8,128)(2,1)} %get-tuple-element.91), calls=%async_computation | async-start | bytes 2097152 | tf_op jit(solution)/shard_map/all_to_all | solution.py:30
  18.3 11.5 %collective-permute-start = (bf16[128,128]{1,0:T(8,128)(2,1)S(1)}, bf16[128,128]{1,0:T(8,128)(2,1)S(1)}, u32[]{:S(2)}, u32[]{:S(2)}) collective-permute-start(bf16[128,128]{1,0:T(8,128)(2,1)S(1)} %copy-done.41), channel_id=1, source_target_pairs={{0,8},{4,12},{8,0},{12,4},{16,24},{20,28},{24,16},{28,20},{32,40},... | collective-permute-start | bytes 98312 | tf_op jit(solution)/shard_map/ppermute | solution.py:649
  20.2 28.3 %copy-start.12 = (bf16[256,1024]{1,0:T(8,128)(2,1)S(1)}, bf16[256,1024]{1,0:T(8,128)(2,1)}, u32[]{:S(2)}) copy-start(bf16[256,1024]{1,0:T(8,128)(2,1)} %refs_10_.1) | copy-start | bytes 1572868
  20.2 15.8 %collective-permute-start.1 = (bf16[1024,128]{1,0:T(8,128)(2,1)S(1)}, bf16[1024,128]{1,0:T(8,128)(2,1)S(1)}, u32[]{:S(2)}, u32[]{:S(2)}) collective-permute-start(bf16[1024,128]{1,0:T(8,128)(2,1)S(1)} %bitcast.62), channel_id=1, source_target_pairs={{0,2},{2,0},{1,3},{3,1},{4,6},{6,4},{5,7},{7,5},{8,10},{10,8},{9,1... | collective-permute-start | bytes 786440 | tf_op jit(solution)/shard_map/ppermute | solution.py:662
  39.1 10.7 %collective-permute-start.3 = (bf16[2,1024,128]{2,1,0:T(8,128)(2,1)S(1)}, bf16[2,1024,128]{2,1,0:T(8,128)(2,1)S(1)}, u32[]{:S(2)}, u32[]{:S(2)}) collective-permute-start(bf16[2,1024,128]{2,1,0:T(8,128)(2,1)S(1)} %pad_maximum_fusion.refs_1_), channel_id=1, source_target_pairs={{0,2},{2,0},{1,3},{3,1},{4,6},{6,4},{5,7},{7,5},{8,10},{10,8},{9,1... | collective-permute-start | bytes 1572872 | tf_op jit(solution)/shard_map/ppermute | solution.py:602
  44.5 12.3 %copy-start.17 = (f32[72,512]{1,0:T(8,128)}, f32[72,512]{1,0:T(8,128)S(1)}, u32[]{:S(2)}) copy-start(f32[72,512]{1,0:T(8,128)S(1)} %get-tuple-element.130.refs_5_) | copy-start | bytes 442372
  44.5 4.0 %collective-permute-start.2 = (bf16[128,128]{1,0:T(8,128)(2,1)S(1)}, bf16[128,128]{1,0:T(8,128)(2,1)S(1)}, u32[]{:S(2)}, u32[]{:S(2)}) collective-permute-start(bf16[128,128]{1,0:T(8,128)(2,1)S(1)} %get-tuple-element.96), channel_id=1, source_target_pairs={{0,8},{4,12},{8,0},{12,4},{16,24},{20,28},{24,16},{28,20},{32,40},... | collective-permute-start | bytes 98312 | tf_op jit(solution)/shard_map/ppermute | solution.py:682
  48.5 9.8 %copy-start = (bf16[128,1024]{1,0:T(8,128)(2,1)S(1)}, bf16[128,1024]{1,0:T(8,128)(2,1)}, u32[]{:S(2)}) copy-start(bf16[128,1024]{1,0:T(8,128)(2,1)} %refs_9_.1) | copy-start | bytes 786436
  48.5 9.8 %copy-start.14 = (bf16[1024,32]{0,1:T(8,128)(2,1)S(1)}, bf16[1024,32]{0,1:T(8,128)(2,1)}, u32[]{:S(2)}) copy-start(bf16[1024,32]{0,1:T(8,128)(2,1)} %param.20) | copy-start | bytes 196612
  48.5 9.8 %copy-start.16 = (f32[1024]{0:T(1024)S(1)}, f32[1024]{0:T(1024)}, u32[]{:S(2)}) copy-start(f32[1024]{0:T(1024)} %param.19) | copy-start | bytes 12292
  48.8 9.4 %copy-start.27 = (bf16[256,128]{1,0:T(8,128)(2,1)}, bf16[256,128]{1,0:T(8,128)(2,1)S(1)}, u32[]{:S(2)}) copy-start(bf16[256,128]{1,0:T(8,128)(2,1)S(1)} %get-tuple-element.127.refs_11_) | copy-start | bytes 196612
  49.8 1.3 collective-permute-start.4
  51.2 5.6 %collective-permute-start.5 = (bf16[64,1024]{1,0:T(8,128)(2,1)S(1)}, bf16[64,1024]{1,0:T(8,128)(2,1)S(1)}, u32[]{:S(2)}, u32[]{:S(2)}) collective-permute-start(bf16[64,1024]{1,0:T(8,128)(2,1)S(1)} %add_convert_fusion.3), channel_id=1, source_target_pairs={{0,2},{2,0},{1,3},{3,1},{4,6},{6,4},{5,7},{7,5},{8,10},{10,8},{9,1... | collective-permute-start | bytes 393224 | tf_op jit(solution)/shard_map/ppermute | solution.py:592
  51.9 7.6 %collective-permute-start.7 = (bf16[2,1024,128]{2,1,0:T(8,128)(2,1)S(1)}, bf16[2,1024,128]{2,1,0:T(8,128)(2,1)S(1)}, u32[]{:S(2)}, u32[]{:S(2)}) collective-permute-start(bf16[2,1024,128]{2,1,0:T(8,128)(2,1)S(1)} %pad_maximum_fusion.refs_1_), channel_id=1, source_target_pairs={{0,1},{1,0},{2,3},{3,2},{4,5},{5,4},{6,7},{7,6},{8,9},{9,8},{10,11... | collective-permute-start | bytes 1572872 | tf_op jit(solution)/shard_map/ppermute | solution.py:603
  51.9 7.6 %collective-permute-start.8 = (bf16[2,1024,128]{2,1,0:T(8,128)(2,1)S(1)}, bf16[2,1024,128]{2,1,0:T(8,128)(2,1)S(1)}, u32[]{:S(2)}, u32[]{:S(2)}) collective-permute-start(bf16[2,1024,128]{2,1,0:T(8,128)(2,1)S(1)} %collective-permute-done.3.refs_2_), channel_id=1, source_target_pairs={{0,1},{1,0},{2,3},{3,2},{4,5},{5,4},{6,7},{7,6},{8,9},{9,8},{10,11... | collective-permute-start | bytes 1572872 | tf_op jit(solution)/shard_map/ppermute | solution.py:604
  56.8 1.4 collective-permute-start.6
  56.9 2.5 collective-permute-start.9
  57.4 2.0 collective-permute-start.10
  59.4 39.6 %copy-start.21 = (f32[128,1024]{1,0:T(8,128)}, f32[128,1024]{1,0:T(8,128)S(1)}, u32[]{:S(2)}) copy-start(f32[128,1024]{1,0:T(8,128)S(1)} %get-tuple-element.125.refs_5_) | copy-start | bytes 1572868
  59.4 39.6 %copy-start.23 = (bf16[128,1024]{1,0:T(8,128)(2,1)}, bf16[128,1024]{1,0:T(8,128)(2,1)S(1)}, u32[]{:S(2)}) copy-start(bf16[128,1024]{1,0:T(8,128)(2,1)S(1)} %get-tuple-element.126.refs_6_) | copy-start | bytes 786436
  59.4 39.5 %copy-start.25 = (f32[64,128]{1,0:T(8,128)}, f32[64,128]{1,0:T(8,128)S(1)}, u32[]{:S(2)}) copy-start(f32[64,128]{1,0:T(8,128)S(1)} %get-tuple-element.120.refs_1_.refs_4_) | copy-start | bytes 98308
  109.2 4.7 %collective-permute-start.11 = (bf16[2,3,1024,128]{3,2,1,0:T(8,128)(2,1)}, bf16[2,3,1024,128]{3,2,1,0:T(8,128)(2,1)}, u32[]{:S(2)}, u32[]{:S(2)}) collective-permute-start(bf16[2,3,1024,128]{3,2,1,0:T(8,128)(2,1)} %get-tuple-element.116), channel_id=1, source_target_pairs={{0,1},{1,0},{2,3},{3,2},{4,5},{5,4},{6,7},{7,6},{8,9},{9,8},{10,11... | collective-permute-start | bytes 4718600 | tf_op jit(solution)/shard_map/ppermute | solution.py:734
  109.2 35.0 %all-to-all-start.2 = ((bf16[128,16,512]{2,1,0:T(8,128)(2,1)}), bf16[128,16,512]{2,1,0:T(8,128)(2,1)S(1)}, u32[]{:S(2)}, u32[]{:S(2)}) async-start(bf16[128,16,512]{2,1,0:T(8,128)(2,1)} %bitcast.9), calls=%async_computation.2 | async-start | bytes 4194304 | tf_op jit(solution)/shard_map/all_to_all | solution.py:30
  113.8 2.5 copy-start.8
  115.5 1.7 copy-start.4
  117.2 27.0 %copy-start.26 = (f32[64,128]{1,0:T(8,128)S(1)}, f32[64,128]{1,0:T(8,128)}, u32[]{:S(2)}) copy-start(f32[64,128]{1,0:T(8,128)} %copy-done.25) | copy-start | bytes 98308
  144.2 7.7 %copy-start.33 = (bf16[2,1024,128]{2,1,0:T(8,128)(2,1)S(1)}, bf16[2,1024,128]{2,1,0:T(8,128)(2,1)}, u32[]{:S(2)}) copy-start(bf16[2,1024,128]{2,1,0:T(8,128)(2,1)} %fusion.3) | copy-start | bytes 1572868
  144.2 8.1 %copy-start.9 = (bf16[128,1024]{1,0:T(8,128)(2,1)S(1)}, bf16[128,1024]{1,0:T(8,128)(2,1)}, u32[]{:S(2)}) copy-start(bf16[128,1024]{1,0:T(8,128)(2,1)} %refs_7_.1) | copy-start | bytes 786436
  144.2 8.1 %copy-start.13 = (bf16[256,1024]{1,0:T(8,128)(2,1)S(1)}, bf16[256,1024]{1,0:T(8,128)(2,1)}, u32[]{:S(2)}) copy-start(bf16[256,1024]{1,0:T(8,128)(2,1)} %refs_10_.1) | copy-start | bytes 1572868
  144.2 8.1 %copy-start.15 = (bf16[1024,32]{0,1:T(8,128)(2,1)S(1)}, bf16[1024,32]{0,1:T(8,128)(2,1)}, u32[]{:S(2)}) copy-start(bf16[1024,32]{0,1:T(8,128)(2,1)} %param.20) | copy-start | bytes 196612
  144.2 8.1 %copy-start.22 = (f32[128,1024]{1,0:T(8,128)S(1)}, f32[128,1024]{1,0:T(8,128)}, u32[]{:S(2)}) copy-start(f32[128,1024]{1,0:T(8,128)} %copy-done.21) | copy-start | bytes 1572868
  144.2 8.1 %copy-start.24 = (bf16[128,1024]{1,0:T(8,128)(2,1)S(1)}, bf16[128,1024]{1,0:T(8,128)(2,1)}, u32[]{:S(2)}) copy-start(bf16[128,1024]{1,0:T(8,128)(2,1)} %copy-done.23) | copy-start | bytes 786436
  144.3 8.1 %copy-start.28 = (bf16[256,128]{1,0:T(8,128)(2,1)S(1)}, bf16[256,128]{1,0:T(8,128)(2,1)}, u32[]{:S(2)}) copy-start(bf16[256,128]{1,0:T(8,128)(2,1)} %copy-done.27) | copy-start | bytes 196612
  145.3 5.2 %collective-permute-start.12 = (bf16[272,256]{1,0:T(8,128)(2,1)S(1)}, bf16[272,256]{1,0:T(8,128)(2,1)S(1)}, u32[]{:S(2)}, u32[]{:S(2)}) collective-permute-start(bf16[272,256]{1,0:T(8,128)(2,1)S(1)} %combine.1.refs_0_), channel_id=1, source_target_pairs={{0,2},{2,0},{1,3},{3,1},{4,6},{6,4},{5,7},{7,5},{8,10},{10,8},{9,1... | collective-permute-start | bytes 417800 | tf_op jit(solution)/shard_map/ppermute | solution.py:602
  145.9 4.6 %collective-permute-start.13 = (bf16[272,256]{1,0:T(8,128)(2,1)S(1)}, bf16[272,256]{1,0:T(8,128)(2,1)S(1)}, u32[]{:S(2)}, u32[]{:S(2)}) collective-permute-start(bf16[272,256]{1,0:T(8,128)(2,1)S(1)} %combine.1.refs_0_), channel_id=1, source_target_pairs={{0,1},{1,0},{2,3},{3,2},{4,5},{5,4},{6,7},{7,6},{8,9},{9,8},{10,11... | collective-permute-start | bytes 417800 | tf_op jit(solution)/shard_map/ppermute | solution.py:603
  150.5 1.4 collective-permute-start.14
  151.9 14.0 %collective-permute-start.16 = (bf16[2,1024,128]{2,1,0:T(8,128)(2,1)S(1)}, bf16[2,1024,128]{2,1,0:T(8,128)(2,1)S(1)}, u32[]{:S(2)}, u32[]{:S(2)}) collective-permute-start(bf16[2,1024,128]{2,1,0:T(8,128)(2,1)S(1)} %copy-done.33), channel_id=1, source_target_pairs={{0,2},{2,0},{1,3},{3,1},{4,6},{6,4},{5,7},{7,5},{8,10},{10,8},{9,1... | collective-permute-start | bytes 1572872 | tf_op jit(solution)/shard_map/ppermute | solution.py:751
  152.4 6.5 %copy-start.10 = (f32[32,128]{1,0:T(8,128)S(1)}, f32[32,128]{1,0:T(8,128)}, u32[]{:S(2)}) copy-start(f32[32,128]{1,0:T(8,128)} %get-tuple-element.179.refs_7_.refs_6_) | copy-start | bytes 49156
  152.4 6.5 %copy-start.11 = (f32[32,128]{1,0:T(8,128)S(1)}, f32[32,128]{1,0:T(8,128)}, u32[]{:S(2)}) copy-start(f32[32,128]{1,0:T(8,128)} %get-tuple-element.180.refs_8_.refs_7_) | copy-start | bytes 49156
  152.4 6.5 %copy-start.18 = (f32[72,512]{1,0:T(8,128)S(1)}, f32[72,512]{1,0:T(8,128)}, u32[]{:S(2)}) copy-start(f32[72,512]{1,0:T(8,128)} %copy-done.17) | copy-start | bytes 442372
  152.4 6.5 %copy-start.20 = (bf16[128,128]{1,0:T(8,128)(2,1)S(1)}, bf16[128,128]{1,0:T(8,128)(2,1)}, u32[]{:S(2)}) copy-start(bf16[128,128]{1,0:T(8,128)(2,1)} %get-tuple-element.90.refs_0_) | copy-start | bytes 98308
  155.0 3.9 %collective-permute-start.15 = (bf16[128,128]{1,0:T(8,128)(2,1)S(1)}, bf16[128,128]{1,0:T(8,128)(2,1)S(1)}, u32[]{:S(2)}, u32[]{:S(2)}) collective-permute-start(bf16[128,128]{1,0:T(8,128)(2,1)S(1)} %get-tuple-element.129), channel_id=1, source_target_pairs={{0,8},{4,12},{8,0},{12,4},{16,24},{20,28},{24,16},{28,20},{32,40},... | collective-permute-start | bytes 98312 | tf_op jit(solution)/shard_map/ppermute | solution.py:766
  165.4 9.5 %copy-start.29 = (bf16[128,128]{1,0:T(8,128)(2,1)}, bf16[128,128]{1,0:T(8,128)(2,1)S(1)}, u32[]{:S(2)}) copy-start(bf16[128,128]{1,0:T(8,128)(2,1)S(1)} %get-tuple-element.141.refs_7_) | copy-start | bytes 98308
  165.4 5.6 %copy-start.36 = (bf16[1024,128]{1,0:T(8,128)(2,1)S(1)}, bf16[1024,128]{1,0:T(8,128)(2,1)}, u32[]{:S(2)}) copy-start(bf16[1024,128]{1,0:T(8,128)(2,1)} %fusion.13) | copy-start | bytes 786436
  166.6 25.2 %all-to-all-start.3 = ((bf16[32,128,128]{2,1,0:T(8,128)(2,1)}), bf16[32,128,128]{2,1,0:T(8,128)(2,1)S(1)}, u32[]{:S(2)}, u32[]{:S(2)}) async-start(bf16[32,128,128]{2,1,0:T(8,128)(2,1)} %get-tuple-element.134), calls=%async_computation.3 | async-start | bytes 2097152 | tf_op jit(solution)/shard_map/all_to_all | solution.py:30
  171.1 17.3 %collective-permute-start.18 = (bf16[1024,128]{1,0:T(8,128)(2,1)S(1)}, bf16[1024,128]{1,0:T(8,128)(2,1)S(1)}, u32[]{:S(2)}, u32[]{:S(2)}) collective-permute-start(bf16[1024,128]{1,0:T(8,128)(2,1)S(1)} %copy-done.36), channel_id=1, source_target_pairs={{0,2},{2,0},{1,3},{3,1},{4,6},{6,4},{5,7},{7,5},{8,10},{10,8},{9,1... | collective-permute-start | bytes 786440 | tf_op jit(solution)/shard_map/ppermute | solution.py:787
  171.8 10.2 %collective-permute-start.17 = (bf16[128,128]{1,0:T(8,128)(2,1)S(1)}, bf16[128,128]{1,0:T(8,128)(2,1)S(1)}, u32[]{:S(2)}, u32[]{:S(2)}) collective-permute-start(bf16[128,128]{1,0:T(8,128)(2,1)S(1)} %get-tuple-element.136), channel_id=1, source_target_pairs={{0,8},{4,12},{8,0},{12,4},{16,24},{20,28},{24,16},{28,20},{32,40},... | collective-permute-start | bytes 98312 | tf_op jit(solution)/shard_map/ppermute | solution.py:789
  182.0 9.9 %copy-start.42 = (bf16[128,128]{1,0:T(8,128)(2,1)}, bf16[128,128]{1,0:T(8,128)(2,1)S(1)}, u32[]{:S(2)}) copy-start(bf16[128,128]{1,0:T(8,128)(2,1)S(1)} %collective-permute-done.17.refs_8_) | copy-start | bytes 98308
  198.1 7.0 %copy-start.40 = (bf16[80,1024]{1,0:T(8,128)(2,1)S(1)}, bf16[80,1024]{1,0:T(8,128)(2,1)}, u32[]{:S(2)}) copy-start(bf16[80,1024]{1,0:T(8,128)(2,1)} %get-tuple-element.146) | copy-start | bytes 491524
  198.1 8.4 %copy-start.37 = (bf16[80,1024]{1,0:T(8,128)(2,1)S(1)}, bf16[80,1024]{1,0:T(8,128)(2,1)}, u32[]{:S(2)}) copy-start(bf16[80,1024]{1,0:T(8,128)(2,1)} %get-tuple-element.145) | copy-start | bytes 491524
  198.1 34.7 %all-to-all-start.4 = ((bf16[32,112,256]{2,1,0:T(8,128)(2,1)}), bf16[32,112,256]{2,1,0:T(8,128)(2,1)S(1)}, u32[]{:S(2)}, u32[]{:S(2)}) async-start(bf16[32,112,256]{2,1,0:T(8,128)(2,1)} %get-tuple-element.144), calls=%async_computation.4 | async-start | bytes 3670016 | tf_op jit(solution)/shard_map/all_to_all | solution.py:30
  205.1 1.5 collective-permute-start.19
  206.6 20.0 %collective-permute-start.20 = (bf16[80,1024]{1,0:T(8,128)(2,1)S(1)}, bf16[80,1024]{1,0:T(8,128)(2,1)S(1)}, u32[]{:S(2)}, u32[]{:S(2)}) collective-permute-start(bf16[80,1024]{1,0:T(8,128)(2,1)S(1)} %add_convert_fusion.1), channel_id=1, source_target_pairs={{0,2},{2,0},{1,3},{3,1},{4,6},{6,4},{5,7},{7,5},{8,10},{10,8},{9,1... | collective-permute-start | bytes 491528 | tf_op jit(solution)/shard_map/ppermute | solution.py:592
  235.0 4.2 %copy-start.1 = (bf16[128,1024]{1,0:T(8,128)(2,1)S(1)}, bf16[128,1024]{1,0:T(8,128)(2,1)}, u32[]{:S(2)}) copy-start(bf16[128,1024]{1,0:T(8,128)(2,1)} %refs_9_.1) | copy-start | bytes 786436
  235.0 4.3 %copy-start.32 = (bf16[2,1024,128]{2,1,0:T(8,128)(2,1)S(1)}, bf16[2,1024,128]{2,1,0:T(8,128)(2,1)}, u32[]{:S(2)}) copy-start(bf16[2,1024,128]{2,1,0:T(8,128)(2,1)} %copy-done.31) | copy-start | bytes 1572868
  235.0 28.8 %all-to-all-start.5 = ((bf16[32,112,256]{2,1,0:T(8,128)(2,1)}), bf16[32,112,256]{2,1,0:T(8,128)(2,1)S(1)}, u32[]{:S(2)}, u32[]{:S(2)}) async-start(bf16[32,112,256]{2,1,0:T(8,128)(2,1)} %copy-done.2), calls=%async_computation.5 | async-start | bytes 3670016 | tf_op jit(solution)/shard_map/all_to_all | solution.py:30
  241.6 2.1 copy-start.38
  241.6 2.4 copy-start.6
  241.7 2.1 collective-permute-start.21
  (6 other events, 5.5 us)

commit v4 on v3

--- a/solution.py
+++ b/solution.py
@@ -731,12 +731,14 @@
         ),
         us=3,
     )(arrived, hidden)
+    back, near_own, near_two, near_last, far = lax.optimization_barrier(
+        (back, near_own, near_two, near_last, far)
+    )
     far = lax.ppermute(far, "wa", CORE_SWAP)
     far = far.astype(f32)
     near_own = near_own.astype(f32) + far[0]
     near_two = (near_two.astype(f32) + far[1, :2]).astype(bf16)
     near_last = (near_last.astype(f32) + far[1, 2]).astype(bf16)
-    back, near_own, near_two, near_last = lax.optimization_barrier((back, near_own, near_two, near_last))
     (sent,) = on_device(
         combine_kernel,
         "combine",
@@ -784,10 +786,8 @@
     )
     dkv, near_got, near_last = lax.optimization_barrier((dkv, near_got, near_last))
     kv_back = exchange(dkv, "ctx")
-    near_last = lax.ppermute(near_last, "wa", CHIP_SWAP)
 
     dq_got = lax.ppermute(dq_give, "ctx", PARTNER)
-    dq_got, near_last = lax.optimization_barrier((dq_got, near_last))
     filled = jnp.pad(parts, ((0, 0), (32, 32), (0, 0)))
     kv_back, filled, dq_got = lax.optimization_barrier((kv_back, filled, dq_got))
     parts_all, first_keep, first_give = on_device(
@@ -821,7 +821,9 @@
         [pltpu.VMEM((112, 256), f32)],
         us=0.5,
     )(summed, first_mine[64:])
+    shared, near_last = lax.optimization_barrier((shared, near_last))
     spread_out = exchange(shared, "ctx")
+    near_last = lax.ppermute(near_last, "wa", CHIP_SWAP)
 
     first_half = first_mine[:64]
     first_theirs = lax.ppermute(first_half, "wa", CORE_SWAP)

time: 267 us -> 265 us (level)
  local copies, waits for them, and re-layouts: 8.95 us -> 17 us
  other arithmetic: 12.5 us -> 7.62 us
    all_to_all x5, waiting for transfers between devices: 57.3 us -> 42.6 us  [exchange(): return lax.all_to_all(value, axes, split_axis=0, concat_axis=0, tiled=True)]
    ppermute x1, waiting for transfers between devices: 6.43 us -> 18.5 us  [local(): near_last = lax.ppermute(near_last, 'wa', CHIP_SWAP)]
    unnamed x87 -> x97, local copies, waits for them, and re-layouts: 5.68 us -> 13.7 us
  transfers between devices with their start and end apart: 27 -> 27, of which waited for: 20 -> 19; matrix products, arithmetic and copies ran while one was open for 5% -> 3% of each run, Pallas kernels for 5% -> 7%
where the time goes in v4:
time: 265 us; the launch traced here: 264 us
  waiting for transfers between devices  125 us (47%)
  starting transfers between devices  39.6 us (15%)
  blocking collectives  39.5 us (15%)
  Pallas kernels  33.9 us (13%)
  local copies, waits for them, and re-layouts  17 us (6%)
  other arithmetic  7.62 us (3%)
    all_to_all x5, waiting for transfers between devices, exchange(): return lax.all_to_all(value, axes, split_axis=0, concat_axis=0, tiled=True)  42.6 us
    all_to_all x1, blocking collectives, exchange(): return lax.all_to_all(value, axes, split_axis=0, concat_axis=0, tiled=True)  39.5 us
    pallas_call x12, Pallas kernels, call(): pl.pallas_call(body, out_shape=tuple((o for _, o in outs)), in_specs=[pl....  33.9 us
    all_to_all x5, starting transfers between devices, exchange(): return lax.all_to_all(value, axes, split_axis=0, concat_axis=0, tiled=True)  28.7 us
    ppermute x2, waiting for transfers between devices, pair_over_wa(): return (pair, lax.ppermute(pair, 'wa', CHIP_SWAP))  24.7 us
    ppermute x1, waiting for transfers between devices, local(): near_last = lax.ppermute(near_last, 'wa', CHIP_SWAP)  18.5 us
    unnamed x97, local copies, waits for them, and re-layouts  13.7 us
    ppermute x1, waiting for transfers between devices, local(): dq_got = lax.ppermute(dq_give, 'ctx', PARTNER)  8.34 us
  transfers between devices with their start and end apart: 27, of which 19 were waited for; matrix products, arithmetic and copies ran while one was open for 3% of the time, Pallas kernels for 7%

profile of v4, /device:TPU:0, one launch (start us, length us, event | category | flops | bytes accessed | tf_op | source)
XLA Modules:
  0.0 264.5 jit_solution(4658597087028664665)
XLA Ops:
  1.2 0.8 multiply_sine_fusion.1
  2.0 0.8 maximum_maximum_fusion
  2.7 4.4 %prelude.1 = (bf16[32,128,128]{2,1,0:T(8,128)(2,1)}, bf16[128,1024]{1,0:T(8,128)(2,1)}, bf16[128,128]{1,0:T(8,128)(2,1)}, bf16[128,128]{1,0:T(8,128)(2,1)}) custom-call(bf16[128,1024]{1,0:T(8,128)(2,1)} %refs_9_.1, f32[1,1024]{1,0:T(1,128)} %bitcast.79, bf16[1024,256]{1,0:T(8,128)(2,1)} %refs_6_.1, bf16[1024,128]{1,0:T(8,128)(2,1)} %refs_4_.3, ...), custom_call_target="tpu_custom_call" | custom-call | flops 2200000000 | tf_op jit(solution)/shard_map/prelude/pallas_call | solution.py:90
  7.2 11.0 %all-to-all-start = ((bf16[32,128,128]{2,1,0:T(8,128)(2,1)}), bf16[32,128,128]{2,1,0:T(8,128)(2,1)S(1)}, u32[]{:S(2)}, u32[]{:S(2)}) async-start(bf16[32,128,128]{2,1,0:T(8,128)(2,1)} %get-tuple-element.92), calls=%async_computation | async-start | bytes 2097152 | tf_op jit(solution)/shard_map/all_to_all | solution.py:30
  18.3 1.9 collective-permute-start
  20.2 0.7 collective-permute-start.1
  21.2 0.9 constant_dynamic-slice_fusion.refs_6_.refs_2_
  22.0 7.7 %collective-permute-done.refs_1_ = bf16[128,128]{1,0:T(8,128)(2,1)S(1)} collective-permute-done((bf16[128,128]{1,0:T(8,128)(2,1)S(1)}, bf16[128,128]{1,0:T(8,128)(2,1)S(1)}, u32[]{:S(2)}, u32[]{:S(2)}) %collective-permute-start) | collective-permute-done | bytes 32800 | tf_op jit(solution)/shard_map/ppermute | solution.py:649
  29.7 6.3 %collective-permute-done.1.refs_6_ = bf16[1024,128]{1,0:T(8,128)(2,1)S(1)} collective-permute-done((bf16[1024,128]{1,0:T(8,128)(2,1)S(1)}, bf16[1024,128]{1,0:T(8,128)(2,1)S(1)}, u32[]{:S(2)}, u32[]{:S(2)}) %collective-permute-start.1) | collective-permute-done | bytes 262176 | tf_op jit(solution)/shard_map/ppermute | solution.py:662
  36.1 3.0 %all-to-all-done.refs_2_ = bf16[32,128,128]{2,1,0:T(8,128)(2,1)S(1)} async-done(((bf16[32,128,128]{2,1,0:T(8,128)(2,1)}), bf16[32,128,128]{2,1,0:T(8,128)(2,1)S(1)}, u32[]{:S(2)}, u32[]{:S(2)}) %all-to-all-start) | async-done | bytes 1048608 | tf_op jit(solution)/shard_map/all_to_all | solution.py:30
  39.1 0.6 collective-permute-start.3
  39.7 4.8 %attend.1 = (bf16[128,128]{1,0:T(8,128)(2,1)S(1)}, bf16[128,128]{1,0:T(8,128)(2,1)S(1)}, f32[72,512]{1,0:T(8,128)S(1)}) custom-call(bf16[128,128]{1,0:T(8,128)(2,1)S(1)} %copy-done.23, bf16[128,128]{1,0:T(8,128)(2,1)S(1)} %collective-permute-done.refs_1_, bf16[32,128,128]{2,1,0:T(8,128)(2,1)S(1)} %all-to-all-done.refs_2_), custom_call_target="tpu_custom_call" | custom-call | flops 550000000 | tf_op jit(solution)/shard_map/attend/pallas_call | solution.py:90
  44.5 0.7 copy-done.21
  45.7 3.3 %collective-permute-done.2.refs_1_ = bf16[128,128]{1,0:T(8,128)(2,1)S(1)} collective-permute-done((bf16[128,128]{1,0:T(8,128)(2,1)S(1)}, bf16[128,128]{1,0:T(8,128)(2,1)S(1)}, u32[]{:S(2)}, u32[]{:S(2)}) %collective-permute-start.2) | collective-permute-done | bytes 32800 | tf_op jit(solution)/shard_map/ppermute | solution.py:682
  49.8 1.3 collective-permute-done.4
  51.2 1.2 collective-permute-start.5
  52.9 3.9 %collective-permute-done.5 = bf16[64,1024]{1,0:T(8,128)(2,1)S(1)} collective-permute-done((bf16[64,1024]{1,0:T(8,128)(2,1)S(1)}, bf16[64,1024]{1,0:T(8,128)(2,1)S(1)}, u32[]{:S(2)}, u32[]{:S(2)}) %collective-permute-start.5) | collective-permute-done | bytes 131104 | tf_op jit(solution)/shard_map/ppermute | solution.py:592
  57.5 0.7 collective-permute-done.6.refs_2_
  58.3 1.1 route.1
  59.5 39.5 %all_to_all.30 = bf16[128,16,512]{2,1,0:T(8,128)(2,1)S(1)} all-to-all(bf16[128,16,512]{2,1,0:T(8,128)(2,1)S(1)} %bitcast.64), channel_id=1, replica_groups=mesh['ctx'=32,'wa'=4] {'ctx','wa'}, dimensions={0} | all-to-all | bytes 4194304 | tf_op jit(solution)/shard_map/all_to_all | solution.py:30
  99.0 4.2 %experts.1 = (bf16[32,4,16,512]{3,2,1,0:T(8,128)(2,1)S(1)}, bf16[512,1536]{1,0:T(8,128)(2,1)S(1)}) custom-call(bf16[32,4,16,512]{3,2,1,0:T(8,128)(2,1)S(1)} %bitcast.61, bf16[2,1024,128]{2,1,0:T(8,128)(2,1)S(1)} %pad_maximum_fusion.refs_1_, bf16[2,1024,128]{2,1,0:T(8,128)(2,1)S(1)} %collective-permute-done.3.refs_2_, ...), custom_call_target="tpu_custom_call" | custom-call | flops 5500000256 | tf_op jit(solution)/shard_map/experts/pallas_call | solution.py:90
  103.2 1.3 copy-done.4
  104.5 1.2 copy-done.27
  105.7 4.6 %all-to-all-start.2 = ((bf16[128,16,512]{2,1,0:T(8,128)(2,1)}), bf16[128,16,512]{2,1,0:T(8,128)(2,1)S(1)}, u32[]{:S(2)}, u32[]{:S(2)}) async-start(bf16[128,16,512]{2,1,0:T(8,128)(2,1)} %bitcast.63), calls=%async_computation.2 | async-start | bytes 4194304 | tf_op jit(solution)/shard_map/all_to_all | solution.py:30
  110.3 1.6 copy-done.3
  111.9 1.4 copy-done.28
  113.3 1.8 expert_grads.1
  115.2 0.9 copy-done.6
  116.1 0.8 copy-done.10
  116.9 1.2 copy-done.15
  118.0 22.7 %all-to-all-done.2 = bf16[128,16,512]{2,1,0:T(8,128)(2,1)S(1)} async-done(((bf16[128,16,512]{2,1,0:T(8,128)(2,1)}), bf16[128,16,512]{2,1,0:T(8,128)(2,1)S(1)}, u32[]{:S(2)}, u32[]{:S(2)}) %all-to-all-start.2) | async-done | bytes 2097184 | tf_op jit(solution)/shard_map/all_to_all | solution.py:30
  140.7 0.8 copy-done.32
  141.5 1.1 combine.1.refs_0_
  142.6 0.7 collective-permute-start.11
  143.5 5.3 %collective-permute-done.11.refs_1_ = bf16[272,256]{1,0:T(8,128)(2,1)S(1)} collective-permute-done((bf16[272,256]{1,0:T(8,128)(2,1)S(1)}, bf16[272,256]{1,0:T(8,128)(2,1)S(1)}, u32[]{:S(2)}, u32[]{:S(2)}) %collective-permute-start.11) | collective-permute-done | bytes 139296 | tf_op jit(solution)/shard_map/ppermute | solution.py:602
  149.2 0.9 collective-permute-done.13.refs_3_
  150.1 0.6 collective-permute-start.16
  150.7 0.6 copy-done.26
  151.5 1.8 second_norm.1
  153.3 0.8 copy-done.8
  154.3 3.8 %collective-permute-done.15.refs_4_ = bf16[128,128]{1,0:T(8,128)(2,1)S(1)} collective-permute-done((bf16[128,128]{1,0:T(8,128)(2,1)S(1)}, bf16[128,128]{1,0:T(8,128)(2,1)S(1)}, u32[]{:S(2)}, u32[]{:S(2)}) %collective-permute-start.15) | collective-permute-done | bytes 32800 | tf_op jit(solution)/shard_map/ppermute | solution.py:768
  158.0 6.5 %reverse.1 = (bf16[128,128]{1,0:T(8,128)(2,1)S(1)}, bf16[128,128]{1,0:T(8,128)(2,1)S(1)}, bf16[32,128,128]{2,1,0:T(8,128)(2,1)}) custom-call(bf16[128,128]{1,0:T(8,128)(2,1)S(1)} %copy-done.24, bf16[128,128]{1,0:T(8,128)(2,1)S(1)} %collective-permute-done.refs_1_, bf16[32,128,128]{2,1,0:T(8,128)(2,1)S(1)} %all-to-all-done.refs_2_, ...), custom_call_target="tpu_custom_call" | custom-call | flops 1100000000 | tf_op jit(solution)/shard_map/reverse/pallas_call | solution.py:90
  164.5 4.0 %all-to-all-start.3 = ((bf16[32,128,128]{2,1,0:T(8,128)(2,1)}), bf16[32,128,128]{2,1,0:T(8,128)(2,1)S(1)}, u32[]{:S(2)}, u32[]{:S(2)}) async-start(bf16[32,128,128]{2,1,0:T(8,128)(2,1)} %get-tuple-element.136), calls=%async_computation.3 | async-start | bytes 2097152 | tf_op jit(solution)/shard_map/all_to_all | solution.py:30
  168.5 1.9 collective-permute-start.17
  170.3 1.4 pad.4.refs_10_
  171.7 8.3 %collective-permute-done.17.refs_8_ = bf16[128,128]{1,0:T(8,128)(2,1)S(1)} collective-permute-done((bf16[128,128]{1,0:T(8,128)(2,1)S(1)}, bf16[128,128]{1,0:T(8,128)(2,1)S(1)}, u32[]{:S(2)}, u32[]{:S(2)}) %collective-permute-start.17) | collective-permute-done | bytes 32800 | tf_op jit(solution)/shard_map/ppermute | solution.py:790
  180.1 8.0 %all-to-all-done.3.refs_0_ = bf16[32,128,128]{2,1,0:T(8,128)(2,1)S(1)} async-done(((bf16[32,128,128]{2,1,0:T(8,128)(2,1)}), bf16[32,128,128]{2,1,0:T(8,128)(2,1)S(1)}, u32[]{:S(2)}, u32[]{:S(2)}) %all-to-all-start.3) | async-done | bytes 1048608 | tf_op jit(solution)/shard_map/all_to_all | solution.py:30
  188.0 1.0 copy-done.38
  189.0 5.2 %late.1 = (bf16[32,112,256]{2,1,0:T(8,128)(2,1)}, bf16[80,1024]{1,0:T(8,128)(2,1)}, bf16[80,1024]{1,0:T(8,128)(2,1)}) custom-call(bf16[32,128,128]{2,1,0:T(8,128)(2,1)} %copy-done.38, f32[128,128]{1,0:T(8,128)} %get-tuple-element.183.refs_5_.refs_1_, f32[128,128]{1,0:T(8,128)} %get-tuple-element.184.refs_6_.refs_2_, ...), custom_call_target="tpu_custom_call", output_to_operand_aliasing={{0}: (10, {})} | custom-call | flops 2200000000 | tf_op jit(solution)/shard_map/late/pallas_call | solution.py:90
  194.2 4.2 %all-to-all-start.4 = ((bf16[32,112,256]{2,1,0:T(8,128)(2,1)}), bf16[32,112,256]{2,1,0:T(8,128)(2,1)S(1)}, u32[]{:S(2)}, u32[]{:S(2)}) async-start(bf16[32,112,256]{2,1,0:T(8,128)(2,1)} %get-tuple-element.144), calls=%async_computation.4 | async-start | bytes 3670016 | tf_op jit(solution)/shard_map/all_to_all | solution.py:30
  198.7 1.2 collective-permute-done.18
  200.0 0.8 collective-permute-start.19
  200.8 20.8 %collective-permute-done.19 = bf16[80,1024]{1,0:T(8,128)(2,1)S(1)} collective-permute-done((bf16[80,1024]{1,0:T(8,128)(2,1)S(1)}, bf16[80,1024]{1,0:T(8,128)(2,1)S(1)}, u32[]{:S(2)}, u32[]{:S(2)}) %collective-permute-start.19) | collective-permute-done | bytes 163872 | tf_op jit(solution)/shard_map/ppermute | solution.py:592
  221.6 5.6 %all-to-all-done.4.refs_0_ = bf16[32,112,256]{2,1,0:T(8,128)(2,1)S(1)} async-done(((bf16[32,112,256]{2,1,0:T(8,128)(2,1)}), bf16[32,112,256]{2,1,0:T(8,128)(2,1)S(1)}, u32[]{:S(2)}, u32[]{:S(2)}) %all-to-all-start.4) | async-done | bytes 1835040 | tf_op jit(solution)/shard_map/all_to_all | solution.py:30
  227.2 0.9 share.1
  228.2 1.2 copy-done.5
  229.4 4.8 %all-to-all-start.5 = ((bf16[32,112,256]{2,1,0:T(8,128)(2,1)}), bf16[32,112,256]{2,1,0:T(8,128)(2,1)S(1)}, u32[]{:S(2)}, u32[]{:S(2)}) async-start(bf16[32,112,256]{2,1,0:T(8,128)(2,1)} %copy-done.5), calls=%async_computation.5 | async-start | bytes 3670016 | tf_op jit(solution)/shard_map/all_to_all | solution.py:30
  234.2 1.5 fusion
  235.9 2.2 fusion.13
  238.8 0.9 fusion.10
  239.7 18.5 %collective-permute-done.21 = bf16[1024,128]{1,0:T(8,128)(2,1)S(1)} collective-permute-done((bf16[1024,128]{1,0:T(8,128)(2,1)S(1)}, bf16[1024,128]{1,0:T(8,128)(2,1)S(1)}, u32[]{:S(2)}, u32[]{:S(2)}) %collective-permute-start.21) | collective-permute-done | bytes 262176 | tf_op jit(solution)/shard_map/ppermute | solution.py:826
  258.3 0.8 copy.37
  259.1 3.3 %all-to-all-done.5.refs_0_ = bf16[32,112,256]{2,1,0:T(8,128)(2,1)S(1)} async-done(((bf16[32,112,256]{2,1,0:T(8,128)(2,1)}), bf16[32,112,256]{2,1,0:T(8,128)(2,1)S(1)}, u32[]{:S(2)}, u32[]{:S(2)}) %all-to-all-start.5) | async-done | bytes 1835040 | tf_op jit(solution)/shard_map/all_to_all | solution.py:30
  262.5 1.8 final.1
  (135 shorter events, 5.6 us)
Async XLA Ops:
  7.2 11.1 %copy-start.46 = (bf16[128,128]{1,0:T(8,128)(2,1)S(1)}, bf16[128,128]{1,0:T(8,128)(2,1)}, u32[]{:S(2)}) copy-start(bf16[128,128]{1,0:T(8,128)(2,1)} %get-tuple-element.93) | copy-start | bytes 98308
  7.2 13.0 %copy-start.39 = (bf16[1,128,1024]{2,1,0:T(8,128)(2,1)S(1)}, bf16[1,128,1024]{2,1,0:T(8,128)(2,1)}, u32[]{:S(2)}) copy-start(bf16[1,128,1024]{2,1,0:T(8,128)(2,1)} %param.23) | copy-start | bytes 786436
  7.2 13.7 %copy-start.44 = (s32[128,8]{0,1:T(8,128)S(1)}, s32[128,8]{0,1:T(8,128)}, u32[]{:S(2)}) copy-start(s32[128,8]{0,1:T(8,128)} %param.24) | copy-start | bytes 12292
  7.2 13.9 %copy-start.40 = (bf16[1,1024,128]{2,1,0:T(8,128)(2,1)S(1)}, bf16[1,1024,128]{2,1,0:T(8,128)(2,1)}, u32[]{:S(2)}) copy-start(bf16[1,1024,128]{2,1,0:T(8,128)(2,1)} %param.22) | copy-start | bytes 786436
  7.2 13.9 %copy-start.41 = (bf16[1,1024,128]{2,1,0:T(8,128)(2,1)S(1)}, bf16[1,1024,128]{2,1,0:T(8,128)(2,1)}, u32[]{:S(2)}) copy-start(bf16[1,1024,128]{2,1,0:T(8,128)(2,1)} %param.21) | copy-start | bytes 786436
  7.2 32.4 %copy-start.23 = (bf16[128,128]{1,0:T(8,128)(2,1)S(1)}, bf16[128,128]{1,0:T(8,128)(2,1)}, u32[]{:S(2)}) copy-start(bf16[128,128]{1,0:T(8,128)(2,1)} %get-tuple-element.91.refs_0_) | copy-start | bytes 98308
  7.2 31.8 %all-to-all-start = ((bf16[32,128,128]{2,1,0:T(8,128)(2,1)}), bf16[32,128,128]{2,1,0:T(8,128)(2,1)S(1)}, u32[]{:S(2)}, u32[]{:S(2)}) async-start(bf16[32,128,128]{2,1,0:T(8,128)(2,1)} %get-tuple-element.92), calls=%async_computation | async-start | bytes 2097152 | tf_op jit(solution)/shard_map/all_to_all | solution.py:30
  18.3 11.5 %collective-permute-start = (bf16[128,128]{1,0:T(8,128)(2,1)S(1)}, bf16[128,128]{1,0:T(8,128)(2,1)S(1)}, u32[]{:S(2)}, u32[]{:S(2)}) collective-permute-start(bf16[128,128]{1,0:T(8,128)(2,1)S(1)} %copy-done.46), channel_id=1, source_target_pairs={{0,8},{4,12},{8,0},{12,4},{16,24},{20,28},{24,16},{28,20},{32,40},... | collective-permute-start | bytes 98312 | tf_op jit(solution)/shard_map/ppermute | solution.py:649
  20.2 28.9 %copy-start.16 = (bf16[256,1024]{1,0:T(8,128)(2,1)S(1)}, bf16[256,1024]{1,0:T(8,128)(2,1)}, u32[]{:S(2)}) copy-start(bf16[256,1024]{1,0:T(8,128)(2,1)} %refs_10_.1) | copy-start | bytes 1572868
  20.2 15.8 %collective-permute-start.1 = (bf16[1024,128]{1,0:T(8,128)(2,1)S(1)}, bf16[1024,128]{1,0:T(8,128)(2,1)S(1)}, u32[]{:S(2)}, u32[]{:S(2)}) collective-permute-start(bf16[1024,128]{1,0:T(8,128)(2,1)S(1)} %bitcast.65), channel_id=1, source_target_pairs={{0,2},{2,0},{1,3},{3,1},{4,6},{6,4},{5,7},{7,5},{8,10},{10,8},{9,1... | collective-permute-start | bytes 786440 | tf_op jit(solution)/shard_map/ppermute | solution.py:662
  39.1 10.7 %collective-permute-start.3 = (bf16[2,1024,128]{2,1,0:T(8,128)(2,1)S(1)}, bf16[2,1024,128]{2,1,0:T(8,128)(2,1)S(1)}, u32[]{:S(2)}, u32[]{:S(2)}) collective-permute-start(bf16[2,1024,128]{2,1,0:T(8,128)(2,1)S(1)} %pad_maximum_fusion.refs_1_), channel_id=1, source_target_pairs={{0,2},{2,0},{1,3},{3,1},{4,6},{6,4},{5,7},{7,5},{8,10},{10,8},{9,1... | collective-permute-start | bytes 1572872 | tf_op jit(solution)/shard_map/ppermute | solution.py:602
  45.1 3.9 %collective-permute-start.2 = (bf16[128,128]{1,0:T(8,128)(2,1)S(1)}, bf16[128,128]{1,0:T(8,128)(2,1)S(1)}, u32[]{:S(2)}, u32[]{:S(2)}) collective-permute-start(bf16[128,128]{1,0:T(8,128)(2,1)S(1)} %get-tuple-element.97), channel_id=1, source_target_pairs={{0,8},{4,12},{8,0},{12,4},{16,24},{20,28},{24,16},{28,20},{32,40},... | collective-permute-start | bytes 98312 | tf_op jit(solution)/shard_map/ppermute | solution.py:682
  49.1 9.2 %copy-start = (bf16[128,1024]{1,0:T(8,128)(2,1)S(1)}, bf16[128,1024]{1,0:T(8,128)(2,1)}, u32[]{:S(2)}) copy-start(bf16[128,1024]{1,0:T(8,128)(2,1)} %refs_9_.1) | copy-start | bytes 786436
  49.1 9.2 %copy-start.18 = (bf16[1024,32]{0,1:T(8,128)(2,1)S(1)}, bf16[1024,32]{0,1:T(8,128)(2,1)}, u32[]{:S(2)}) copy-start(bf16[1024,32]{0,1:T(8,128)(2,1)} %param.20) | copy-start | bytes 196612
  49.1 9.2 %copy-start.20 = (f32[1024]{0:T(1024)S(1)}, f32[1024]{0:T(1024)}, u32[]{:S(2)}) copy-start(f32[1024]{0:T(1024)} %param.19) | copy-start | bytes 12292
  49.4 8.9 %copy-start.34 = (bf16[256,128]{1,0:T(8,128)(2,1)}, bf16[256,128]{1,0:T(8,128)(2,1)S(1)}, u32[]{:S(2)}) copy-start(bf16[256,128]{1,0:T(8,128)(2,1)S(1)} %get-tuple-element.129.refs_11_) | copy-start | bytes 196612
  49.8 1.3 collective-permute-start.4
  51.2 5.6 %collective-permute-start.5 = (bf16[64,1024]{1,0:T(8,128)(2,1)S(1)}, bf16[64,1024]{1,0:T(8,128)(2,1)S(1)}, u32[]{:S(2)}, u32[]{:S(2)}) collective-permute-start(bf16[64,1024]{1,0:T(8,128)(2,1)S(1)} %add_convert_fusion.3), channel_id=1, source_target_pairs={{0,2},{2,0},{1,3},{3,1},{4,6},{6,4},{5,7},{7,5},{8,10},{10,8},{9,1... | collective-permute-start | bytes 393224 | tf_op jit(solution)/shard_map/ppermute | solution.py:592
  52.4 7.1 %collective-permute-start.7 = (bf16[2,1024,128]{2,1,0:T(8,128)(2,1)S(1)}, bf16[2,1024,128]{2,1,0:T(8,128)(2,1)S(1)}, u32[]{:S(2)}, u32[]{:S(2)}) collective-permute-start(bf16[2,1024,128]{2,1,0:T(8,128)(2,1)S(1)} %pad_maximum_fusion.refs_1_), channel_id=1, source_target_pairs={{0,1},{1,0},{2,3},{3,2},{4,5},{5,4},{6,7},{7,6},{8,9},{9,8},{10,11... | collective-permute-start | bytes 1572872 | tf_op jit(solution)/shard_map/ppermute | solution.py:603
  52.4 7.1 %collective-permute-start.8 = (bf16[2,1024,128]{2,1,0:T(8,128)(2,1)S(1)}, bf16[2,1024,128]{2,1,0:T(8,128)(2,1)S(1)}, u32[]{:S(2)}, u32[]{:S(2)}) collective-permute-start(bf16[2,1024,128]{2,1,0:T(8,128)(2,1)S(1)} %collective-permute-done.3.refs_2_), channel_id=1, source_target_pairs={{0,1},{1,0},{2,3},{3,2},{4,5},{5,4},{6,7},{7,6},{8,9},{9,8},{10,11... | collective-permute-start | bytes 1572872 | tf_op jit(solution)/shard_map/ppermute | solution.py:604
  56.8 1.4 collective-permute-start.6
  56.9 2.5 collective-permute-start.9
  57.4 2.0 collective-permute-start.10
  59.4 39.6 %copy-start.25 = (f32[128,1024]{1,0:T(8,128)}, f32[128,1024]{1,0:T(8,128)S(1)}, u32[]{:S(2)}) copy-start(f32[128,1024]{1,0:T(8,128)S(1)} %get-tuple-element.127.refs_5_) | copy-start | bytes 1572868
  59.4 39.6 %copy-start.29 = (bf16[128,1024]{1,0:T(8,128)(2,1)}, bf16[128,1024]{1,0:T(8,128)(2,1)S(1)}, u32[]{:S(2)}) copy-start(bf16[128,1024]{1,0:T(8,128)(2,1)S(1)} %get-tuple-element.128.refs_6_) | copy-start | bytes 786436
  59.4 39.5 %copy-start.31 = (f32[64,128]{1,0:T(8,128)}, f32[64,128]{1,0:T(8,128)S(1)}, u32[]{:S(2)}) copy-start(f32[64,128]{1,0:T(8,128)S(1)} %get-tuple-element.121.refs_1_.refs_4_) | copy-start | bytes 98308
  99.0 4.2 %copy-start.2 = (bf16[128,16,512]{2,1,0:T(8,128)(2,1)}, bf16[128,16,512]{2,1,0:T(8,128)(2,1)S(1)}, u32[]{:S(2)}) copy-start(bf16[128,16,512]{2,1,0:T(8,128)(2,1)S(1)} %all_to_all.30) | copy-start | bytes 6291460
  105.7 35.0 %all-to-all-start.2 = ((bf16[128,16,512]{2,1,0:T(8,128)(2,1)}), bf16[128,16,512]{2,1,0:T(8,128)(2,1)S(1)}, u32[]{:S(2)}, u32[]{:S(2)}) async-start(bf16[128,16,512]{2,1,0:T(8,128)(2,1)} %bitcast.63), calls=%async_computation.2 | async-start | bytes 4194304 | tf_op jit(solution)/shard_map/all_to_all | solution.py:30
  110.3 1.6 copy-start.3
  140.7 8.0 %collective-permute-start.14 = (bf16[2,3,1024,128]{3,2,1,0:T(8,128)(2,1)}, bf16[2,3,1024,128]{3,2,1,0:T(8,128)(2,1)S(1)}, u32[]{:S(2)}, u32[]{:S(2)}) collective-permute-start(bf16[2,3,1024,128]{3,2,1,0:T(8,128)(2,1)} %copy-done.15), channel_id=1, source_target_pairs={{0,1},{1,0},{2,3},{3,2},{4,5},{5,4},{6,7},{7,6},{8,9},{9,8},{10,11... | collective-permute-start | bytes 4718600 | tf_op jit(solution)/shard_map/ppermute | solution.py:737
  142.6 6.4 %copy-start.11 = (bf16[2,1024,128]{2,1,0:T(8,128)(2,1)S(1)}, bf16[2,1024,128]{2,1,0:T(8,128)(2,1)}, u32[]{:S(2)}) copy-start(bf16[2,1024,128]{2,1,0:T(8,128)(2,1)} %copy-done.10) | copy-start | bytes 1572868
  142.6 6.2 %collective-permute-start.11 = (bf16[272,256]{1,0:T(8,128)(2,1)S(1)}, bf16[272,256]{1,0:T(8,128)(2,1)S(1)}, u32[]{:S(2)}, u32[]{:S(2)}) collective-permute-start(bf16[272,256]{1,0:T(8,128)(2,1)S(1)} %combine.1.refs_0_), channel_id=1, source_target_pairs={{0,2},{2,0},{1,3},{3,1},{4,6},{6,4},{5,7},{7,5},{8,10},{10,8},{9,1... | collective-permute-start | bytes 417800 | tf_op jit(solution)/shard_map/ppermute | solution.py:602
  143.2 5.9 %collective-permute-start.12 = (bf16[272,256]{1,0:T(8,128)(2,1)S(1)}, bf16[272,256]{1,0:T(8,128)(2,1)S(1)}, u32[]{:S(2)}, u32[]{:S(2)}) collective-permute-start(bf16[272,256]{1,0:T(8,128)(2,1)S(1)} %combine.1.refs_0_), channel_id=1, source_target_pairs={{0,1},{1,0},{2,3},{3,2},{4,5},{5,4},{6,7},{7,6},{8,9},{9,8},{10,11... | collective-permute-start | bytes 417800 | tf_op jit(solution)/shard_map/ppermute | solution.py:603
  148.7 1.4 collective-permute-start.13
  149.0 5.2 %copy-start.37 = (f32[2,3,1024,128]{3,2,1,0:T(8,128)}, f32[2,3,1024,128]{3,2,1,0:T(8,128)S(1)}, u32[]{:S(2)}) copy-start(f32[2,3,1024,128]{3,2,1,0:T(8,128)S(1)} %convert_element_type.103) | copy-start | bytes 9437188
  149.0 1.7 copy-start.12
  149.0 1.7 copy-start.17
  149.0 1.7 copy-start.19
  149.0 2.3 copy-start.26
  149.0 2.5 copy-start.30
  149.0 2.4 copy-start.33
  149.1 2.4 copy-start.35
  150.1 14.4 %collective-permute-start.16 = (bf16[2,1024,128]{2,1,0:T(8,128)(2,1)S(1)}, bf16[2,1024,128]{2,1,0:T(8,128)(2,1)}, u32[]{:S(2)}, u32[]{:S(2)}) collective-permute-start(bf16[2,1024,128]{2,1,0:T(8,128)(2,1)S(1)} %fusion.3), channel_id=1, source_target_pairs={{0,2},{2,0},{1,3},{3,1},{4,6},{6,4},{5,7},{7,5},{8,10},{10,8},{9,1... | collective-permute-start | bytes 1572872 | tf_op jit(solution)/shard_map/ppermute | solution.py:753
  151.5 6.5 %copy-start.13 = (f32[32,128]{1,0:T(8,128)S(1)}, f32[32,128]{1,0:T(8,128)}, u32[]{:S(2)}) copy-start(f32[32,128]{1,0:T(8,128)} %get-tuple-element.181.refs_7_.refs_6_) | copy-start | bytes 49156
  151.5 6.5 %copy-start.14 = (f32[32,128]{1,0:T(8,128)S(1)}, f32[32,128]{1,0:T(8,128)}, u32[]{:S(2)}) copy-start(f32[32,128]{1,0:T(8,128)} %get-tuple-element.182.refs_8_.refs_7_) | copy-start | bytes 49156
  151.5 6.5 %copy-start.22 = (f32[72,512]{1,0:T(8,128)S(1)}, f32[72,512]{1,0:T(8,128)}, u32[]{:S(2)}) copy-start(f32[72,512]{1,0:T(8,128)} %copy-done.21) | copy-start | bytes 442372
  151.5 6.5 %copy-start.24 = (bf16[128,128]{1,0:T(8,128)(2,1)S(1)}, bf16[128,128]{1,0:T(8,128)(2,1)}, u32[]{:S(2)}) copy-start(bf16[128,128]{1,0:T(8,128)(2,1)} %get-tuple-element.91.refs_0_) | copy-start | bytes 98308
  154.1 3.9 %collective-permute-start.15 = (bf16[128,128]{1,0:T(8,128)(2,1)S(1)}, bf16[128,128]{1,0:T(8,128)(2,1)S(1)}, u32[]{:S(2)}, u32[]{:S(2)}) collective-permute-start(bf16[128,128]{1,0:T(8,128)(2,1)S(1)} %get-tuple-element.131), channel_id=1, source_target_pairs={{0,8},{4,12},{8,0},{12,4},{16,24},{20,28},{24,16},{28,20},{32,40},... | collective-permute-start | bytes 98312 | tf_op jit(solution)/shard_map/ppermute | solution.py:768
  164.5 7.2 %copy-start.36 = (bf16[128,128]{1,0:T(8,128)(2,1)}, bf16[128,128]{1,0:T(8,128)(2,1)S(1)}, u32[]{:S(2)}) copy-start(bf16[128,128]{1,0:T(8,128)(2,1)S(1)} %get-tuple-element.141.refs_7_) | copy-start | bytes 98308
  164.5 23.5 %all-to-all-start.3 = ((bf16[32,128,128]{2,1,0:T(8,128)(2,1)}), bf16[32,128,128]{2,1,0:T(8,128)(2,1)S(1)}, u32[]{:S(2)}, u32[]{:S(2)}) async-start(bf16[32,128,128]{2,1,0:T(8,128)(2,1)} %get-tuple-element.136), calls=%async_computation.3 | async-start | bytes 2097152 | tf_op jit(solution)/shard_map/all_to_all | solution.py:30
  168.5 11.6 %collective-permute-start.17 = (bf16[128,128]{1,0:T(8,128)(2,1)S(1)}, bf16[128,128]{1,0:T(8,128)(2,1)S(1)}, u32[]{:S(2)}, u32[]{:S(2)}) collective-permute-start(bf16[128,128]{1,0:T(8,128)(2,1)S(1)} %get-tuple-element.138), channel_id=1, source_target_pairs={{0,8},{4,12},{8,0},{12,4},{16,24},{20,28},{24,16},{28,20},{32,40},... | collective-permute-start | bytes 98312 | tf_op jit(solution)/shard_map/ppermute | solution.py:790
  180.1 8.0 %copy-start.47 = (bf16[128,128]{1,0:T(8,128)(2,1)}, bf16[128,128]{1,0:T(8,128)(2,1)S(1)}, u32[]{:S(2)}) copy-start(bf16[128,128]{1,0:T(8,128)(2,1)S(1)} %collective-permute-done.17.refs_8_) | copy-start | bytes 98308
  194.2 4.3 %copy-start.45 = (bf16[80,1024]{1,0:T(8,128)(2,1)S(1)}, bf16[80,1024]{1,0:T(8,128)(2,1)}, u32[]{:S(2)}) copy-start(bf16[80,1024]{1,0:T(8,128)(2,1)} %get-tuple-element.146) | copy-start | bytes 491524
  194.2 4.4 %copy-start.1 = (bf16[128,1024]{1,0:T(8,128)(2,1)S(1)}, bf16[128,1024]{1,0:T(8,128)(2,1)}, u32[]{:S(2)}) copy-start(bf16[128,1024]{1,0:T(8,128)(2,1)} %refs_9_.1) | copy-start | bytes 786436
  194.2 5.8 %copy-start.42 = (bf16[80,1024]{1,0:T(8,128)(2,1)S(1)}, bf16[80,1024]{1,0:T(8,128)(2,1)}, u32[]{:S(2)}) copy-start(bf16[80,1024]{1,0:T(8,128)(2,1)} %get-tuple-element.145) | copy-start | bytes 491524
  194.2 32.9 %all-to-all-start.4 = ((bf16[32,112,256]{2,1,0:T(8,128)(2,1)}), bf16[32,112,256]{2,1,0:T(8,128)(2,1)S(1)}, u32[]{:S(2)}, u32[]{:S(2)}) async-start(bf16[32,112,256]{2,1,0:T(8,128)(2,1)} %get-tuple-element.144), calls=%async_computation.4 | async-start | bytes 3670016 | tf_op jit(solution)/shard_map/all_to_all | solution.py:30
  198.5 1.5 collective-permute-start.18
  200.0 21.6 %collective-permute-start.19 = (bf16[80,1024]{1,0:T(8,128)(2,1)S(1)}, bf16[80,1024]{1,0:T(8,128)(2,1)S(1)}, u32[]{:S(2)}, u32[]{:S(2)}) collective-permute-start(bf16[80,1024]{1,0:T(8,128)(2,1)S(1)} %add_convert_fusion.1), channel_id=1, source_target_pairs={{0,2},{2,0},{1,3},{3,1},{4,6},{6,4},{5,7},{7,5},{8,10},{10,8},{9,1... | collective-permute-start | bytes 491528 | tf_op jit(solution)/shard_map/ppermute | solution.py:592
  229.4 4.8 %copy-start.7 = (bf16[3,1024,128]{2,1,0:T(8,128)(2,1)S(1)}, bf16[3,1024,128]{2,1,0:T(8,128)(2,1)}, u32[]{:S(2)}) copy-start(bf16[3,1024,128]{2,1,0:T(8,128)(2,1)} %copy-done.6) | copy-start | bytes 2359300
  229.4 33.1 %all-to-all-start.5 = ((bf16[32,112,256]{2,1,0:T(8,128)(2,1)}), bf16[32,112,256]{2,1,0:T(8,128)(2,1)S(1)}, u32[]{:S(2)}, u32[]{:S(2)}) async-start(bf16[32,112,256]{2,1,0:T(8,128)(2,1)} %copy-done.5), calls=%async_computation.5 | async-start | bytes 3670016 | tf_op jit(solution)/shard_map/all_to_all | solution.py:30
  235.8 2.7 %copy-start.43 = (f32[1024]{0:T(1024)S(1)}, f32[1024]{0:T(1024)}, u32[]{:S(2)}) copy-start(f32[1024]{0:T(1024)} %param.14) | copy-start | bytes 12292
  235.8 2.9 %copy-start.9 = (f32[128,1024]{1,0:T(8,128)S(1)}, f32[128,1024]{1,0:T(8,128)}, u32[]{:S(2)}) copy-start(f32[128,1024]{1,0:T(8,128)} %copy-done.8) | copy-start | bytes 1572868
  235.8 2.7 %collective-permute-start.20 = (bf16[64,1024]{1,0:T(8,128)(2,1)S(1)}, bf16[64,1024]{1,0:T(8,128)(2,1)S(1)}, u32[]{:S(2)}, u32[]{:S(2)}) collective-permute-start(bf16[64,1024]{1,0:T(8,128)(2,1)S(1)} %get-tuple-element.173), channel_id=1, source_target_pairs={{0,1},{1,0},{2,3},{3,2},{4,5},{5,4},{6,7},{7,6},{8,9},{9,8},{10,11... | collective-permute-start | bytes 393224 | tf_op jit(solution)/shard_map/ppermute | solution.py:829
  238.1 20.2 %collective-permute-start.21 = (bf16[1024,128]{1,0:T(8,128)(2,1)S(1)}, bf16[1024,128]{1,0:T(8,128)(2,1)S(1)}, u32[]{:S(2)}, u32[]{:S(2)}) collective-permute-start(bf16[1024,128]{1,0:T(8,128)(2,1)S(1)} %fusion.16), channel_id=1, source_target_pairs={{0,2},{2,0},{1,3},{3,1},{4,6},{6,4},{5,7},{7,5},{8,10},{10,8},{9,1... | collective-permute-start | bytes 786440 | tf_op jit(solution)/shard_map/ppermute | solution.py:826
  (11 other events, 11.1 us)

commit v5 on v4

--- a/solution.py
+++ b/solution.py
@@ -150,7 +150,7 @@
 
 
 def prelude_kernel(
-    tokens_ref, gain_ref, wq_ref, wk_ref, wv_ref, cos_ref, sin_ref, cos_t_ref, sin_t_ref,
+    tokens_ref, gain_ref, wq_ref, wk_ref, wv_ref, cos_t_ref, sin_t_ref,
     kv_ref, normed_ref, q_ref, q_give_ref, *, send, ready
 ):
     _, side, _, _ = places()
@@ -170,7 +170,10 @@
         jnp.where(low, k, swap_halves(v)),
         jnp.where(low, swap_halves(k), v),
     )
-    heads = [turn_lanes(y, cos_ref[...], sin_ref[...]).astype(bf16) for y in heads]
+    cosine, sine = cos_t_ref[...], sin_t_ref[...]
+    cos_lanes = jnp.concatenate([cosine, cosine, jnp.ones((64, 128), f32)], 0).T
+    sin_lanes = jnp.concatenate([-sine, sine, jnp.zeros((64, 128), f32)], 0).T
+    heads = [turn_lanes(y, cos_lanes, sin_lanes).astype(bf16) for y in heads]
     for d in range(32):
         kv_ref[d] = heads[(d >> 1) & 1]
     send(0)
@@ -565,7 +568,7 @@
     for q in range(4):
         here = slice(256 * q, 256 * q + 256)
         gain2_ref[:, here] = total_ref[68 + q : 69 + q, :]
-        total_ref[72 + q : 73 + q, :] = gain_ref[0:1, here].astype(f32)
+        total_ref[72 + q : 73 + q, :] = gain_ref[:, here].astype(f32)[0:1]
     out_ref[...] = jnp.broadcast_to(total_ref[...].astype(bf16)[None], (32, 112, 256))
 
 
@@ -634,7 +637,7 @@
     kv_send, normed1, q_own, q_give = on_device(
         prelude_kernel,
         "prelude",
-        "FFFFFVVVV",
+        "FFFFFVV",
         (
             ("S", shape((32, rows, 128))),
             ("S", shape((rows, width))),
@@ -644,7 +647,7 @@
         megabytes=56,
         us=2,
         lazy=True,
-    )(tokens, gain1, w_query, key_weight, value_weight, cos_lanes, sin_lanes, cos_rows, sin_rows)
+    )(tokens, gain1, w_query, key_weight, value_weight, cos_rows, sin_rows)
     kv = exchange(kv_send, "ctx")
     q_other = lax.ppermute(q_give, "ctx", PARTNER)
 

time: 265 us -> 265 us (level)
    unnamed x97 -> x101, local copies, waits for them, and re-layouts: 13.7 us -> 14.5 us
  transfers between devices with their start and end apart: 27 -> 27, of which waited for: 19 -> 19; matrix products, arithmetic and copies ran while one was open for 3% -> 4% of each run, Pallas kernels for 7% -> 7%
where the time goes in v5:
time: 265 us; the launch traced here: 264 us
  waiting for transfers between devices  123 us (46%)
  blocking collectives  39.5 us (15%)
  starting transfers between devices  39.1 us (15%)
  Pallas kernels  33.7 us (13%)
  local copies, waits for them, and re-layouts  17.7 us (7%)
  other arithmetic  8.87 us (3%)
    all_to_all x5, waiting for transfers between devices, exchange(): return lax.all_to_all(value, axes, split_axis=0, concat_axis=0, tiled=True)  42.7 us
    all_to_all x1, blocking collectives, exchange(): return lax.all_to_all(value, axes, split_axis=0, concat_axis=0, tiled=True)  39.5 us
    pallas_call x12, Pallas kernels, call(): pl.pallas_call(body, out_shape=tuple((o for _, o in outs)), in_specs=[pl....  33.7 us
    all_to_all x5, starting transfers between devices, exchange(): return lax.all_to_all(value, axes, split_axis=0, concat_axis=0, tiled=True)  28.9 us
    ppermute x2, waiting for transfers between devices, pair_over_wa(): return (pair, lax.ppermute(pair, 'wa', CHIP_SWAP))  25.1 us
    ppermute x1, waiting for transfers between devices, local(): near_last = lax.ppermute(near_last, 'wa', CHIP_SWAP)  19.3 us
    unnamed x101, local copies, waits for them, and re-layouts  14.5 us
    ppermute x1, waiting for transfers between devices, local(): q_other = lax.ppermute(q_give, 'ctx', PARTNER)  6.79 us
  transfers between devices with their start and end apart: 27, of which 19 were waited for; matrix products, arithmetic and copies ran while one was open for 4% of the time, Pallas kernels for 7%

profile of v5, /device:TPU:0, one launch (start us, length us, event | category | flops | bytes accessed | tf_op | source)
XLA Modules:
  0.0 264.1 jit_solution(2205110134938252426)
XLA Ops:
  0.7 0.8 multiply_sine_fusion.1
  1.5 4.3 %prelude.1 = (bf16[32,128,128]{2,1,0:T(8,128)(2,1)}, bf16[128,1024]{1,0:T(8,128)(2,1)}, bf16[128,128]{1,0:T(8,128)(2,1)}, bf16[128,128]{1,0:T(8,128)(2,1)}) custom-call(bf16[128,1024]{1,0:T(8,128)(2,1)} %refs_9_.1, f32[1,1024]{1,0:T(1,128)} %bitcast.79, bf16[1024,256]{1,0:T(8,128)(2,1)} %refs_6_.1, bf16[1024,128]{1,0:T(8,128)(2,1)} %refs_4_.3, ...), custom_call_target="tpu_custom_call" | custom-call | flops 2200000000 | tf_op jit(solution)/shard_map/prelude/pallas_call | solution.py:90
  5.8 11.0 %all-to-all-start = ((bf16[32,128,128]{2,1,0:T(8,128)(2,1)}), bf16[32,128,128]{2,1,0:T(8,128)(2,1)S(1)}, u32[]{:S(2)}, u32[]{:S(2)}) async-start(bf16[32,128,128]{2,1,0:T(8,128)(2,1)} %get-tuple-element.92), calls=%async_computation | async-start | bytes 2097152 | tf_op jit(solution)/shard_map/all_to_all | solution.py:30
  16.9 1.9 collective-permute-start
  18.9 0.7 collective-permute-start.1
  19.7 1.0 pad_maximum_fusion.refs_1_
  20.7 0.9 constant_dynamic-slice_fusion.refs_6_.refs_2_
  21.6 6.8 %collective-permute-done.refs_1_ = bf16[128,128]{1,0:T(8,128)(2,1)S(1)} collective-permute-done((bf16[128,128]{1,0:T(8,128)(2,1)S(1)}, bf16[128,128]{1,0:T(8,128)(2,1)S(1)}, u32[]{:S(2)}, u32[]{:S(2)}) %collective-permute-start) | collective-permute-done | bytes 32800 | tf_op jit(solution)/shard_map/ppermute | solution.py:652
  28.4 6.3 %collective-permute-done.1.refs_6_ = bf16[1024,128]{1,0:T(8,128)(2,1)S(1)} collective-permute-done((bf16[1024,128]{1,0:T(8,128)(2,1)S(1)}, bf16[1024,128]{1,0:T(8,128)(2,1)S(1)}, u32[]{:S(2)}, u32[]{:S(2)}) %collective-permute-start.1) | collective-permute-done | bytes 262176 | tf_op jit(solution)/shard_map/ppermute | solution.py:665
  34.7 3.0 %all-to-all-done.refs_2_ = bf16[32,128,128]{2,1,0:T(8,128)(2,1)S(1)} async-done(((bf16[32,128,128]{2,1,0:T(8,128)(2,1)}), bf16[32,128,128]{2,1,0:T(8,128)(2,1)S(1)}, u32[]{:S(2)}, u32[]{:S(2)}) %all-to-all-start) | async-done | bytes 1048608 | tf_op jit(solution)/shard_map/all_to_all | solution.py:30
  38.3 4.8 %attend.1 = (bf16[128,128]{1,0:T(8,128)(2,1)S(1)}, bf16[128,128]{1,0:T(8,128)(2,1)S(1)}, f32[72,512]{1,0:T(8,128)S(1)}) custom-call(bf16[128,128]{1,0:T(8,128)(2,1)S(1)} %copy-done.23, bf16[128,128]{1,0:T(8,128)(2,1)S(1)} %collective-permute-done.refs_1_, bf16[32,128,128]{2,1,0:T(8,128)(2,1)S(1)} %all-to-all-done.refs_2_), custom_call_target="tpu_custom_call" | custom-call | flops 550000000 | tf_op jit(solution)/shard_map/attend/pallas_call | solution.py:90
  43.8 3.3 %collective-permute-done.2.refs_1_ = bf16[128,128]{1,0:T(8,128)(2,1)S(1)} collective-permute-done((bf16[128,128]{1,0:T(8,128)(2,1)S(1)}, bf16[128,128]{1,0:T(8,128)(2,1)S(1)}, u32[]{:S(2)}, u32[]{:S(2)}) %collective-permute-start.2) | collective-permute-done | bytes 32800 | tf_op jit(solution)/shard_map/ppermute | solution.py:685
  47.4 0.9 collective-permute-done.3.refs_2_
  48.4 1.3 collective-permute-done.4
  49.8 0.7 collective-permute-start.5
  51.0 4.4 %collective-permute-done.5 = bf16[64,1024]{1,0:T(8,128)(2,1)S(1)} collective-permute-done((bf16[64,1024]{1,0:T(8,128)(2,1)S(1)}, bf16[64,1024]{1,0:T(8,128)(2,1)S(1)}, u32[]{:S(2)}, u32[]{:S(2)}) %collective-permute-start.5) | collective-permute-done | bytes 131104 | tf_op jit(solution)/shard_map/ppermute | solution.py:595
  56.1 0.7 collective-permute-done.6.refs_2_
  56.9 1.1 route.1
  58.1 39.5 %all_to_all.30 = bf16[128,16,512]{2,1,0:T(8,128)(2,1)S(1)} all-to-all(bf16[128,16,512]{2,1,0:T(8,128)(2,1)S(1)} %bitcast.64), channel_id=1, replica_groups=mesh['ctx'=32,'wa'=4] {'ctx','wa'}, dimensions={0} | all-to-all | bytes 4194304 | tf_op jit(solution)/shard_map/all_to_all | solution.py:30
  97.6 4.2 %experts.1 = (bf16[32,4,16,512]{3,2,1,0:T(8,128)(2,1)S(1)}, bf16[512,1536]{1,0:T(8,128)(2,1)S(1)}) custom-call(bf16[32,4,16,512]{3,2,1,0:T(8,128)(2,1)S(1)} %bitcast.61, bf16[2,1024,128]{2,1,0:T(8,128)(2,1)S(1)} %pad_maximum_fusion.refs_1_, bf16[2,1024,128]{2,1,0:T(8,128)(2,1)S(1)} %collective-permute-done.3.refs_2_, ...), custom_call_target="tpu_custom_call" | custom-call | flops 5500000256 | tf_op jit(solution)/shard_map/experts/pallas_call | solution.py:90
  101.8 1.3 copy-done.4
  103.1 1.2 copy-done.27
  104.3 4.6 %all-to-all-start.2 = ((bf16[128,16,512]{2,1,0:T(8,128)(2,1)}), bf16[128,16,512]{2,1,0:T(8,128)(2,1)S(1)}, u32[]{:S(2)}, u32[]{:S(2)}) async-start(bf16[128,16,512]{2,1,0:T(8,128)(2,1)} %bitcast.63), calls=%async_computation.2 | async-start | bytes 4194304 | tf_op jit(solution)/shard_map/all_to_all | solution.py:30
  108.9 1.6 copy-done.3
  110.5 1.4 copy-done.28
  111.9 1.8 expert_grads.1
  113.8 0.9 copy-done.6
  114.7 0.8 copy-done.10
  115.5 1.2 copy-done.15
  116.6 22.7 %all-to-all-done.2 = bf16[128,16,512]{2,1,0:T(8,128)(2,1)S(1)} async-done(((bf16[128,16,512]{2,1,0:T(8,128)(2,1)}), bf16[128,16,512]{2,1,0:T(8,128)(2,1)S(1)}, u32[]{:S(2)}, u32[]{:S(2)}) %all-to-all-start.2) | async-done | bytes 2097184 | tf_op jit(solution)/shard_map/all_to_all | solution.py:30
  139.3 0.8 copy-done.32
  140.1 1.0 combine.1.refs_0_
  142.0 5.3 %collective-permute-done.11.refs_1_ = bf16[272,256]{1,0:T(8,128)(2,1)S(1)} collective-permute-done((bf16[272,256]{1,0:T(8,128)(2,1)S(1)}, bf16[272,256]{1,0:T(8,128)(2,1)S(1)}, u32[]{:S(2)}, u32[]{:S(2)}) %collective-permute-start.11) | collective-permute-done | bytes 139296 | tf_op jit(solution)/shard_map/ppermute | solution.py:605
  147.7 0.9 collective-permute-done.13.refs_3_
  150.0 1.8 second_norm.1
  151.8 0.8 copy-done.8
  152.7 0.8 fusion.16
  153.5 3.1 %collective-permute-done.15.refs_4_ = bf16[128,128]{1,0:T(8,128)(2,1)S(1)} collective-permute-done((bf16[128,128]{1,0:T(8,128)(2,1)S(1)}, bf16[128,128]{1,0:T(8,128)(2,1)S(1)}, u32[]{:S(2)}, u32[]{:S(2)}) %collective-permute-start.15) | collective-permute-done | bytes 32800 | tf_op jit(solution)/shard_map/ppermute | solution.py:771
  156.6 6.5 %reverse.1 = (bf16[128,128]{1,0:T(8,128)(2,1)S(1)}, bf16[128,128]{1,0:T(8,128)(2,1)S(1)}, bf16[32,128,128]{2,1,0:T(8,128)(2,1)}) custom-call(bf16[128,128]{1,0:T(8,128)(2,1)S(1)} %copy-done.24, bf16[128,128]{1,0:T(8,128)(2,1)S(1)} %collective-permute-done.refs_1_, bf16[32,128,128]{2,1,0:T(8,128)(2,1)S(1)} %all-to-all-done.refs_2_, ...), custom_call_target="tpu_custom_call" | custom-call | flops 1100000000 | tf_op jit(solution)/shard_map/reverse/pallas_call | solution.py:90
  163.6 0.8 copy-done.39
  164.4 3.9 %all-to-all-start.3 = ((bf16[32,128,128]{2,1,0:T(8,128)(2,1)}), bf16[32,128,128]{2,1,0:T(8,128)(2,1)S(1)}, u32[]{:S(2)}, u32[]{:S(2)}) async-start(bf16[32,128,128]{2,1,0:T(8,128)(2,1)} %get-tuple-element.136), calls=%async_computation.3 | async-start | bytes 2097152 | tf_op jit(solution)/shard_map/all_to_all | solution.py:30
  168.9 0.7 maximum_maximum_fusion.refs_1_
  169.6 1.8 collective-permute-start.17
  171.4 0.7 maximum_maximum_fusion.1.refs_2_
  172.1 1.4 pad.4.refs_10_
  173.4 6.4 %collective-permute-done.17.refs_8_ = bf16[128,128]{1,0:T(8,128)(2,1)S(1)} collective-permute-done((bf16[128,128]{1,0:T(8,128)(2,1)S(1)}, bf16[128,128]{1,0:T(8,128)(2,1)S(1)}, u32[]{:S(2)}, u32[]{:S(2)}) %collective-permute-start.17) | collective-permute-done | bytes 32800 | tf_op jit(solution)/shard_map/ppermute | solution.py:793
  179.9 8.0 %all-to-all-done.3.refs_0_ = bf16[32,128,128]{2,1,0:T(8,128)(2,1)S(1)} async-done(((bf16[32,128,128]{2,1,0:T(8,128)(2,1)}), bf16[32,128,128]{2,1,0:T(8,128)(2,1)S(1)}, u32[]{:S(2)}, u32[]{:S(2)}) %all-to-all-start.3) | async-done | bytes 1048608 | tf_op jit(solution)/shard_map/all_to_all | solution.py:30
  187.8 1.0 copy-done.38
  188.8 5.2 %late.1 = (bf16[32,112,256]{2,1,0:T(8,128)(2,1)}, bf16[80,1024]{1,0:T(8,128)(2,1)}, bf16[80,1024]{1,0:T(8,128)(2,1)}) custom-call(bf16[32,128,128]{2,1,0:T(8,128)(2,1)} %copy-done.38, f32[128,128]{1,0:T(8,128)} %maximum_maximum_fusion.refs_1_, f32[128,128]{1,0:T(8,128)} %maximum_maximum_fusion.1.refs_2_, ...), custom_call_target="tpu_custom_call", output_to_operand_aliasing={{0}: (10, {})} | custom-call | flops 2200000000 | tf_op jit(solution)/shard_map/late/pallas_call | solution.py:90
  194.0 4.4 %all-to-all-start.4 = ((bf16[32,112,256]{2,1,0:T(8,128)(2,1)}), bf16[32,112,256]{2,1,0:T(8,128)(2,1)S(1)}, u32[]{:S(2)}, u32[]{:S(2)}) async-start(bf16[32,112,256]{2,1,0:T(8,128)(2,1)} %get-tuple-element.144), calls=%async_computation.4 | async-start | bytes 3670016 | tf_op jit(solution)/shard_map/all_to_all | solution.py:30
  198.7 1.2 collective-permute-done.18
  199.9 0.8 collective-permute-start.19
  200.7 20.7 %collective-permute-done.19 = bf16[80,1024]{1,0:T(8,128)(2,1)S(1)} collective-permute-done((bf16[80,1024]{1,0:T(8,128)(2,1)S(1)}, bf16[80,1024]{1,0:T(8,128)(2,1)S(1)}, u32[]{:S(2)}, u32[]{:S(2)}) %collective-permute-start.19) | collective-permute-done | bytes 163872 | tf_op jit(solution)/shard_map/ppermute | solution.py:595
  221.4 5.5 %all-to-all-done.4.refs_0_ = bf16[32,112,256]{2,1,0:T(8,128)(2,1)S(1)} async-done(((bf16[32,112,256]{2,1,0:T(8,128)(2,1)}), bf16[32,112,256]{2,1,0:T(8,128)(2,1)S(1)}, u32[]{:S(2)}, u32[]{:S(2)}) %all-to-all-start.4) | async-done | bytes 1835040 | tf_op jit(solution)/shard_map/all_to_all | solution.py:30
  226.9 0.9 share.1
  227.9 1.2 copy-done.5
  229.1 4.9 %all-to-all-start.5 = ((bf16[32,112,256]{2,1,0:T(8,128)(2,1)}), bf16[32,112,256]{2,1,0:T(8,128)(2,1)S(1)}, u32[]{:S(2)}, u32[]{:S(2)}) async-start(bf16[32,112,256]{2,1,0:T(8,128)(2,1)} %copy-done.5), calls=%async_computation.5 | async-start | bytes 3670016 | tf_op jit(solution)/shard_map/all_to_all | solution.py:30
  234.0 1.6 fusion
  235.8 1.1 fusion.13
  237.4 0.9 fusion.10
  238.4 19.3 %collective-permute-done.21 = bf16[1024,128]{1,0:T(8,128)(2,1)S(1)} collective-permute-done((bf16[1024,128]{1,0:T(8,128)(2,1)S(1)}, bf16[1024,128]{1,0:T(8,128)(2,1)S(1)}, u32[]{:S(2)}, u32[]{:S(2)}) %collective-permute-start.21) | collective-permute-done | bytes 262176 | tf_op jit(solution)/shard_map/ppermute | solution.py:829
  257.8 0.8 copy.37
  258.6 3.5 %all-to-all-done.5.refs_0_ = bf16[32,112,256]{2,1,0:T(8,128)(2,1)S(1)} async-done(((bf16[32,112,256]{2,1,0:T(8,128)(2,1)}), bf16[32,112,256]{2,1,0:T(8,128)(2,1)S(1)}, u32[]{:S(2)}, u32[]{:S(2)}) %all-to-all-start.5) | async-done | bytes 1835040 | tf_op jit(solution)/shard_map/all_to_all | solution.py:30
  262.1 1.8 final.1
  (139 shorter events, 8.1 us)
Async XLA Ops:
  5.8 11.1 %copy-start.48 = (bf16[128,128]{1,0:T(8,128)(2,1)S(1)}, bf16[128,128]{1,0:T(8,128)(2,1)}, u32[]{:S(2)}) copy-start(bf16[128,128]{1,0:T(8,128)(2,1)} %get-tuple-element.93) | copy-start | bytes 98308
  5.8 13.0 %copy-start.41 = (bf16[1,128,1024]{2,1,0:T(8,128)(2,1)S(1)}, bf16[1,128,1024]{2,1,0:T(8,128)(2,1)}, u32[]{:S(2)}) copy-start(bf16[1,128,1024]{2,1,0:T(8,128)(2,1)} %param.23) | copy-start | bytes 786436
  5.8 13.7 %copy-start.46 = (s32[128,8]{0,1:T(8,128)S(1)}, s32[128,8]{0,1:T(8,128)}, u32[]{:S(2)}) copy-start(s32[128,8]{0,1:T(8,128)} %param.24) | copy-start | bytes 12292
  5.8 13.9 %copy-start.42 = (bf16[1,1024,128]{2,1,0:T(8,128)(2,1)S(1)}, bf16[1,1024,128]{2,1,0:T(8,128)(2,1)}, u32[]{:S(2)}) copy-start(bf16[1,1024,128]{2,1,0:T(8,128)(2,1)} %param.22) | copy-start | bytes 786436
  5.8 32.4 %copy-start.23 = (bf16[128,128]{1,0:T(8,128)(2,1)S(1)}, bf16[128,128]{1,0:T(8,128)(2,1)}, u32[]{:S(2)}) copy-start(bf16[128,128]{1,0:T(8,128)(2,1)} %get-tuple-element.91.refs_0_) | copy-start | bytes 98308
  5.8 31.8 %all-to-all-start = ((bf16[32,128,128]{2,1,0:T(8,128)(2,1)}), bf16[32,128,128]{2,1,0:T(8,128)(2,1)S(1)}, u32[]{:S(2)}, u32[]{:S(2)}) async-start(bf16[32,128,128]{2,1,0:T(8,128)(2,1)} %get-tuple-element.92), calls=%async_computation | async-start | bytes 2097152 | tf_op jit(solution)/shard_map/all_to_all | solution.py:30
  16.9 11.5 %collective-permute-start = (bf16[128,128]{1,0:T(8,128)(2,1)S(1)}, bf16[128,128]{1,0:T(8,128)(2,1)S(1)}, u32[]{:S(2)}, u32[]{:S(2)}) collective-permute-start(bf16[128,128]{1,0:T(8,128)(2,1)S(1)} %copy-done.48), channel_id=1, source_target_pairs={{0,8},{4,12},{8,0},{12,4},{16,24},{20,28},{24,16},{28,20},{32,40},... | collective-permute-start | bytes 98312 | tf_op jit(solution)/shard_map/ppermute | solution.py:652
  18.8 28.3 %copy-start.16 = (bf16[256,1024]{1,0:T(8,128)(2,1)S(1)}, bf16[256,1024]{1,0:T(8,128)(2,1)}, u32[]{:S(2)}) copy-start(bf16[256,1024]{1,0:T(8,128)(2,1)} %refs_10_.1) | copy-start | bytes 1572868
  18.9 15.8 %collective-permute-start.1 = (bf16[1024,128]{1,0:T(8,128)(2,1)S(1)}, bf16[1024,128]{1,0:T(8,128)(2,1)S(1)}, u32[]{:S(2)}, u32[]{:S(2)}) collective-permute-start(bf16[1024,128]{1,0:T(8,128)(2,1)S(1)} %bitcast.65), channel_id=1, source_target_pairs={{0,2},{2,0},{1,3},{3,1},{4,6},{6,4},{5,7},{7,5},{8,10},{10,8},{9,1... | collective-permute-start | bytes 786440 | tf_op jit(solution)/shard_map/ppermute | solution.py:665
  37.7 10.7 %collective-permute-start.3 = (bf16[2,1024,128]{2,1,0:T(8,128)(2,1)S(1)}, bf16[2,1024,128]{2,1,0:T(8,128)(2,1)S(1)}, u32[]{:S(2)}, u32[]{:S(2)}) collective-permute-start(bf16[2,1024,128]{2,1,0:T(8,128)(2,1)S(1)} %pad_maximum_fusion.refs_1_), channel_id=1, source_target_pairs={{0,2},{2,0},{1,3},{3,1},{4,6},{6,4},{5,7},{7,5},{8,10},{10,8},{9,1... | collective-permute-start | bytes 1572872 | tf_op jit(solution)/shard_map/ppermute | solution.py:605
  43.1 12.3 %copy-start.21 = (f32[72,512]{1,0:T(8,128)}, f32[72,512]{1,0:T(8,128)S(1)}, u32[]{:S(2)}) copy-start(f32[72,512]{1,0:T(8,128)S(1)} %get-tuple-element.132.refs_5_) | copy-start | bytes 442372
  43.1 4.0 %collective-permute-start.2 = (bf16[128,128]{1,0:T(8,128)(2,1)S(1)}, bf16[128,128]{1,0:T(8,128)(2,1)S(1)}, u32[]{:S(2)}, u32[]{:S(2)}) collective-permute-start(bf16[128,128]{1,0:T(8,128)(2,1)S(1)} %get-tuple-element.97), channel_id=1, source_target_pairs={{0,8},{4,12},{8,0},{12,4},{16,24},{20,28},{24,16},{28,20},{32,40},... | collective-permute-start | bytes 98312 | tf_op jit(solution)/shard_map/ppermute | solution.py:685
  47.1 9.8 %copy-start = (bf16[128,1024]{1,0:T(8,128)(2,1)S(1)}, bf16[128,1024]{1,0:T(8,128)(2,1)}, u32[]{:S(2)}) copy-start(bf16[128,1024]{1,0:T(8,128)(2,1)} %refs_9_.1) | copy-start | bytes 786436
  47.1 9.8 %copy-start.18 = (bf16[1024,32]{0,1:T(8,128)(2,1)S(1)}, bf16[1024,32]{0,1:T(8,128)(2,1)}, u32[]{:S(2)}) copy-start(bf16[1024,32]{0,1:T(8,128)(2,1)} %param.20) | copy-start | bytes 196612
  47.1 9.8 %copy-start.20 = (f32[1024]{0:T(1024)S(1)}, f32[1024]{0:T(1024)}, u32[]{:S(2)}) copy-start(f32[1024]{0:T(1024)} %param.19) | copy-start | bytes 12292
  47.4 9.5 %copy-start.34 = (bf16[256,128]{1,0:T(8,128)(2,1)}, bf16[256,128]{1,0:T(8,128)(2,1)S(1)}, u32[]{:S(2)}) copy-start(bf16[256,128]{1,0:T(8,128)(2,1)S(1)} %get-tuple-element.129.refs_11_) | copy-start | bytes 196612
  48.4 1.3 collective-permute-start.4
  49.8 5.6 %collective-permute-start.5 = (bf16[64,1024]{1,0:T(8,128)(2,1)S(1)}, bf16[64,1024]{1,0:T(8,128)(2,1)S(1)}, u32[]{:S(2)}, u32[]{:S(2)}) collective-permute-start(bf16[64,1024]{1,0:T(8,128)(2,1)S(1)} %add_convert_fusion.3), channel_id=1, source_target_pairs={{0,2},{2,0},{1,3},{3,1},{4,6},{6,4},{5,7},{7,5},{8,10},{10,8},{9,1... | collective-permute-start | bytes 393224 | tf_op jit(solution)/shard_map/ppermute | solution.py:595
  50.5 7.6 %collective-permute-start.7 = (bf16[2,1024,128]{2,1,0:T(8,128)(2,1)S(1)}, bf16[2,1024,128]{2,1,0:T(8,128)(2,1)S(1)}, u32[]{:S(2)}, u32[]{:S(2)}) collective-permute-start(bf16[2,1024,128]{2,1,0:T(8,128)(2,1)S(1)} %pad_maximum_fusion.refs_1_), channel_id=1, source_target_pairs={{0,1},{1,0},{2,3},{3,2},{4,5},{5,4},{6,7},{7,6},{8,9},{9,8},{10,11... | collective-permute-start | bytes 1572872 | tf_op jit(solution)/shard_map/ppermute | solution.py:606
  50.5 7.6 %collective-permute-start.8 = (bf16[2,1024,128]{2,1,0:T(8,128)(2,1)S(1)}, bf16[2,1024,128]{2,1,0:T(8,128)(2,1)S(1)}, u32[]{:S(2)}, u32[]{:S(2)}) collective-permute-start(bf16[2,1024,128]{2,1,0:T(8,128)(2,1)S(1)} %collective-permute-done.3.refs_2_), channel_id=1, source_target_pairs={{0,1},{1,0},{2,3},{3,2},{4,5},{5,4},{6,7},{7,6},{8,9},{9,8},{10,11... | collective-permute-start | bytes 1572872 | tf_op jit(solution)/shard_map/ppermute | solution.py:607
  55.4 1.4 collective-permute-start.6
  55.5 2.5 collective-permute-start.9
  56.0 2.0 collective-permute-start.10
  58.0 39.6 %copy-start.25 = (f32[128,1024]{1,0:T(8,128)}, f32[128,1024]{1,0:T(8,128)S(1)}, u32[]{:S(2)}) copy-start(f32[128,1024]{1,0:T(8,128)S(1)} %get-tuple-element.127.refs_5_) | copy-start | bytes 1572868
  58.0 39.6 %copy-start.29 = (bf16[128,1024]{1,0:T(8,128)(2,1)}, bf16[128,1024]{1,0:T(8,128)(2,1)S(1)}, u32[]{:S(2)}) copy-start(bf16[128,1024]{1,0:T(8,128)(2,1)S(1)} %get-tuple-element.128.refs_6_) | copy-start | bytes 786436
  58.1 39.5 %copy-start.31 = (f32[64,128]{1,0:T(8,128)}, f32[64,128]{1,0:T(8,128)S(1)}, u32[]{:S(2)}) copy-start(f32[64,128]{1,0:T(8,128)S(1)} %get-tuple-element.121.refs_1_.refs_4_) | copy-start | bytes 98308
  97.6 4.2 %copy-start.2 = (bf16[128,16,512]{2,1,0:T(8,128)(2,1)}, bf16[128,16,512]{2,1,0:T(8,128)(2,1)S(1)}, u32[]{:S(2)}) copy-start(bf16[128,16,512]{2,1,0:T(8,128)(2,1)S(1)} %all_to_all.30) | copy-start | bytes 6291460
  104.3 35.0 %all-to-all-start.2 = ((bf16[128,16,512]{2,1,0:T(8,128)(2,1)}), bf16[128,16,512]{2,1,0:T(8,128)(2,1)S(1)}, u32[]{:S(2)}, u32[]{:S(2)}) async-start(bf16[128,16,512]{2,1,0:T(8,128)(2,1)} %bitcast.63), calls=%async_computation.2 | async-start | bytes 4194304 | tf_op jit(solution)/shard_map/all_to_all | solution.py:30
  108.9 1.6 copy-start.3
  139.3 8.0 %collective-permute-start.14 = (bf16[2,3,1024,128]{3,2,1,0:T(8,128)(2,1)}, bf16[2,3,1024,128]{3,2,1,0:T(8,128)(2,1)S(1)}, u32[]{:S(2)}, u32[]{:S(2)}) collective-permute-start(bf16[2,3,1024,128]{3,2,1,0:T(8,128)(2,1)} %copy-done.15), channel_id=1, source_target_pairs={{0,1},{1,0},{2,3},{3,2},{4,5},{5,4},{6,7},{7,6},{8,9},{9,8},{10,11... | collective-permute-start | bytes 4718600 | tf_op jit(solution)/shard_map/ppermute | solution.py:740
  141.1 6.4 %copy-start.11 = (bf16[2,1024,128]{2,1,0:T(8,128)(2,1)S(1)}, bf16[2,1024,128]{2,1,0:T(8,128)(2,1)}, u32[]{:S(2)}) copy-start(bf16[2,1024,128]{2,1,0:T(8,128)(2,1)} %copy-done.10) | copy-start | bytes 1572868
  141.1 6.2 %collective-permute-start.11 = (bf16[272,256]{1,0:T(8,128)(2,1)S(1)}, bf16[272,256]{1,0:T(8,128)(2,1)S(1)}, u32[]{:S(2)}, u32[]{:S(2)}) collective-permute-start(bf16[272,256]{1,0:T(8,128)(2,1)S(1)} %combine.1.refs_0_), channel_id=1, source_target_pairs={{0,2},{2,0},{1,3},{3,1},{4,6},{6,4},{5,7},{7,5},{8,10},{10,8},{9,1... | collective-permute-start | bytes 417800 | tf_op jit(solution)/shard_map/ppermute | solution.py:605
  141.8 5.9 %collective-permute-start.12 = (bf16[272,256]{1,0:T(8,128)(2,1)S(1)}, bf16[272,256]{1,0:T(8,128)(2,1)S(1)}, u32[]{:S(2)}, u32[]{:S(2)}) collective-permute-start(bf16[272,256]{1,0:T(8,128)(2,1)S(1)} %combine.1.refs_0_), channel_id=1, source_target_pairs={{0,1},{1,0},{2,3},{3,2},{4,5},{5,4},{6,7},{7,6},{8,9},{9,8},{10,11... | collective-permute-start | bytes 417800 | tf_op jit(solution)/shard_map/ppermute | solution.py:606
  147.3 1.4 collective-permute-start.13
  147.5 15.5 %copy-start.37 = (f32[2,3,1024,128]{3,2,1,0:T(8,128)}, f32[2,3,1024,128]{3,2,1,0:T(8,128)S(1)}, u32[]{:S(2)}) copy-start(f32[2,3,1024,128]{3,2,1,0:T(8,128)S(1)} %convert_element_type.103) | copy-start | bytes 9437188
  147.5 1.7 copy-start.12
  147.5 1.7 copy-start.17
  147.5 1.7 copy-start.19
  147.5 2.3 copy-start.26
  147.6 2.5 copy-start.30
  147.6 2.4 copy-start.33
  147.6 2.4 copy-start.35
  148.6 15.0 %collective-permute-start.16 = (bf16[2,1024,128]{2,1,0:T(8,128)(2,1)S(1)}, bf16[2,1024,128]{2,1,0:T(8,128)(2,1)S(1)}, u32[]{:S(2)}, u32[]{:S(2)}) collective-permute-start(bf16[2,1024,128]{2,1,0:T(8,128)(2,1)S(1)} %fusion.3), channel_id=1, source_target_pairs={{0,2},{2,0},{1,3},{3,1},{4,6},{6,4},{5,7},{7,5},{8,10},{10,8},{9,1... | collective-permute-start | bytes 1572872 | tf_op jit(solution)/shard_map/ppermute | solution.py:756
  150.0 6.5 %copy-start.13 = (f32[32,128]{1,0:T(8,128)S(1)}, f32[32,128]{1,0:T(8,128)}, u32[]{:S(2)}) copy-start(f32[32,128]{1,0:T(8,128)} %get-tuple-element.181.refs_5_.refs_6_) | copy-start | bytes 49156
  150.0 6.5 %copy-start.14 = (f32[32,128]{1,0:T(8,128)S(1)}, f32[32,128]{1,0:T(8,128)}, u32[]{:S(2)}) copy-start(f32[32,128]{1,0:T(8,128)} %get-tuple-element.182.refs_6_.refs_7_) | copy-start | bytes 49156
  150.0 6.5 %copy-start.22 = (f32[72,512]{1,0:T(8,128)S(1)}, f32[72,512]{1,0:T(8,128)}, u32[]{:S(2)}) copy-start(f32[72,512]{1,0:T(8,128)} %copy-done.21) | copy-start | bytes 442372
  150.0 6.5 %copy-start.24 = (bf16[128,128]{1,0:T(8,128)(2,1)S(1)}, bf16[128,128]{1,0:T(8,128)(2,1)}, u32[]{:S(2)}) copy-start(bf16[128,128]{1,0:T(8,128)(2,1)} %get-tuple-element.91.refs_0_) | copy-start | bytes 98308
  152.6 3.9 %collective-permute-start.15 = (bf16[128,128]{1,0:T(8,128)(2,1)S(1)}, bf16[128,128]{1,0:T(8,128)(2,1)S(1)}, u32[]{:S(2)}, u32[]{:S(2)}) collective-permute-start(bf16[128,128]{1,0:T(8,128)(2,1)S(1)} %get-tuple-element.131), channel_id=1, source_target_pairs={{0,8},{4,12},{8,0},{12,4},{16,24},{20,28},{24,16},{28,20},{32,40},... | collective-permute-start | bytes 98312 | tf_op jit(solution)/shard_map/ppermute | solution.py:771
  164.4 23.4 %all-to-all-start.3 = ((bf16[32,128,128]{2,1,0:T(8,128)(2,1)}), bf16[32,128,128]{2,1,0:T(8,128)(2,1)S(1)}, u32[]{:S(2)}, u32[]{:S(2)}) async-start(bf16[32,128,128]{2,1,0:T(8,128)(2,1)} %get-tuple-element.136), calls=%async_computation.3 | async-start | bytes 2097152 | tf_op jit(solution)/shard_map/all_to_all | solution.py:30
  169.6 10.3 %collective-permute-start.17 = (bf16[128,128]{1,0:T(8,128)(2,1)S(1)}, bf16[128,128]{1,0:T(8,128)(2,1)S(1)}, u32[]{:S(2)}, u32[]{:S(2)}) collective-permute-start(bf16[128,128]{1,0:T(8,128)(2,1)S(1)} %get-tuple-element.138), channel_id=1, source_target_pairs={{0,8},{4,12},{8,0},{12,4},{16,24},{20,28},{24,16},{28,20},{32,40},... | collective-permute-start | bytes 98312 | tf_op jit(solution)/shard_map/ppermute | solution.py:793
  179.8 8.0 %copy-start.49 = (bf16[128,128]{1,0:T(8,128)(2,1)}, bf16[128,128]{1,0:T(8,128)(2,1)S(1)}, u32[]{:S(2)}) copy-start(bf16[128,128]{1,0:T(8,128)(2,1)S(1)} %collective-permute-done.17.refs_8_) | copy-start | bytes 98308
  194.0 4.4 %copy-start.47 = (bf16[80,1024]{1,0:T(8,128)(2,1)S(1)}, bf16[80,1024]{1,0:T(8,128)(2,1)}, u32[]{:S(2)}) copy-start(bf16[80,1024]{1,0:T(8,128)(2,1)} %get-tuple-element.146) | copy-start | bytes 491524
  194.0 4.5 %copy-start.1 = (bf16[128,1024]{1,0:T(8,128)(2,1)S(1)}, bf16[128,1024]{1,0:T(8,128)(2,1)}, u32[]{:S(2)}) copy-start(bf16[128,1024]{1,0:T(8,128)(2,1)} %refs_9_.1) | copy-start | bytes 786436
  194.0 5.9 %copy-start.44 = (bf16[80,1024]{1,0:T(8,128)(2,1)S(1)}, bf16[80,1024]{1,0:T(8,128)(2,1)}, u32[]{:S(2)}) copy-start(bf16[80,1024]{1,0:T(8,128)(2,1)} %get-tuple-element.145) | copy-start | bytes 491524
  194.0 32.8 %all-to-all-start.4 = ((bf16[32,112,256]{2,1,0:T(8,128)(2,1)}), bf16[32,112,256]{2,1,0:T(8,128)(2,1)S(1)}, u32[]{:S(2)}, u32[]{:S(2)}) async-start(bf16[32,112,256]{2,1,0:T(8,128)(2,1)} %get-tuple-element.144), calls=%async_computation.4 | async-start | bytes 3670016 | tf_op jit(solution)/shard_map/all_to_all | solution.py:30
  198.4 1.5 collective-permute-start.18
  199.9 21.5 %collective-permute-start.19 = (bf16[80,1024]{1,0:T(8,128)(2,1)S(1)}, bf16[80,1024]{1,0:T(8,128)(2,1)S(1)}, u32[]{:S(2)}, u32[]{:S(2)}) collective-permute-start(bf16[80,1024]{1,0:T(8,128)(2,1)S(1)} %add_convert_fusion.1), channel_id=1, source_target_pairs={{0,2},{2,0},{1,3},{3,1},{4,6},{6,4},{5,7},{7,5},{8,10},{10,8},{9,1... | collective-permute-start | bytes 491528 | tf_op jit(solution)/shard_map/ppermute | solution.py:595
  229.1 4.9 %copy-start.7 = (bf16[3,1024,128]{2,1,0:T(8,128)(2,1)S(1)}, bf16[3,1024,128]{2,1,0:T(8,128)(2,1)}, u32[]{:S(2)}) copy-start(bf16[3,1024,128]{2,1,0:T(8,128)(2,1)} %copy-done.6) | copy-start | bytes 2359300
  229.1 33.0 %all-to-all-start.5 = ((bf16[32,112,256]{2,1,0:T(8,128)(2,1)}), bf16[32,112,256]{2,1,0:T(8,128)(2,1)S(1)}, u32[]{:S(2)}, u32[]{:S(2)}) async-start(bf16[32,112,256]{2,1,0:T(8,128)(2,1)} %copy-done.5), calls=%async_computation.5 | async-start | bytes 3670016 | tf_op jit(solution)/shard_map/all_to_all | solution.py:30
  234.0 1.8 copy-start.40
  235.6 1.6 copy-start.45
  235.7 1.8 copy-start.9
  235.7 1.5 collective-permute-start.20
  236.8 20.9 %collective-permute-start.21 = (bf16[1024,128]{1,0:T(8,128)(2,1)S(1)}, bf16[1024,128]{1,0:T(8,128)(2,1)S(1)}, u32[]{:S(2)}, u32[]{:S(2)}) collective-permute-start(bf16[1024,128]{1,0:T(8,128)(2,1)S(1)} %copy-done.43), channel_id=1, source_target_pairs={{0,2},{2,0},{1,3},{3,1},{4,6},{6,4},{5,7},{7,5},{8,10},{10,8},{9,1... | collective-permute-start | bytes 786440 | tf_op jit(solution)/shard_map/ppermute | solution.py:829
  (13 other events, 13.1 us)
